TPU v7x, 256 devices: a whole 4x4x8 slice. The times are simulated.
256 devices in a mesh: seq: 64 (over y_hi, x, z), head: 4 (over y_lo, core).
Axes of the slice: x: 4, y: 4 (y_hi: 2, y_lo: 2; y = y_hi * 2 + y_lo), z: 8, core: 2. Of those that a mesh axis runs over, the one named last changes fastest.
Arguments:
- tokens: bfloat16 [131072, 768], P(('seq', 'head')), may hold values from -6 to 6
- cotangent: bfloat16 [131072, 768], P(('seq', 'head')), may hold values from -6 to 6
- w_query: bfloat16 [768, 768], P('head'), may hold values from -0.21875 to 0.21875
- w_key: bfloat16 [768, 768], P('head'), may hold values from -0.21875 to 0.21875
- w_value: bfloat16 [768, 768], P('head'), may hold values from -0.21875 to 0.21875
- w_out: bfloat16 [768, 768], P('head'), may hold values from -0.21875 to 0.21875
- offsets: int32 [3, 12], replicated, may hold values from 0 to 127, as said below
Outputs:
- mixed: bfloat16 [131072, 768], P(('seq', 'head'))
- grad_tokens: bfloat16 [131072, 768], P(('seq', 'head'))
- grad_query: float32 [768, 768], P('head')
- grad_key: float32 [768, 768], P('head')
- grad_value: float32 [768, 768], P('head')
- grad_out: float32 [768, 768], P('head')
Inputs may be any that keep to these rules, and one draw needn't show every extreme that they name: Row l of offsets lies in 0 to the dilation of level l + 1 minus 1; in every row some head has 0 and some head has the row's largest allowed value.
All inputs are finite; a program needn't handle non-finite values.
Results may differ from a plain program's by a relative error of at most 0.017.
Values may be sent and summed in bfloat16 or wider, within the bound.
No kernel may reach another device: no remote copies, remote signals or barrier semaphores. Data moves between devices by JAX's collectives and lax.ppermute only.
A program may use at most 128 MiB of HBM per device.

v0:
```python
import jax
import jax.numpy as jnp
from jax import lax
from jax.sharding import PartitionSpec as P

HEAD_DIM = 64
SEL = 512


def swapped(value, axis, stride):
    mask = 2**stride
    pairs = [(source, source ^ mask) for source in range(lax.axis_size(axis))]
    return lax.ppermute(value, axis, pairs)


def as_sent(value):

    def short(part):
        return part.astype(jnp.bfloat16) if part.dtype == jnp.float32 else part

    return jax.tree.map(short, value)


def compact_rows(field, dilation, selected):
    shaped = field.reshape(-1, dilation, field.shape[1])
    return jnp.sum(jnp.where(selected[None], shaped, jnp.zeros((), field.dtype)), axis=1)


def widen_rows(packed, selected):
    full_rows = jnp.where(selected[None], packed[:, None, :], jnp.zeros((), packed.dtype))
    return full_rows.reshape(-1, packed.shape[1])


def collect_groups(blocks, level_bits, bit_order, seq_index):
    for bit_step in bit_order:
        active = [level_id for level_id in range(3) if level_bits[level_id] > bit_step]
        packed = jnp.concatenate([blocks[level_id] for level_id in active], 0)
        partner = swapped(packed, "seq", bit_step)
        upper_bit = seq_index >> bit_step & 1 == 1
        cursor = 0
        for level_id in active:
            row_count = blocks[level_id].shape[0]
            theirs = partner[cursor : cursor + row_count]
            own_rows = blocks[level_id]
            blocks[level_id] = jnp.concatenate(
                [jnp.where(upper_bit, theirs, own_rows), jnp.where(upper_bit, own_rows, theirs)], 0
            )
            cursor += row_count
    return blocks


def return_groups(blocks, level_bits, bit_order, seq_index):
    for bit_step in bit_order:
        active = [level_id for level_id in range(3) if level_bits[level_id] > bit_step]
        upper_bit = seq_index >> bit_step & 1 == 1
        outgoing = []
        kept_rows = []
        for level_id in active:
            half_rows = blocks[level_id].shape[0] // 2
            lower_half = blocks[level_id][:half_rows]
            upper_half = blocks[level_id][half_rows:]
            kept_rows.append(jnp.where(upper_bit, upper_half, lower_half))
            outgoing.append(jnp.where(upper_bit, lower_half, upper_half))
        incoming = swapped(as_sent(jnp.concatenate(outgoing, 0)), "seq", bit_step)
        cursor = 0
        for position, level_id in enumerate(active):
            row_count = kept_rows[position].shape[0]
            blocks[level_id] = kept_rows[position] + incoming[cursor : cursor + row_count]
            cursor += row_count
    return blocks


def per_device(tokens, cotangent, w_query, w_key, w_value, w_out, offsets):
    whole_tokens, whole_grads = (
        lax.all_gather(tokens, "head", axis=0, tiled=True),
        lax.all_gather(cotangent, "head", axis=0, tiled=True),
    )
    contract_cols = (((1,), (1,)), ((), ()))
    queries = lax.dot_general(
        whole_tokens, w_query, contract_cols, preferred_element_type=jnp.float32
    ).astype(jnp.bfloat16)
    key_rows = lax.dot_general(
        whole_tokens, w_key, contract_cols, preferred_element_type=jnp.float32
    ).astype(jnp.bfloat16)
    value_rows = lax.dot_general(
        whole_tokens, w_value, contract_cols, preferred_element_type=jnp.float32
    ).astype(jnp.bfloat16)
    local_rows = whole_tokens.shape[0]
    columns = queries.shape[1]
    head_count = columns // HEAD_DIM
    head_first = lax.axis_index("head") * head_count
    head_offsets = lax.dynamic_slice_in_dim(offsets, head_first, head_count, 1)
    seq_count = lax.axis_size("seq")
    wide_mesh = min(1, seq_count // 32)
    level_bits = [1, 2 + wide_mesh, 3 + 2 * wide_mesh]
    dilations = [2 ** level_bits[level_id] * local_rows // SEL for level_id in range(3)]
    seq_index = lax.axis_index("seq")
    score_scale = HEAD_DIM ** (-0.5)
    head_marks = []
    wide_marks = []
    query_levels = []
    pair_blocks = []
    for level_id in range(3):
        selected = (
            jnp.arange(dilations[level_id], dtype=jnp.int32)[:, None]
            == head_offsets[level_id][None, :]
        )
        head_marks.append(selected)
        wide_marks.append(jnp.repeat(selected, HEAD_DIM, axis=1))
        query_levels.append(compact_rows(queries, dilations[level_id], wide_marks[level_id]))
        pair_blocks.append(
            jnp.concatenate(
                [
                    compact_rows(key_rows, dilations[level_id], wide_marks[level_id]),
                    compact_rows(value_rows, dilations[level_id], wide_marks[level_id]),
                ],
                1,
            )
        )
    groups = collect_groups(list(pair_blocks), level_bits, list(range(level_bits[2])), seq_index)
    back_order = list(reversed(range(level_bits[2])))
    totals = jnp.zeros((local_rows, head_count), jnp.float32)
    covered = jnp.zeros((local_rows, head_count), bool)
    stored = []
    for level_id in range(3):
        query_heads = query_levels[level_id].reshape(-1, head_count, HEAD_DIM)
        key_heads = groups[level_id][:, :columns].reshape(-1, head_count, HEAD_DIM)
        value_heads = groups[level_id][:, columns:].reshape(-1, head_count, HEAD_DIM)
        scores = (
            jnp.einsum("qhe,khe->hqk", query_heads, key_heads, preferred_element_type=jnp.float32)
            * score_scale
        )
        exponent = jnp.exp(scores)
        totals = totals + widen_rows(jnp.sum(exponent, -1).T, head_marks[level_id])
        residue = jnp.arange(local_rows, dtype=jnp.int32) % dilations[level_id]
        covered = covered | (residue[:, None] == head_offsets[level_id][None, :])
        stored.append((query_heads, key_heads, value_heads, exponent))
    totals = totals + jnp.where(covered, 0.0, 1.0).astype(jnp.float32)
    attended = jnp.zeros((local_rows, columns), jnp.float32)
    weight_store = []
    for level_id in range(3):
        query_heads, key_heads, value_heads, exponent = stored[level_id]
        row_totals = compact_rows(totals, dilations[level_id], head_marks[level_id])
        weights = exponent / row_totals.T[:, :, None]
        rounded_weights = weights.astype(jnp.bfloat16)
        level_part = jnp.einsum(
            "hqk,khe->qhe", rounded_weights, value_heads, preferred_element_type=jnp.float32
        ).reshape(-1, columns)
        attended = attended + widen_rows(level_part, wide_marks[level_id])
        weight_store.append((weights, rounded_weights))
    attention_out = attended.astype(jnp.bfloat16)
    mixed_terms = jnp.dot(attention_out, w_out, preferred_element_type=jnp.float32)
    grad_attention = lax.dot_general(
        whole_grads, w_out, contract_cols, preferred_element_type=jnp.float32
    ).astype(jnp.bfloat16)
    contract_rows = (((0,), (0,)), ((), ()))
    output_terms = lax.dot_general(
        attention_out, whole_grads, contract_rows, preferred_element_type=jnp.float32
    )
    row_delta = jnp.sum(
        (grad_attention.astype(jnp.float32) * attended).reshape(local_rows, head_count, HEAD_DIM),
        -1,
    )
    query_grad = jnp.zeros((local_rows, columns), jnp.float32)
    pair_parts = []
    for level_id in range(3):
        query_heads, key_heads, value_heads, exponent = stored[level_id]
        weights, rounded_weights = weight_store[level_id]
        grad_rows = compact_rows(grad_attention, dilations[level_id], wide_marks[level_id]).reshape(
            -1, head_count, HEAD_DIM
        )
        delta_rows = compact_rows(row_delta, dilations[level_id], head_marks[level_id])
        grad_weights = jnp.einsum(
            "qhe,khe->hqk", grad_rows, value_heads, preferred_element_type=jnp.float32
        )
        grad_scores = (weights * (grad_weights - delta_rows.T[:, :, None]) * score_scale).astype(
            jnp.bfloat16
        )
        query_part = jnp.einsum(
            "hqk,khe->qhe", grad_scores, key_heads, preferred_element_type=jnp.float32
        ).reshape(-1, columns)
        query_grad = query_grad + widen_rows(query_part, wide_marks[level_id])
        key_part = jnp.einsum(
            "hqk,qhe->khe", grad_scores, query_heads, preferred_element_type=jnp.float32
        ).reshape(-1, columns)
        value_part = jnp.einsum(
            "hqk,qhe->khe", rounded_weights, grad_rows, preferred_element_type=jnp.float32
        ).reshape(-1, columns)
        pair_parts.append(jnp.concatenate([key_part, value_part], 1))
    owned = return_groups(list(pair_parts), level_bits, back_order, seq_index)
    pair_grad = jnp.zeros((local_rows, 2 * columns), jnp.float32)
    for level_id in range(3):
        pair_marks = jnp.concatenate([wide_marks[level_id], wide_marks[level_id]], 1)
        pair_grad = pair_grad + widen_rows(owned[level_id], pair_marks)
    query_change = query_grad.astype(jnp.bfloat16)
    key_change = pair_grad[:, :columns].astype(jnp.bfloat16)
    value_change = pair_grad[:, columns:].astype(jnp.bfloat16)
    query_terms = lax.dot_general(
        query_change, whole_tokens, contract_rows, preferred_element_type=jnp.float32
    )
    key_terms = lax.dot_general(
        key_change, whole_tokens, contract_rows, preferred_element_type=jnp.float32
    )
    value_terms = lax.dot_general(
        value_change, whole_tokens, contract_rows, preferred_element_type=jnp.float32
    )
    grad_query, grad_key, grad_value, grad_out = lax.psum(
        (query_terms, key_terms, value_terms, output_terms), "seq"
    )
    input_terms = jnp.dot(query_change, w_query, preferred_element_type=jnp.float32)
    input_terms = input_terms + jnp.dot(key_change, w_key, preferred_element_type=jnp.float32)
    input_terms = input_terms + jnp.dot(value_change, w_value, preferred_element_type=jnp.float32)
    mixed, grad_tokens = (
        lax.psum_scatter(
            mixed_terms.astype(jnp.bfloat16), "head", scatter_dimension=0, tiled=True
        ).astype(jnp.float32),
        lax.psum_scatter(
            input_terms.astype(jnp.bfloat16), "head", scatter_dimension=0, tiled=True
        ).astype(jnp.float32),
    )
    return (
        mixed.astype(jnp.bfloat16),
        grad_tokens.astype(jnp.bfloat16),
        grad_query,
        grad_key,
        grad_value,
        grad_out,
    )


def solution(mesh):
    return jax.shard_map(
        per_device,
        mesh=mesh,
        in_specs=(
            P(("seq", "head"), None),
            P(("seq", "head"), None),
            P("head", None),
            P("head", None),
            P("head", None),
            P("head", None),
            P(),
        ),
        out_specs=(
            P(("seq", "head"), None),
            P(("seq", "head"), None),
            P("head", None),
            P("head", None),
            P("head", None),
            P("head", None),
        ),
        check_vma=False,
    )
```

profile of v0, /device:TPU:1, one launch (start us, length us, event | category | flops | bytes accessed | tf_op | source)
XLA Modules:
  0.0 1044.0 jit_solution(1321595648134753142)
XLA Ops:
  12.0 42.4 %all-gather.3.cloned.1.call-done = bf16[2048,768]{1,0:T(8,128)(2,1)} async-done(((bf16[512,768]{1,0:T(8,128)(2,1)}), bf16[2048,768]{1,0:T(8,128)(2,1)}) %all-gather.3.cloned.1.call-update) | async-done | bytes 3145744 | tf_op jit(solution)/shard_map/all_gather | solution.py:75
  54.5 3.1 convolution_convert_fusion.4
  58.1 1.1 copy.286
  59.2 3.1 convolution_convert_fusion.3
  62.8 1.1 copy.287
  63.9 4.0 convolution_convert_fusion.2
  67.9 1.5 copy.235
  69.3 2.2 copy.288
  71.6 26.0 %all-gather.5.cloned.1.call-done = bf16[2048,768]{1,0:T(8,128)(2,1)} async-done(((bf16[512,768]{1,0:T(8,128)(2,1)}), bf16[2048,768]{1,0:T(8,128)(2,1)}) %all-gather.5.cloned.1.call-update) | async-done | bytes 3145744 | tf_op jit(solution)/shard_map/all_gather | solution.py:76
  97.6 3.9 convolution_convert_fusion.1
  101.5 2.2 copy.253
  103.7 1.4 copy.290
  105.3 3.8 select_reduce_fusion.4
  110.9 3.0 select_reduce_fusion
  113.9 2.7 fusion.10
  117.3 1.4 collective-permute-start
  123.3 1.7 copy.254
  124.9 1.5 copy.257
  130.0 2.8 collective-permute-start.1
  132.8 1.1 broadcast_select_fusion.11
  135.0 4.3 collective-permute-done.1
  139.4 4.2 collective-permute-start.2
  144.1 11.6 %collective-permute-done.2 = bf16[320,384]{1,0:T(8,128)(2,1)S(1)} collective-permute-done((bf16[320,384]{1,0:T(8,128)(2,1)S(1)}, bf16[320,384]{1,0:T(8,128)(2,1)S(1)}, u32[]{:S(2)}, u32[]{:S(2)}) %collective-permute-start.2) | collective-permute-done | bytes 245792 | tf_op jit(solution)/shard_map/ppermute | solution.py:13
  155.7 1.3 collective-permute-start.3
  158.2 1.2 collective-permute-done.3
  160.4 2.8 collective-permute-start.4
  163.7 2.8 collective-permute-done.4
  166.9 1.8 fusion.49
  169.0 2.0 select_reduce_fusion.10
  171.1 1.1 convolution_bitcast_fusion.1
  176.2 1.7 broadcast_select_fusion.5
  178.1 1.7 copy.248
  180.1 1.7 copy.249
  181.9 4.6 convert_multiply_fusion
  186.5 1.6 reduce_sum.268
  195.9 1.6 copy.259
  197.5 2.0 copy.267
  199.5 2.0 copy.271
  201.5 1.9 select_convert_fusion
  203.4 2.8 collective-permute-start.5
  206.2 1.2 select_reduce_fusion.8
  207.4 1.4 multiply_convert_fusion
  209.9 2.5 broadcast_select_fusion.4
  212.4 1.8 copy.264
  215.7 1.5 copy-done.64
  217.2 1.6 fusion.62
  218.9 1.3 convert_add_fusion.2
  220.7 3.0 collective-permute-done.6
  223.9 2.8 collective-permute-start.7
  226.9 6.1 collective-permute-done.7
  234.2 6.7 collective-permute-done.8
  241.1 3.5 fusion.25
  244.6 3.0 collective-permute-done.9
  249.3 1.3 copy-done.65
  250.6 1.7 fusion.17
  252.3 1.9 fusion.14
  254.2 2.7 convolution_convert_fusion
  257.8 2.2 fusion.56
  261.0 2.9 add_convert_fusion
  263.9 644.0 %all-reduce.3.cloned.1.call-done = (f32[192,768]{1,0:T(8,128)}, f32[192,768]{1,0:T(8,128)}, f32[192,768]{1,0:T(8,128)}, f32[192,768]{1,0:T(8,128)}) async-done(((f32[192,768]{1,0:T(8,128)}, f32[192,768]{1,0:T(8,128)}, f32[192,768]{1,0:T(8,128)}, f32[192,768]{1,0:T(8,128)}), (f32[192,768]{1,0:T(8,128)}, f32[192,768]{1,0:T(8,128)}, f32[192,768]{1,0:T(8,128)}, ...) | async-done | bytes 2359312 | tf_op jit(solution)/shard_map/psum | solution.py:207
  907.9 80.4 %reduce-scatter.3.cloned.1.call-done = bf16[512,768]{1,0:T(8,128)(2,1)} async-done(((bf16[2048,768]{1,0:T(8,128)(2,1)}), bf16[512,768]{1,0:T(8,128)(2,1)}) %reduce-scatter.3.cloned.1.call-update) | async-done | bytes 786448 | tf_op jit(solution)/shard_map/reduce_scatter | solution.py:214
  988.3 43.5 %reduce-scatter.5.cloned.1.call-done = bf16[512,768]{1,0:T(8,128)(2,1)} async-done(((bf16[2048,768]{1,0:T(8,128)(2,1)}), bf16[512,768]{1,0:T(8,128)(2,1)}) %reduce-scatter.5.cloned.1.call-update) | async-done | bytes 786448 | tf_op jit(solution)/shard_map/reduce_scatter | solution.py:217
  1031.8 1.9 copy.299
  1033.7 1.9 copy.300
  (262 shorter events, 43.8 us)
Async XLA Ops:
  7.2 90.4 %copy-start = (bf16[192,768]{1,0:T(8,128)(2,1)S(1)}, bf16[192,768]{1,0:T(8,128)(2,1)}, u32[]{:S(2)}) copy-start(bf16[192,768]{1,0:T(8,128)(2,1)} %param.12) | copy-start | bytes 884740
  7.2 47.3 %all-gather.3.cloned.1.call-start = ((), (), s32[]{:S(2)}) async-start(), calls=%async_computation.2 | async-start | bytes 3932160 | tf_op jit(solution)/shard_map/all_gather | solution.py:75
  7.9 89.7 %all-gather.5.cloned.1.call-start = ((), (), s32[]{:S(2)}) async-start(), calls=%async_computation.4 | async-start | bytes 3932160 | tf_op jit(solution)/shard_map/all_gather | solution.py:76
  8.7 899.3 %all-reduce.3.cloned.1.call-start = ((), (), s32[]{:S(2)}) async-start(), calls=%async_computation.6 | async-start | bytes 4718592 | tf_op jit(solution)/shard_map/psum | solution.py:207
  9.5 2.4 copy-start.63
  9.5 48.1 %copy-start.62 = (s32[3]{0:T(128)}, s32[3]{0:T(128)S(1)}, u32[]{:S(2)}) copy-start(s32[3]{0:T(128)S(1)} %get-tuple-element.52) | copy-start | bytes 40
  10.9 107.8 %copy-start.50 = (pred[8,192]{1,0:T(8,128)(4,1)}, pred[8,192]{1,0:T(8,128)(4,1)S(1)}, u32[]{:S(2)}) copy-start(pred[8,192]{1,0:T(8,128)(4,1)S(1)} %broadcast_in_dim.385) | copy-start | bytes 4612
  10.9 109.1 %copy-start.54 = (pred[32,3]{0,1:T(4,128)(4,1)}, pred[32,3]{0,1:T(4,128)(4,1)S(1)}, u32[]{:S(2)}) copy-start(pred[32,3]{0,1:T(4,128)(4,1)S(1)} %iota_compare_fusion.1) | copy-start | bytes 292
  12.0 108.9 %copy-start.56 = (pred[128,3]{0,1:T(4,128)(4,1)}, pred[128,3]{0,1:T(4,128)(4,1)S(1)}, u32[]{:S(2)}) copy-start(pred[128,3]{0,1:T(4,128)(4,1)S(1)} %iota_compare_fusion) | copy-start | bytes 1156
  12.0 93.1 %copy-start.29 = (pred[128,3,64]{0,2,1:T(8,128)(4,1)}, pred[128,3,64]{0,2,1:T(8,128)(4,1)S(1)}, u32[]{:S(2)}) copy-start(pred[128,3,64]{0,2,1:T(8,128)(4,1)S(1)} %broadcast_in_dim.392) | copy-start | bytes 73732
  110.9 5.6 copy-start.49
  110.9 3.0 copy-start.1
  113.8 2.7 copy-start.39
  113.8 2.7 copy-start.40
  117.3 11.0 %collective-permute-start = (bf16[336,384]{1,0:T(8,128)(2,1)S(1)}, bf16[336,384]{1,0:T(8,128)(2,1)S(1)}, u32[]{:S(2)}, u32[]{:S(2)}) collective-permute-start(bf16[336,384]{1,0:T(8,128)(2,1)S(1)} %maximum_maximum_fusion), channel_id=1, source_target_pairs={{0,4},{4,0},{8,12},{12,8},{16,20},{20,16},{24,28},{28,24},{32,36},... | collective-permute-start | bytes 774152 | tf_op jit(solution)/shard_map/ppermute | solution.py:13
  127.3 35.9 %copy-start.33 = (bf16[64,192]{0,1:T(8,128)(2,1)}, bf16[64,192]{0,1:T(8,128)(2,1)S(1)}, u32[]{:S(2)}) copy-start(bf16[64,192]{0,1:T(8,128)(2,1)S(1)} %copy.239) | copy-start | bytes 73732
  130.0 9.3 collective-permute-start.1
  139.4 16.3 %collective-permute-start.2 = (bf16[320,384]{1,0:T(8,128)(2,1)S(1)}, bf16[320,384]{1,0:T(8,128)(2,1)S(1)}, u32[]{:S(2)}, u32[]{:S(2)}) collective-permute-start(bf16[320,384]{1,0:T(8,128)(2,1)S(1)} %pad_maximum_fusion.7), channel_id=1, source_target_pairs={{0,16},{4,20},{8,24},{12,28},{16,0},{20,4},{24,8},{28,12},{32,48},... | collective-permute-start | bytes 737288 | tf_op jit(solution)/shard_map/ppermute | solution.py:13
  144.1 30.5 %copy-start.6 = (f32[3,256,512]{2,1,0:T(8,128)}, f32[3,256,512]{2,1,0:T(8,128)S(1)}, u32[]{:S(2)}) copy-start(f32[3,256,512]{2,1,0:T(8,128)S(1)} %get-tuple-element.59) | copy-start | bytes 4718596
  155.7 3.7 collective-permute-start.3
  158.2 10.6 %copy-start.17 = (bf16[512,192]{0,1:T(8,128)(2,1)}, bf16[512,192]{0,1:T(8,128)(2,1)S(1)}, u32[]{:S(2)}) copy-start(bf16[512,192]{0,1:T(8,128)(2,1)S(1)} %copy.240) | copy-start | bytes 589828
  160.3 8.6 copy-start.59
  160.4 8.6 copy-start.61
  160.4 6.1 collective-permute-start.4
  163.5 9.7 copy-start.21
  166.7 6.9 copy-start.46
  166.9 7.8 copy-start.19
  166.9 6.5 copy-start.27
  169.0 4.1 copy-start.44
  173.3 2.4 copy-start.26
  174.8 3.1 copy-start.51
  180.1 1.8 copy-start.5
  181.9 6.3 copy-start.55
  181.9 6.4 copy-start.22
  181.9 6.5 copy-start.28
  186.5 2.9 copy-start.18
  186.5 3.8 copy-start.34
  186.5 4.8 copy-start.38
  186.5 4.8 copy-start.47
  188.1 3.4 copy-start.57
  188.1 3.5 copy-start.45
  188.1 3.7 copy-start.20
  188.4 3.6 copy-start.35
  189.4 4.5 copy-start.23
  195.1 13.7 %copy-start.10 = (f32[512,192]{1,0:T(8,128)}, f32[512,192]{1,0:T(8,128)S(1)}, u32[]{:S(2)}) copy-start(f32[512,192]{1,0:T(8,128)S(1)} %copy.272) | copy-start | bytes 1179652
  195.1 12.3 %copy-start.7 = (f32[3,256,512]{2,1,0:T(8,128)S(1)}, f32[3,256,512]{2,1,0:T(8,128)}, u32[]{:S(2)}) copy-start(f32[3,256,512]{2,1,0:T(8,128)} %copy-done.6) | copy-start | bytes 4718596
  203.4 15.5 %collective-permute-start.5 = (bf16[256,384]{1,0:T(8,128)(2,1)}, bf16[256,384]{1,0:T(8,128)(2,1)}, u32[]{:S(2)}, u32[]{:S(2)}) collective-permute-start(bf16[256,384]{1,0:T(8,128)(2,1)} %select_convert_fusion), channel_id=1, source_target_pairs={{0,64},{4,68},{8,72},{12,76},{16,80},{20,84},{24,88},{28,92},{32,9... | collective-permute-start | bytes 589832 | tf_op jit(solution)/shard_map/ppermute | solution.py:13
  215.3 1.9 copy-start.64
  218.9 1.7 copy-start.9
  218.9 7.8 copy-start.4
  218.9 7.8 copy-start.36
  220.2 3.6 collective-permute-start.6
  223.8 9.6 copy-start.14
  223.9 9.1 collective-permute-start.7
  233.3 7.6 collective-permute-start.8
  241.0 6.6 collective-permute-start.9
  241.1 6.5 copy-start.52
  244.6 3.4 copy-start.48
  248.7 1.9 copy-start.65
  254.2 734.2 %reduce-scatter.3.cloned.1.call-start = ((), (), s32[]{:S(2)}) async-start(), calls=%async_computation.3 | async-start | bytes 3932160 | tf_op jit(solution)/shard_map/reduce_scatter | solution.py:214
  256.9 3.1 copy-start.42
  256.9 774.9 %reduce-scatter.5.cloned.1.call-start = ((), (), s32[]{:S(2)}) async-start(), calls=%async_computation.5 | async-start | bytes 3932160 | tf_op jit(solution)/shard_map/reduce_scatter | solution.py:217
  907.9 127.7 %copy-start.32 = (f32[192,768]{1,0:T(8,128)S(1)}, f32[192,768]{1,0:T(8,128)}, u32[]{:S(2)}) copy-start(f32[192,768]{1,0:T(8,128)} %get-tuple-element.68) | copy-start | bytes 1769476
  907.9 128.5 %copy-start.31 = (f32[192,768]{1,0:T(8,128)S(1)}, f32[192,768]{1,0:T(8,128)}, u32[]{:S(2)}) copy-start(f32[192,768]{1,0:T(8,128)} %get-tuple-element.69) | copy-start | bytes 1769476
  (17 other events, 19.8 us)
Sparse Core Ops, SparseCore 0:
  9.8 44.5 all-gather.2
  56.3 41.2 all-gather.4
  254.3 653.5 all-reduce.2
  911.1 77.2 reduce-scatter.2
  991.5 40.2 reduce-scatter.4
where the time goes:
time: 1050 us; the launch traced here: 1040 us
  waiting for transfers between devices  876 us (83%)
  local copies, waits for them, and re-layouts  51.8 us (5%)
  matrix products  43.3 us (4%)
  other arithmetic  38.5 us (4%)
  starting transfers between devices  19.1 us (2%)
  between operations  15.1 us (1%)
    psum x1, waiting for transfers between devices, per_device(): lax.psum((query_terms, key_terms, value_terms, output_terms), 'seq')  644 us
    reduce_scatter x1, waiting for transfers between devices, per_device(): lax.psum_scatter(mixed_terms.astype(jnp.bfloat16), 'head', scatter_dimens...  80.4 us
    reduce_scatter x1, waiting for transfers between devices, per_device(): lax.psum_scatter(input_terms.astype(jnp.bfloat16), 'head', scatter_dimens...  43.5 us
    all_gather x1, waiting for transfers between devices, per_device(): lax.all_gather(tokens, 'head', axis=0, tiled=True)  42.4 us
    ppermute x10, waiting for transfers between devices, swapped(): return lax.ppermute(value, axis, pairs)  38.6 us
    all_gather x1, waiting for transfers between devices, per_device(): lax.all_gather(cotangent, 'head', axis=0, tiled=True)  26 us
  transfers between devices with their start and end apart: 15, of which 13 were waited for; matrix products, arithmetic and copies ran while one was open for 5% of the time, Pallas kernels for 0%

commit v1 on v0

v1 whole, which is shorter than its diff:
```python
import functools

import jax
import jax.numpy as jnp
from jax import lax
from jax.experimental import pallas as pl
from jax.experimental.pallas import tpu as pltpu
from jax.sharding import PartitionSpec as P

BF = jnp.bfloat16
F32 = jnp.float32
WIDTH = 768
ROWS = 512
SLOT = 256
PER_HEAD = 336
SPANS = ((0, 256), (256, 320), (320, 336))
SCALE = 0.125
HEAD_AXES = ("yl", "core")


def nn(a, b):
    return jnp.dot(a, b, preferred_element_type=F32)


def nt(a, b):
    return lax.dot_general(a, b, (((1,), (1,)), ((), ())), preferred_element_type=F32)


def tn(a, b):
    return lax.dot_general(a, b, (((0,), (0,)), ((), ())), preferred_element_type=F32)


def iota(shape, dim):
    return lax.broadcasted_iota(jnp.int32, shape, dim)


def ones_where(mask):
    return jnp.where(mask, 1.0, 0.0).astype(BF)


def pick_first(offs, group):
    row, col = iota((64, ROWS), 0), iota((64, ROWS), 1)
    return jnp.concatenate([ones_where(8 * row + offs[0, 3 * group + a] == col) for a in range(3)], 0)


def pick_rest(offs, group):
    row, col = iota((16, ROWS), 0), iota((16, ROWS), 1)
    parts = [ones_where(32 * row + offs[1, 3 * group + a] == col) for a in range(3)]
    third = [offs[2, 3 * group + a] for a in range(3)]
    off = jnp.where(row < 4, third[0], jnp.where(row < 8, third[1], jnp.where(row < 12, third[2], 4 * ROWS)))
    parts.append(ones_where(128 * (row & 3) + off == col))
    return jnp.concatenate(parts, 0)


def spread_matrix(offs, group):
    lane = iota((1, SLOT), 1)
    o = [[offs[level, 3 * group + a] for a in range(3)] for level in range(3)]
    first = 8 * (lane & 63) + jnp.where(lane < 64, o[0][0], jnp.where(lane < 128, o[0][1], o[0][2]))
    second = 32 * (lane & 15) + jnp.where(lane < 208, o[1][0], jnp.where(lane < 224, o[1][1], o[1][2]))
    third = 128 * (lane & 3) + jnp.where(
        lane < 244, o[2][0], jnp.where(lane < 248, o[2][1], jnp.where(lane < 252, o[2][2], 4 * ROWS))
    )
    pos = jnp.where(lane < 192, first, jnp.where(lane < 240, second, third))
    return ones_where(iota((ROWS, SLOT), 0) == pos)


def third_order(dim):
    new, old = iota((64, 64), dim), iota((64, 64), 1 - dim)
    source = 16 * ((new >> 2) & 3) + 4 * (new >> 4) + (new & 3)
    return ones_where((source == old) & (new < 48))


def call(body, outs, scratch=(), smem=0, flops=0, nbytes=4 << 20):
    def run(*args):
        vmem = pl.BlockSpec(memory_space=pltpu.VMEM)
        specs = [pl.BlockSpec(memory_space=pltpu.SMEM)] * smem + [vmem] * (len(args) - smem)
        return pl.pallas_call(
            body,
            out_shape=tuple(jax.ShapeDtypeStruct(shape, kind) for shape, kind in outs),
            in_specs=specs,
            out_specs=tuple(vmem for _ in outs),
            scratch_shapes=[pltpu.VMEM(shape, kind) for shape, kind in scratch],
            compiler_params=pltpu.CompilerParams(vmem_limit_bytes=40 << 20),
            cost_estimate=pl.CostEstimate(flops=flops, bytes_accessed=nbytes, transcendentals=0),
        )(*args)

    return run


def pick_kernel(first, rest, offs, where, source, *outs):
    for k in (2, 3, 1, 0):
        group = where[0] ^ k
        parts = ([pick_first(offs, group)] if first else []) + ([pick_rest(offs, group)] if rest else [])
        outs[k][...] = nn(jnp.concatenate(parts, 0), source[...]).astype(BF)


def regroup_rest(rests, whole):
    third = jnp.concatenate([rest[48:64] for rest in rests], 0)
    third = nn(third_order(0), third).astype(BF)
    for a in range(3):
        for k in range(4):
            whole[80 * a + 16 * k : 80 * a + 16 * k + 16] = rests[k][16 * a : 16 * a + 16]
        whole[80 * a + 64 : 80 * a + 80] = third[16 * a : 16 * a + 16]


def regroup_first(firsts, whole):
    for a in range(3):
        for k in range(4):
            whole[256 * a + 64 * k : 256 * a + 64 * k + 64] = firsts[k][64 * a : 64 * a + 64]


def ungroup(parts, slots):
    third = jnp.concatenate([part[320:336] for part in parts] + [jnp.zeros((16, WIDTH), BF)], 0)
    third = nn(third_order(1), third).astype(BF)
    for k in range(4):
        for a in range(3):
            slots[k][64 * a : 64 * a + 64] = parts[a][64 * k : 64 * k + 64]
            slots[k][192 + 16 * a : 208 + 16 * a] = parts[a][256 + 16 * k : 272 + 16 * k]
        slots[k][240:256] = third[16 * k : 16 * k + 16]


def join_kernel(w_query, w_key, w_value, joined):
    for a in range(3):
        own = slice(64 * a, 64 * a + 64)
        joined[256 * a : 256 * a + 64] = w_key[own]
        joined[256 * a + 64 : 256 * a + 128] = w_value[own]
        joined[256 * a + 128 : 256 * a + 192] = w_query[own]
        joined[256 * a + 192 : 256 * a + 256] = jnp.zeros((64, WIDTH), BF)


def pad_out(w_out, a):
    return jnp.concatenate([jnp.zeros((64, WIDTH), BF), w_out[64 * a : 64 * a + 64]], 0)


def project_rest_kernel(x0, x1, x2, x3, joined, whole, query, rest):
    regroup_rest((x0, x1, x2, x3), whole)
    for a in range(3):
        made = nt(whole[80 * a : 80 * a + 80], joined[256 * a : 256 * a + 256]).astype(BF)
        query[80 * a : 80 * a + 80] = made[:, 128:256]
        for k in range(8):
            rest[k, 64 * a : 64 * a + 64] = made[0:64, 0:128]
            rest[k, 192 + 16 * a : 208 + 16 * a] = made[64:80, 0:128]


def project_first_kernel(x0, x1, x2, x3, joined, whole, query, first):
    regroup_first((x0, x1, x2, x3), whole)
    for a in range(3):
        own = slice(256 * a, 256 * a + 256)
        made = nt(whole[own], joined[own]).astype(BF)
        query[own] = made[:, 128:256]
        first[own] = made[:, 0:128]


def rows_of(first, rest, a):
    return jnp.concatenate([first[256 * a : 256 * a + 256], rest[80 * a : 80 * a + 80]], 0)


def grad_rows_kernel(c0, c1, c2, c3, w_out, whole_first, whole_rest, grads):
    slots = (c0, c1, c2, c3)
    regroup_first(slots, whole_first)
    regroup_rest([slot.at[192:256] for slot in slots], whole_rest)
    for a in range(3):
        base = PER_HEAD * a
        grads[base : base + PER_HEAD] = nt(rows_of(whole_first, whole_rest, a), pad_out(w_out, a)).astype(BF)


def attention_kernel(offs, where, query_first, query_rest, grads, first_own, first_other, rest, *refs):
    thirds = refs[:3]
    attended, query_grad, first_back, first_send, second_back = refs[3:8]
    third_back, keys = refs[8:12], refs[12]
    for a in range(3):
        keys[a, 0:256] = first_own[256 * a : 256 * a + 256]
        keys[a, 256:512] = first_other[256 * a : 256 * a + 256]
        for k in range(8):
            keys[3 + a, 64 * k : 64 * k + 64] = rest[k, 64 * a : 64 * a + 64]
            keys[6 + a, 16 * k : 16 * k + 16] = rest[k, 192 + 16 * a : 208 + 16 * a]
            for j in range(3):
                keys[6 + a, 128 * (j + 1) + 16 * k : 128 * (j + 1) + 16 * k + 16] = thirds[j][
                    k, 16 * a : 16 * a + 16
                ]

    def position(index, a):
        o = [offs[level, 3 * where[0] + a] for level in range(3)]
        return jnp.where(
            index < 256,
            8 * index + o[0],
            jnp.where(index < 320, 32 * (index - 256) + o[1], 128 * (index - 320) + o[2]),
        )

    for a in range(3):
        base = PER_HEAD * a
        q, g = rows_of(query_first, query_rest, a), grads[base : base + PER_HEAD]
        same = jnp.where(
            position(iota((PER_HEAD, 1), 0), a) == position(iota((1, PER_HEAD), 1), a), 1.0, 0.0
        ).astype(F32)

        def over_levels(column):
            wide = jnp.broadcast_to(column, (PER_HEAD, 128))
            return jnp.dot(same, wide, precision=lax.Precision.HIGHEST, preferred_element_type=F32)[:, 0:1]

        expo = [
            jnp.exp(nt(q[low:high], keys[3 * level + a]) * SCALE) for level, (low, high) in enumerate(SPANS)
        ]
        total = over_levels(jnp.concatenate([jnp.sum(e, 1, keepdims=True) for e in expo], 0))
        inverse = 1.0 / total
        weights = [e * inverse[low:high] for e, (low, high) in zip(expo, SPANS)]
        rounded = [w.astype(BF) for w in weights]
        out = jnp.concatenate([nn(rounded[level], keys[3 * level + a]) for level in range(3)], 0)
        attended[base : base + PER_HEAD] = out.astype(BF)
        delta = over_levels(jnp.sum(g.astype(F32) * out, 1, keepdims=True))
        for level, (low, high) in enumerate(SPANS):
            block = keys[3 * level + a]
            back = nt(g[low:high], block)
            score = (weights[level] * (back - delta[low:high]) * SCALE).astype(BF)
            query_grad[base + low : base + high] = nn(score, block).astype(BF)
            pair = (tn(score, q[low:high]) + tn(rounded[level], g[low:high])).astype(BF)
            if level == 0:
                first_back[256 * a : 256 * a + 256] = pair[0:256]
                first_send[256 * a : 256 * a + 256] = pair[256:512]
            elif level == 1:
                for k in range(8):
                    second_back[k, 64 * a : 64 * a + 64] = pair[64 * k : 64 * k + 64]
            else:
                for j in range(4):
                    for k in range(8):
                        third_back[j][k, 16 * a : 16 * a + 16] = pair[128 * j + 16 * k : 128 * j + 16 * k + 16]


def put_chunks(place, held, chunks, sends):
    for c in range(64):
        chunks[c // 16, c % 16] = held[36 * c : 36 * c + 36].astype(BF)
    for k in range(4):
        sends[k][...] = chunks[place[0] ^ k]


def put_grad(held, kind, a, value):
    for b in range(6):
        start = 384 * b + 192 * kind + 64 * a
        held[start : start + 64] = value[:, 128 * b : 128 * b + 128]


def early_kernel(place, attended, query_grad, c_first, c_rest, x_first, x_rest, *refs):
    sends, held, chunks = refs[:4], refs[4], refs[5]
    for a in range(3):
        own = slice(PER_HEAD * a, PER_HEAD * a + PER_HEAD)
        put_grad(held, 0, a, tn(query_grad[own], rows_of(x_first, x_rest, a))[0:64])
        put_grad(held, 1, a, tn(attended[own], rows_of(c_first, c_rest, a))[64:128])
    put_chunks(place, held, chunks, sends)


def output_kernel(attended, w_out, s0, s1, s2, s3):
    parts = []
    for a in range(3):
        own = slice(PER_HEAD * a, PER_HEAD * a + PER_HEAD)
        parts.append(nn(attended[own], pad_out(w_out, a)).astype(BF))
    ungroup(parts, (s0, s1, s2, s3))


def total_of(parts, count):
    return functools.reduce(lambda x, y: x + y, [parts[k].astype(F32) for k in range(count)])


def third_sum_kernel(second, t0, t1, t2, t3, sends):
    for k in range(8):
        sends[k, 0:192] = second[k]
        sends[k, 192:240] = total_of([t[k] for t in (t0, t1, t2, t3)], 4).astype(BF)


def change_kernel(place, first_own, first_other, rests, query_grad, x_first, x_rest, *refs):
    sends, changes, held, chunks = refs[:4], refs[4], refs[5], refs[6]
    first = first_own[...].astype(F32) + first_other[...].astype(F32)
    rest = total_of(rests, 8)
    for a in range(3):
        own = slice(PER_HEAD * a, PER_HEAD * a + PER_HEAD)
        pair = jnp.concatenate(
            [first[256 * a : 256 * a + 256], rest[64 * a : 64 * a + 64], rest[192 + 16 * a : 208 + 16 * a]], 0
        ).astype(BF)
        made = tn(pair, rows_of(x_first, x_rest, a))
        put_grad(held, 0, a, made[0:64])
        put_grad(held, 1, a, made[64:128])
        changes[own] = jnp.concatenate([pair, query_grad[own]], 1)
    put_chunks(place, held, chunks, sends)


def input_kernel(changes, joined, s0, s1, s2, s3):
    parts = []
    for a in range(3):
        own = slice(PER_HEAD * a, PER_HEAD * a + PER_HEAD)
        parts.append(nn(changes[own], joined[256 * a : 256 * a + 256]).astype(BF))
    ungroup(parts, (s0, s1, s2, s3))


def x_sum_kernel(*refs):
    out, held = refs[8], refs[9]
    for y in range(16):
        for half in range(2):
            held[36 * half : 36 * half + 36] = total_of([part[y] for part in refs[4 * half : 4 * half + 4]], 4)
        out[y] = held[...].astype(BF)


def yz_sum_kernel(got, sends):
    total = total_of(got, 16).astype(BF)
    for y in range(16):
        sends[y] = total


def place_kernel(place, b0, b1, b2, b3, *refs):
    outs, chunks, wide, held = refs[:4], refs[4], refs[5], refs[6]
    for k, block in enumerate((b0, b1, b2, b3)):
        chunks[place[0] ^ k] = block[...]
    for c in range(64):
        wide[...] = chunks[c // 16, c % 16].astype(F32)
        for half in range(2):
            held[half, 36 * c : 36 * c + 36] = wide[36 * half : 36 * half + 36]
    for half in range(2):
        for kind in range(2):
            for b in range(6):
                start = 384 * b + 192 * kind
                outs[2 * half + kind][:, 128 * b : 128 * b + 128] = held[half, start : start + 192]


def spread_kernel(offs, where, s0, s1, s2, s3, out):
    total = None
    for k, slot in enumerate((s0, s1, s2, s3)):
        term = nn(spread_matrix(offs, where[0] ^ k), slot[...])
        total = term if total is None else total + term
    out[...] = total.astype(BF)


def swap(value, axis, k):
    count = lax.axis_size(axis)
    return lax.ppermute(value, axis, [(i, i ^ k) for i in range(count)])


def deal(value, axis):
    return lax.all_to_all(value, axis, 0, 0, tiled=True)


YZ_AXES = ("yh", "z")


def per_device(tokens, cotangent, w_query, w_key, w_value, w_out, offsets):
    where = lax.axis_index(HEAD_AXES).reshape(1).astype(jnp.int32)
    place = lax.axis_index("x").reshape(1).astype(jnp.int32)

    def picked(source, first, rest, index):
        shape = ((192 * first + 64 * rest, WIDTH), BF)
        body = functools.partial(pick_kernel, first, rest)
        flops = 8 * shape[0][0] * 512 * 768
        return list(call(body, [shape] * 4, smem=2, flops=flops)(offsets, index, source))

    def to_heads(slots):
        return [slots[0]] + [swap(slots[k], HEAD_AXES, k) for k in (1, 2, 3)]

    tie = lax.optimization_barrier
    (joined,) = call(join_kernel, [((768, WIDTH), BF)])(w_query, w_key, w_value)
    token_rest = to_heads(picked(tokens, 0, 1, where))
    token_first, grad_rows = picked(tokens, 1, 0, where), picked(cotangent, 1, 1, where)
    token_rest[2], token_rest[3], token_first = tie((token_rest[2], token_rest[3], token_first))
    token_first, grad_rows = to_heads(token_first), to_heads(grad_rows)
    token_rest, token_first[0], grad_rows[0], joined = tie((token_rest, token_first[0], grad_rows[0], joined))

    half_chunks, full_chunks = ((16, 36, 128), BF), ((16, 72, 128), BF)
    halves = [((2304, 128), F32), ((4, 16, 36, 128), BF)]
    wide, half, short = ((3 * PER_HEAD, 128), BF), ((768, 128), BF), ((240, 128), BF)
    rest_shape, second_shape, third_shape = ((8, 240, 128), BF), ((8, 192, 128), BF), ((8, 48, 128), BF)
    whole_first, whole_rest = ((768, WIDTH), BF), ((240, WIDTH), BF)
    slot = ((SLOT, WIDTH), BF)

    x_rest, query_rest, rest = call(
        project_rest_kernel, [whole_rest, short, rest_shape], flops=2 * 240 * 768 * 256
    )(*token_rest, joined)
    rest, token_first[2] = tie((rest, token_first[2]))
    rest = deal(rest, "z")
    x_first, query_first, first = call(
        project_first_kernel, [whole_first, half, half], flops=2 * 768 * 768 * 256
    )(*token_first, joined)
    first_other = swap(first, "z", 1)
    third, x_first = tie((rest[:, 192:240], x_first))
    thirds = [swap(third, "x", j) for j in (1, 2, 3)]
    c_first, c_rest, grads = call(
        grad_rows_kernel, [whole_first, whole_rest, wide], flops=2 * 1008 * 768 * 128
    )(*grad_rows, w_out)

    attended, query_grad, first_back, first_send, second_back, *third_back = call(
        attention_kernel,
        [wide, wide, half, half, second_shape] + [third_shape] * 4,
        scratch=[((9, 512, 128), BF)],
        smem=2,
        flops=2 * 1008 * 512 * 128 * 7,
    )(offsets, where, query_first, query_rest, grads, first, first_other, rest, *thirds)

    third_got = [third_back[0]] + [swap(third_back[j], "x", j) for j in (1, 2, 3)]
    first_got = swap(first_send, "z", 1)
    early = call(early_kernel, [half_chunks] * 4, scratch=halves, smem=1, flops=4 * 1008 * 768 * 128)(
        place, attended, query_grad, c_first, c_rest, x_first, x_rest
    )
    mixed_slots = call(output_kernel, [slot] * 4, flops=2 * 1008 * 768 * 128)(attended, w_out)
    mixed_slots = to_heads(mixed_slots)
    early = [early[0]] + [swap(early[k], "x", k) for k in (1, 2, 3)]
    third_got, first_got, mixed_slots[0], early[0] = tie((third_got, first_got, mixed_slots[0], early[0]))
    (rest_back,) = call(third_sum_kernel, [rest_shape])(second_back, *third_got)
    rest_got = deal(rest_back, "z")
    rest_got, early = tie((rest_got, early))

    *late, changes = call(
        change_kernel,
        [half_chunks] * 4 + [((3 * PER_HEAD, 256), BF)],
        scratch=halves,
        smem=1,
        flops=2 * 1008 * 768 * 128,
    )(place, first_back, first_got, rest_got, query_grad, x_first, x_rest)
    late = [late[0]] + [swap(late[k], "x", k) for k in (1, 2, 3)]
    change_slots = call(input_kernel, [slot] * 4, flops=2 * 1008 * 768 * 256)(changes, joined)
    spread = call(spread_kernel, [((ROWS, WIDTH), BF)], smem=2, flops=2 * 1024 * 512 * 768)
    (mixed,) = spread(offsets, where, *mixed_slots)
    (parts,) = call(x_sum_kernel, [full_chunks], scratch=[((72, 128), F32)])(*early, *late)
    (part,) = call(yz_sum_kernel, [full_chunks])(deal(parts, YZ_AXES))
    part, mixed, change_slots = tie((part, mixed, change_slots))
    block, change_slots = deal(part, YZ_AXES), to_heads(change_slots)
    blocks = [block] + [swap(block, "x", k) for k in (1, 2, 3)]
    (grad_tokens,) = spread(offsets, where, *change_slots)
    grad_query, grad_out, grad_key, grad_value = call(
        place_kernel,
        [((192, WIDTH), F32)] * 4,
        scratch=[((4, 16, 72, 128), BF), ((72, 128), F32), ((2, 2304, 128), F32)],
        smem=1,
    )(place, *blocks)
    return mixed, grad_tokens, grad_query, grad_key, grad_value, grad_out


def solution(mesh):
    fine = jax.sharding.Mesh(mesh.devices.reshape(2, 4, 8, 2, 2), ("yh", "x", "z", "yl", "core"))
    rows = P(("yh", "x", "z", "yl", "core"), None)
    cut = P(HEAD_AXES, None)
    return jax.shard_map(
        per_device,
        mesh=fine,
        in_specs=(rows, rows, cut, cut, cut, cut, P()),
        out_specs=(rows, rows, cut, cut, cut, cut),
        check_vma=False,
    )
```

time: 1050 us -> 204 us (0.19)
  waiting for transfers between devices: 876 us -> 70.6 us
  starting transfers between devices: 19.1 us -> 67.4 us
  matrix products: 43.3 us -> 0 us
  other arithmetic: 38.5 us -> 0 us
  Pallas kernels: 0 us -> 33.3 us
  local copies, waits for them, and re-layouts: 51.8 us -> 29.1 us
  between operations: 15.1 us -> 0.97 us
    psum x1 -> x0, waiting for transfers between devices: 644 us -> none  [per_device(): lax.psum((query_terms, key_terms, value_terms, output_terms), 'seq')]
    reduce_scatter x2 -> x0, waiting for transfers between devices: 124 us -> none  [the longest x1 80.4 us: per_device(): lax.psum_scatter(mixed_terms.astype(jnp.bfloat16), 'head', scatter_dimens...]
    all_gather x2 -> x0, waiting for transfers between devices: 68.4 us -> none  [the longest x1 42.4 us: per_device(): lax.all_gather(tokens, 'head', axis=0, tiled=True)]
    dot_general x30 -> x0, matrix products: 43.3 us -> none  [the longest x1 3.95 us: per_device(): lax.dot_general(whole_tokens, w_query, contract_cols, preferred_element_t...]
    pallas_call x0 -> x18, Pallas kernels: none -> 33.3 us  [run(): pl.pallas_call(body, out_shape=tuple((jax.ShapeDtypeStruct(shape, kind) f...]
    all_to_all x0 -> x4, starting transfers between devices: none -> 28 us  [deal(): return lax.all_to_all(value, axis, 0, 0, tiled=True)]
    ppermute x10 -> x32, waiting for transfers between devices: 38.6 us -> 60 us  [swap(): return lax.ppermute(value, axis, [(i, i ^ k) for i in range(count)])]
    ppermute x10 -> x32, starting transfers between devices: 18.7 us -> 39.4 us  [swap(): return lax.ppermute(value, axis, [(i, i ^ k) for i in range(count)])]
  transfers between devices with their start and end apart: 15 -> 36, of which waited for: 13 -> 16; matrix products, arithmetic and copies ran while one was open for 5% -> 0% of each run, Pallas kernels for 0% -> 8%
where the time goes in v1:
time: 204 us; the launch traced here: 201 us
  waiting for transfers between devices  70.6 us (35%)
  starting transfers between devices  67.4 us (33%)
  Pallas kernels  33.3 us (16%)
  local copies, waits for them, and re-layouts  29.1 us (14%)
    ppermute x32, waiting for transfers between devices, swap(): return lax.ppermute(value, axis, [(i, i ^ k) for i in range(count)])  60 us
    ppermute x32, starting transfers between devices, swap(): return lax.ppermute(value, axis, [(i, i ^ k) for i in range(count)])  39.4 us
    pallas_call x18, Pallas kernels, run(): pl.pallas_call(body, out_shape=tuple((jax.ShapeDtypeStruct(shape, kind) f...  33.3 us
    unnamed x114, local copies, waits for them, and re-layouts  29.1 us
    all_to_all x4, starting transfers between devices, deal(): return lax.all_to_all(value, axis, 0, 0, tiled=True)  28 us
    all_to_all x4, waiting for transfers between devices, deal(): return lax.all_to_all(value, axis, 0, 0, tiled=True)  10.6 us
  transfers between devices with their start and end apart: 36, of which 16 were waited for; matrix products, arithmetic and copies ran while one was open for 0% of the time, Pallas kernels for 8%

profile of v1, /device:TPU:1, one launch (start us, length us, event | category | flops | bytes accessed | tf_op | source)
XLA Modules:
  0.0 201.4 jit_solution(2383263182290094063)
XLA Ops:
  0.6 1.1 copy-done.2
  2.5 1.2 shard_map.118
  3.7 2.2 %collective-permute-start.1 = (bf16[64,768]{1,0:T(8,128)(2,1)S(1)}, bf16[64,768]{1,0:T(8,128)(2,1)S(1)}, u32[]{:S(2)}, u32[]{:S(2)}) collective-permute-start(bf16[64,768]{1,0:T(8,128)(2,1)S(1)} %get-tuple-element.94), channel_id=1, source_target_pairs={{0,2},{1,3},{2,0},{3,1},{4,6},{5,7},{6,4},{7,5},{8,10},{9,11},{10,... | collective-permute-start | bytes 294920 | tf_op jit(solution)/shard_map/ppermute | solution.py:332
  5.9 2.7 %collective-permute-start.2 = (bf16[64,768]{1,0:T(8,128)(2,1)S(1)}, bf16[64,768]{1,0:T(8,128)(2,1)S(1)}, u32[]{:S(2)}, u32[]{:S(2)}) collective-permute-start(bf16[64,768]{1,0:T(8,128)(2,1)S(1)} %get-tuple-element.95), channel_id=1, source_target_pairs={{0,3},{1,2},{2,1},{3,0},{4,7},{5,6},{6,5},{7,4},{8,11},{9,10},{10,... | collective-permute-start | bytes 294920 | tf_op jit(solution)/shard_map/ppermute | solution.py:332
  8.7 1.4 shard_map.119
  11.5 1.1 collective-permute-done.2.x3
  12.6 1.1 collective-permute-start
  13.9 2.2 %shard_map.120 = (bf16[256,768]{1,0:T(8,128)(2,1)S(1)}, bf16[256,768]{1,0:T(8,128)(2,1)}, bf16[256,768]{1,0:T(8,128)(2,1)}, bf16[256,768]{1,0:T(8,128)(2,1)}) custom-call(s32[3,12]{1,0:T(4,128)S(1)} %copy-done.33, s32[1]{0:T(128)} %bitcast.where, bf16[512,768]{1,0:T(8,128)(2,1)S(1)} %copy-done.35), custom_call_target="tpu_custom_call" | custom-call | flops 805306368 | bytes 4194304 | tf_op jit(solution)/shard_map/pallas_call | solution.py:77
  16.8 1.3 shard_map.122
  18.7 2.8 %collective-permute-done.4.x2 = bf16[192,768]{1,0:T(8,128)(2,1)S(1)} collective-permute-done((bf16[192,768]{1,0:T(8,128)(2,1)S(1)}, bf16[192,768]{1,0:T(8,128)(2,1)S(1)}, u32[]{:S(2)}, u32[]{:S(2)}) %collective-permute-start.4) | collective-permute-done | bytes 294944 | tf_op jit(solution)/shard_map/ppermute | solution.py:332
  21.5 6.4 %all-to-all-start = ((bf16[8,240,128]{2,1,0:T(8,128)(2,1)}), bf16[8,240,128]{2,1,0:T(8,128)(2,1)S(1)}, u32[]{:S(2)}, u32[]{:S(2)}) async-start(bf16[8,240,128]{2,1,0:T(8,128)(2,1)} %get-tuple-element.123), calls=%async_computation | async-start | bytes 983040 | tf_op jit(solution)/shard_map/all_to_all | solution.py:336
  28.0 1.6 collective-permute-start.3
  29.6 1.0 collective-permute-start.5
  31.5 1.2 collective-permute-start.8
  32.7 6.5 %collective-permute-done.5.x3 = bf16[192,768]{1,0:T(8,128)(2,1)S(1)} collective-permute-done((bf16[192,768]{1,0:T(8,128)(2,1)S(1)}, bf16[192,768]{1,0:T(8,128)(2,1)S(1)}, u32[]{:S(2)}, u32[]{:S(2)}) %collective-permute-start.5) | collective-permute-done | bytes 294944 | tf_op jit(solution)/shard_map/ppermute | solution.py:332
  39.1 1.0 copy-done.12
  40.1 1.2 shard_map.123
  42.0 1.3 collective-permute-start.9
  43.4 2.6 %collective-permute-start.12 = (bf16[8,48,128]{2,1,0:T(8,128)(2,1)S(1)}, bf16[8,48,128]{2,1,0:T(8,128)(2,1)S(1)}, u32[]{:S(2)}, u32[]{:S(2)}) collective-permute-start(bf16[8,48,128]{2,1,0:T(8,128)(2,1)S(1)} %slice.4), channel_id=1, source_target_pairs={{0,96},{32,64},{64,32},{96,0},{1,97},{33,65},{65,33},{97,1},{2,98}... | collective-permute-start | bytes 294920 | tf_op jit(solution)/shard_map/ppermute | solution.py:332
  46.6 1.2 collective-permute-start.10
  47.8 7.5 %collective-permute-done.8.c3 = bf16[256,768]{1,0:T(8,128)(2,1)} collective-permute-done((bf16[256,768]{1,0:T(8,128)(2,1)}, bf16[256,768]{1,0:T(8,128)(2,1)}, u32[]{:S(2)}, u32[]{:S(2)}) %collective-permute-start.8) | collective-permute-done | bytes 393248 | tf_op jit(solution)/shard_map/ppermute | solution.py:332
  55.3 1.0 copy-done.6
  56.3 1.0 copy-done.13
  57.2 1.8 shard_map.124
  59.1 1.0 copy-done
  61.6 0.9 copy-done.49
  62.5 0.8 copy-done.54
  63.3 9.8 %shard_map.125 = (bf16[1008,128]{1,0:T(8,128)(2,1)S(1)}, bf16[1008,128]{1,0:T(8,128)(2,1)S(1)}, bf16[768,128]{1,0:T(8,128)(2,1)S(1)}, bf16[768,128]{1,0:T(8,128)...) custom-call(s32[3,12]{1,0:T(4,128)S(1)} %copy-done.34, ...), custom_call_target="tpu_custom_call" | custom-call | flops 924844032 | bytes 4194304 | tf_op jit(solution)/shard_map/pallas_call | solution.py:77
  75.9 1.6 collective-permute-start.16
  77.5 1.2 collective-permute-start.13
  78.7 2.5 %collective-permute-start.14 = (bf16[8,48,128]{2,1,0:T(8,128)(2,1)}, bf16[8,48,128]{2,1,0:T(8,128)(2,1)}, u32[]{:S(2)}, u32[]{:S(2)}) collective-permute-start(bf16[8,48,128]{2,1,0:T(8,128)(2,1)} %get-tuple-element.129), channel_id=1, source_target_pairs={{0,64},{32,96},{64,0},{96,32},{1,65},{33,97},{65,1},{97,33},{2,66}... | collective-permute-start | bytes 294920 | tf_op jit(solution)/shard_map/ppermute | solution.py:332
  81.4 1.0 copy-done.14
  82.3 0.9 copy-done.19
  87.0 1.3 copy-done.1
  88.3 1.0 copy-done.10
  89.2 0.9 copy-done.20
  90.2 0.9 shard_map.127
  93.2 1.8 shard_map.128
  95.1 5.5 %all-to-all-start.1 = ((bf16[8,240,128]{2,1,0:T(8,128)(2,1)}), bf16[8,240,128]{2,1,0:T(8,128)(2,1)S(1)}, u32[]{:S(2)}, u32[]{:S(2)}) async-start(bf16[8,240,128]{2,1,0:T(8,128)(2,1)} %shard_map.128), calls=%async_computation.1 | async-start | bytes 983040 | tf_op jit(solution)/shard_map/all_to_all | solution.py:336
  100.5 3.6 %collective-permute-start.18 = (bf16[16,36,128]{2,1,0:T(8,128)(2,1)}, bf16[16,36,128]{2,1,0:T(8,128)(2,1)S(1)}, u32[]{:S(2)}, u32[]{:S(2)}) collective-permute-start(bf16[16,36,128]{2,1,0:T(8,128)(2,1)} %copy-done.51), channel_id=1, source_target_pairs={{0,64},{32,96},{64,0},{96,32},{1,65},{33,97},{65,1},{97,33},{2,66}... | collective-permute-start | bytes 442376 | tf_op jit(solution)/shard_map/ppermute | solution.py:332
  105.6 5.0 %collective-permute-done.18.refs_2_ = bf16[16,36,128]{2,1,0:T(8,128)(2,1)S(1)} collective-permute-done((bf16[16,36,128]{2,1,0:T(8,128)(2,1)}, bf16[16,36,128]{2,1,0:T(8,128)(2,1)S(1)}, u32[]{:S(2)}, u32[]{:S(2)}) %collective-permute-start.18) | collective-permute-done | bytes 147488 | tf_op jit(solution)/shard_map/ppermute | solution.py:332
  111.2 2.0 collective-permute-done.19.refs_3_
  113.8 2.0 %all-to-all-done.1.rests = bf16[8,240,128]{2,1,0:T(8,128)(2,1)S(1)} async-done(((bf16[8,240,128]{2,1,0:T(8,128)(2,1)}), bf16[8,240,128]{2,1,0:T(8,128)(2,1)S(1)}, u32[]{:S(2)}, u32[]{:S(2)}) %all-to-all-start.1) | async-done | bytes 491552 | tf_op jit(solution)/shard_map/all_to_all | solution.py:336
  115.9 0.9 copy-done.22
  116.8 1.7 shard_map.129
  118.5 0.8 copy-done.3
  119.4 3.6 %collective-permute-start.21 = (bf16[16,36,128]{2,1,0:T(8,128)(2,1)S(1)}, bf16[16,36,128]{2,1,0:T(8,128)(2,1)S(1)}, u32[]{:S(2)}, u32[]{:S(2)}) collective-permute-start(bf16[16,36,128]{2,1,0:T(8,128)(2,1)S(1)} %get-tuple-element.157), channel_id=1, source_target_pairs={{0,64},{32,96},{64,0},{96,32},{1,65},{33,97},{65,1},{97,33},{2,66}... | collective-permute-start | bytes 442376 | tf_op jit(solution)/shard_map/ppermute | solution.py:332
  123.6 4.5 %collective-permute-done.21.refs_6_ = bf16[16,36,128]{2,1,0:T(8,128)(2,1)S(1)} collective-permute-done((bf16[16,36,128]{2,1,0:T(8,128)(2,1)S(1)}, bf16[16,36,128]{2,1,0:T(8,128)(2,1)S(1)}, u32[]{:S(2)}, u32[]{:S(2)}) %collective-permute-start.21) | collective-permute-done | bytes 147488 | tf_op jit(solution)/shard_map/ppermute | solution.py:332
  128.1 1.2 collective-permute-done.22.refs_7_
  129.3 0.9 shard_map.130
  130.2 7.5 %all-to-all-start.2 = ((bf16[16,72,128]{2,1,0:T(8,128)(2,1)}), bf16[16,72,128]{2,1,0:T(8,128)(2,1)S(1)}, u32[]{:S(2)}, u32[]{:S(2)}) async-start(bf16[16,72,128]{2,1,0:T(8,128)(2,1)} %shard_map.130), calls=%async_computation.2 | async-start | bytes 589824 | tf_op jit(solution)/shard_map/all_to_all | solution.py:336
  137.8 2.1 %collective-permute-start.23 = (bf16[256,768]{1,0:T(8,128)(2,1)S(1)}, bf16[256,768]{1,0:T(8,128)(2,1)S(1)}, u32[]{:S(2)}, u32[]{:S(2)}) collective-permute-start(bf16[256,768]{1,0:T(8,128)(2,1)S(1)} %copy-done.41), channel_id=1, source_target_pairs={{0,1},{1,0},{2,3},{3,2},{4,5},{5,4},{6,7},{7,6},{8,9},{9,8},{10,11... | collective-permute-start | bytes 1179656 | tf_op jit(solution)/shard_map/ppermute | solution.py:332
  140.4 1.3 collective-permute-start.25
  141.7 11.3 %collective-permute-done.24.s2 = bf16[256,768]{1,0:T(8,128)(2,1)S(1)} collective-permute-done((bf16[256,768]{1,0:T(8,128)(2,1)S(1)}, bf16[256,768]{1,0:T(8,128)(2,1)S(1)}, u32[]{:S(2)}, u32[]{:S(2)}) %collective-permute-start.24) | collective-permute-done | bytes 393248 | tf_op jit(solution)/shard_map/ppermute | solution.py:332
  152.9 8.5 %collective-permute-done.25.s3 = bf16[256,768]{1,0:T(8,128)(2,1)S(1)} collective-permute-done((bf16[256,768]{1,0:T(8,128)(2,1)S(1)}, bf16[256,768]{1,0:T(8,128)(2,1)S(1)}, u32[]{:S(2)}, u32[]{:S(2)}) %collective-permute-start.25) | collective-permute-done | bytes 393248 | tf_op jit(solution)/shard_map/ppermute | solution.py:332
  161.5 2.4 %shard_map.132 = bf16[512,768]{1,0:T(8,128)(2,1)} custom-call(s32[3,12]{1,0:T(4,128)S(1)} %copy-done.34, s32[1]{0:T(128)} %bitcast.where, bf16[256,768]{1,0:T(8,128)(2,1)S(1)} %copy-done.56, bf16[256,768]{1,0:T(8,128)(2,1)S(1)} %collective-permute-done.23.s1, bf16[256,768]{1,0:T(8,128)(2,1)S(1)} %collective-permute-done.24.s2, ...), custom_call_target="tpu_custom_call" | custom-call | flops 805306368 | bytes 4194304 | tf_op jit(solution)/shard_map/pallas_call | solution.py:77
  165.4 8.5 %all-to-all-start.3 = ((bf16[16,72,128]{2,1,0:T(8,128)(2,1)}), bf16[16,72,128]{2,1,0:T(8,128)(2,1)S(1)}, u32[]{:S(2)}, u32[]{:S(2)}) async-start(bf16[16,72,128]{2,1,0:T(8,128)(2,1)} %shard_map.131), calls=%async_computation.3 | async-start | bytes 589824 | tf_op jit(solution)/shard_map/all_to_all | solution.py:336
  174.9 1.5 collective-permute-start.28
  176.4 8.6 %all-to-all-done.3.b0 = bf16[16,72,128]{2,1,0:T(8,128)(2,1)S(1)} async-done(((bf16[16,72,128]{2,1,0:T(8,128)(2,1)}), bf16[16,72,128]{2,1,0:T(8,128)(2,1)S(1)}, u32[]{:S(2)}, u32[]{:S(2)}) %all-to-all-start.3) | async-done | bytes 294944 | tf_op jit(solution)/shard_map/all_to_all | solution.py:336
  185.0 1.9 collective-permute-start.31
  186.9 1.4 collective-permute-start.29
  188.3 8.8 %collective-permute-done.28.s3 = bf16[256,768]{1,0:T(8,128)(2,1)S(1)} collective-permute-done((bf16[256,768]{1,0:T(8,128)(2,1)S(1)}, bf16[256,768]{1,0:T(8,128)(2,1)S(1)}, u32[]{:S(2)}, u32[]{:S(2)}) %collective-permute-start.28) | collective-permute-done | bytes 393248 | tf_op jit(solution)/shard_map/ppermute | solution.py:332
  197.0 2.4 %shard_map.134 = bf16[512,768]{1,0:T(8,128)(2,1)} custom-call(s32[3,12]{1,0:T(4,128)S(1)} %copy-done.34, s32[1]{0:T(128)} %bitcast.where, bf16[256,768]{1,0:T(8,128)(2,1)S(1)} %get-tuple-element.169.s0, bf16[256,768]{1,0:T(8,128)(2,1)S(1)} %collective-permute-done.26.s1, bf16[256,768]{1,0:T(8,128)(2,1)S(1)} %collective-permute-done.27.s2, ...), custom_call_target="tpu_custom_call" | custom-call | flops 805306368 | bytes 4194304 | tf_op jit(solution)/shard_map/pallas_call | solution.py:77
  199.5 1.9 shard_map.135
  (141 shorter events, 22.3 us)
Async XLA Ops:
  0.6 1.1 copy-start.2
  3.7 10.1 %copy-start.15 = (bf16[192,768]{1,0:T(8,128)(2,1)S(1)}, bf16[192,768]{1,0:T(8,128)(2,1)}, u32[]{:S(2)}) copy-start(bf16[192,768]{1,0:T(8,128)(2,1)} %w_query.1) | copy-start | bytes 884740
  3.7 10.1 %copy-start.16 = (bf16[192,768]{1,0:T(8,128)(2,1)S(1)}, bf16[192,768]{1,0:T(8,128)(2,1)}, u32[]{:S(2)}) copy-start(bf16[192,768]{1,0:T(8,128)(2,1)} %w_key.1) | copy-start | bytes 884740
  3.7 10.1 %copy-start.17 = (bf16[192,768]{1,0:T(8,128)(2,1)S(1)}, bf16[192,768]{1,0:T(8,128)(2,1)}, u32[]{:S(2)}) copy-start(bf16[192,768]{1,0:T(8,128)(2,1)} %w_value.1) | copy-start | bytes 884740
  3.7 7.8 %collective-permute-start.1 = (bf16[64,768]{1,0:T(8,128)(2,1)S(1)}, bf16[64,768]{1,0:T(8,128)(2,1)S(1)}, u32[]{:S(2)}, u32[]{:S(2)}) collective-permute-start(bf16[64,768]{1,0:T(8,128)(2,1)S(1)} %get-tuple-element.94), channel_id=1, source_target_pairs={{0,2},{1,3},{2,0},{3,1},{4,6},{5,7},{6,4},{7,5},{8,10},{9,11},{10,... | collective-permute-start | bytes 294920 | tf_op jit(solution)/shard_map/ppermute | solution.py:332
  5.9 6.7 %collective-permute-start.2 = (bf16[64,768]{1,0:T(8,128)(2,1)S(1)}, bf16[64,768]{1,0:T(8,128)(2,1)S(1)}, u32[]{:S(2)}, u32[]{:S(2)}) collective-permute-start(bf16[64,768]{1,0:T(8,128)(2,1)S(1)} %get-tuple-element.95), channel_id=1, source_target_pairs={{0,3},{1,2},{2,1},{3,0},{4,7},{5,6},{6,5},{7,4},{8,11},{9,10},{10,... | collective-permute-start | bytes 294920 | tf_op jit(solution)/shard_map/ppermute | solution.py:332
  11.5 2.4 %copy-start.35 = (bf16[512,768]{1,0:T(8,128)(2,1)S(1)}, bf16[512,768]{1,0:T(8,128)(2,1)}, u32[]{:S(2)}) copy-start(bf16[512,768]{1,0:T(8,128)(2,1)} %source.5) | copy-start | bytes 2359300
  12.6 8.9 %collective-permute-start.4 = (bf16[192,768]{1,0:T(8,128)(2,1)S(1)}, bf16[192,768]{1,0:T(8,128)(2,1)S(1)}, u32[]{:S(2)}, u32[]{:S(2)}) collective-permute-start(bf16[192,768]{1,0:T(8,128)(2,1)S(1)} %get-tuple-element.112), channel_id=1, source_target_pairs={{0,2},{1,3},{2,0},{3,1},{4,6},{5,7},{6,4},{7,5},{8,10},{9,11},{10,... | collective-permute-start | bytes 884744 | tf_op jit(solution)/shard_map/ppermute | solution.py:332
  12.6 4.2 %collective-permute-start = (bf16[64,768]{1,0:T(8,128)(2,1)S(1)}, bf16[64,768]{1,0:T(8,128)(2,1)S(1)}, u32[]{:S(2)}, u32[]{:S(2)}) collective-permute-start(bf16[64,768]{1,0:T(8,128)(2,1)S(1)} %get-tuple-element.93), channel_id=1, source_target_pairs={{0,1},{1,0},{2,3},{3,2},{4,5},{5,4},{6,7},{7,6},{8,9},{9,8},{10,11... | collective-permute-start | bytes 294920 | tf_op jit(solution)/shard_map/ppermute | solution.py:332
  16.8 11.1 %copy-start.45 = (bf16[192,768]{1,0:T(8,128)(2,1)S(1)}, bf16[192,768]{1,0:T(8,128)(2,1)}, u32[]{:S(2)}) copy-start(bf16[192,768]{1,0:T(8,128)(2,1)} %copy-done.44) | copy-start | bytes 884740
  16.8 12.7 %copy-start.43 = (bf16[192,768]{1,0:T(8,128)(2,1)S(1)}, bf16[192,768]{1,0:T(8,128)(2,1)}, u32[]{:S(2)}) copy-start(bf16[192,768]{1,0:T(8,128)(2,1)} %copy-done.42) | copy-start | bytes 884740
  21.5 11.2 %copy-start.11 = (bf16[192,768]{1,0:T(8,128)(2,1)}, bf16[192,768]{1,0:T(8,128)(2,1)S(1)}, u32[]{:S(2)}) copy-start(bf16[192,768]{1,0:T(8,128)(2,1)S(1)} %collective-permute-done.4.x2) | copy-start | bytes 884740
  21.5 21.8 %all-to-all-start = ((bf16[8,240,128]{2,1,0:T(8,128)(2,1)}), bf16[8,240,128]{2,1,0:T(8,128)(2,1)S(1)}, u32[]{:S(2)}, u32[]{:S(2)}) async-start(bf16[8,240,128]{2,1,0:T(8,128)(2,1)} %get-tuple-element.123), calls=%async_computation | async-start | bytes 983040 | tf_op jit(solution)/shard_map/all_to_all | solution.py:336
  28.0 4.7 %collective-permute-start.3 = (bf16[192,768]{1,0:T(8,128)(2,1)S(1)}, bf16[192,768]{1,0:T(8,128)(2,1)S(1)}, u32[]{:S(2)}, u32[]{:S(2)}) collective-permute-start(bf16[192,768]{1,0:T(8,128)(2,1)S(1)} %copy-done.45), channel_id=1, source_target_pairs={{0,1},{1,0},{2,3},{3,2},{4,5},{5,4},{6,7},{7,6},{8,9},{9,8},{10,11... | collective-permute-start | bytes 884744 | tf_op jit(solution)/shard_map/ppermute | solution.py:332
  29.6 9.6 %collective-permute-start.5 = (bf16[192,768]{1,0:T(8,128)(2,1)S(1)}, bf16[192,768]{1,0:T(8,128)(2,1)S(1)}, u32[]{:S(2)}, u32[]{:S(2)}) collective-permute-start(bf16[192,768]{1,0:T(8,128)(2,1)S(1)} %copy-done.43), channel_id=1, source_target_pairs={{0,3},{1,2},{2,1},{3,0},{4,7},{5,6},{6,5},{7,4},{8,11},{9,10},{10,... | collective-permute-start | bytes 884744 | tf_op jit(solution)/shard_map/ppermute | solution.py:332
  30.5 15.4 %collective-permute-start.6 = (bf16[256,768]{1,0:T(8,128)(2,1)}, bf16[256,768]{1,0:T(8,128)(2,1)}, u32[]{:S(2)}, u32[]{:S(2)}) collective-permute-start(bf16[256,768]{1,0:T(8,128)(2,1)} %get-tuple-element.118), channel_id=1, source_target_pairs={{0,1},{1,0},{2,3},{3,2},{4,5},{5,4},{6,7},{7,6},{8,9},{9,8},{10,11... | collective-permute-start | bytes 1179656 | tf_op jit(solution)/shard_map/ppermute | solution.py:332
  31.0 15.6 %collective-permute-start.7 = (bf16[256,768]{1,0:T(8,128)(2,1)}, bf16[256,768]{1,0:T(8,128)(2,1)}, u32[]{:S(2)}, u32[]{:S(2)}) collective-permute-start(bf16[256,768]{1,0:T(8,128)(2,1)} %get-tuple-element.119), channel_id=1, source_target_pairs={{0,2},{1,3},{2,0},{3,1},{4,6},{5,7},{6,4},{7,5},{8,10},{9,11},{10,... | collective-permute-start | bytes 1179656 | tf_op jit(solution)/shard_map/ppermute | solution.py:332
  31.5 23.8 %collective-permute-start.8 = (bf16[256,768]{1,0:T(8,128)(2,1)}, bf16[256,768]{1,0:T(8,128)(2,1)}, u32[]{:S(2)}, u32[]{:S(2)}) collective-permute-start(bf16[256,768]{1,0:T(8,128)(2,1)} %get-tuple-element.120), channel_id=1, source_target_pairs={{0,3},{1,2},{2,1},{3,0},{4,7},{5,6},{6,5},{7,4},{8,11},{9,10},{10,... | collective-permute-start | bytes 1179656 | tf_op jit(solution)/shard_map/ppermute | solution.py:332
  39.1 1.0 copy-start.12
  42.0 19.5 %copy-start.34 = (s32[3,12]{1,0:T(4,128)S(1)}, s32[3,12]{1,0:T(4,128)}, u32[]{:S(2)}) copy-start(s32[3,12]{1,0:T(4,128)} %offs.11) | copy-start | bytes 436
  42.0 18.8 %collective-permute-start.9 = (bf16[768,128]{1,0:T(8,128)(2,1)}, bf16[768,128]{1,0:T(8,128)(2,1)S(1)}, u32[]{:S(2)}, u32[]{:S(2)}) collective-permute-start(bf16[768,128]{1,0:T(8,128)(2,1)} %get-tuple-element.122.first_own), channel_id=1, source_target_pairs={{0,4},{4,0},{8,12},{12,8},{16,20},{20,16},{24,28},{28,24},{1,5},{5... | collective-permute-start | bytes 589832 | tf_op jit(solution)/shard_map/ppermute | solution.py:332
  43.4 18.2 %copy-start.47 = (bf16[768,128]{1,0:T(8,128)(2,1)S(1)}, bf16[768,128]{1,0:T(8,128)(2,1)}, u32[]{:S(2)}) copy-start(bf16[768,128]{1,0:T(8,128)(2,1)} %copy-done.46) | copy-start | bytes 589828
  43.4 18.1 %collective-permute-start.12 = (bf16[8,48,128]{2,1,0:T(8,128)(2,1)S(1)}, bf16[8,48,128]{2,1,0:T(8,128)(2,1)S(1)}, u32[]{:S(2)}, u32[]{:S(2)}) collective-permute-start(bf16[8,48,128]{2,1,0:T(8,128)(2,1)S(1)} %slice.4), channel_id=1, source_target_pairs={{0,96},{32,64},{64,32},{96,0},{1,97},{33,65},{65,33},{97,1},{2,98}... | collective-permute-start | bytes 294920 | tf_op jit(solution)/shard_map/ppermute | solution.py:332
  46.0 15.6 %collective-permute-start.11 = (bf16[8,48,128]{2,1,0:T(8,128)(2,1)S(1)}, bf16[8,48,128]{2,1,0:T(8,128)(2,1)S(1)}, u32[]{:S(2)}, u32[]{:S(2)}) collective-permute-start(bf16[8,48,128]{2,1,0:T(8,128)(2,1)S(1)} %slice.4), channel_id=1, source_target_pairs={{0,64},{32,96},{64,0},{96,32},{1,65},{33,97},{65,1},{97,33},{2,66}... | collective-permute-start | bytes 294920 | tf_op jit(solution)/shard_map/ppermute | solution.py:332
  46.6 14.9 %collective-permute-start.10 = (bf16[8,48,128]{2,1,0:T(8,128)(2,1)S(1)}, bf16[8,48,128]{2,1,0:T(8,128)(2,1)S(1)}, u32[]{:S(2)}, u32[]{:S(2)}) collective-permute-start(bf16[8,48,128]{2,1,0:T(8,128)(2,1)S(1)} %slice.4), channel_id=1, source_target_pairs={{0,32},{32,0},{64,96},{96,64},{1,33},{33,1},{65,97},{97,65},{2,34}... | collective-permute-start | bytes 294920 | tf_op jit(solution)/shard_map/ppermute | solution.py:332
  55.3 1.0 copy-start.6
  56.3 1.0 copy-start.13
  59.1 1.0 copy-start
  75.9 17.3 %collective-permute-start.16 = (bf16[768,128]{1,0:T(8,128)(2,1)}, bf16[768,128]{1,0:T(8,128)(2,1)}, u32[]{:S(2)}, u32[]{:S(2)}) collective-permute-start(bf16[768,128]{1,0:T(8,128)(2,1)} %get-tuple-element.131), channel_id=1, source_target_pairs={{0,4},{4,0},{8,12},{12,8},{16,20},{20,16},{24,28},{28,24},{1,5},{5... | collective-permute-start | bytes 589832 | tf_op jit(solution)/shard_map/ppermute | solution.py:332
  77.5 15.0 %collective-permute-start.13 = (bf16[8,48,128]{2,1,0:T(8,128)(2,1)}, bf16[8,48,128]{2,1,0:T(8,128)(2,1)}, u32[]{:S(2)}, u32[]{:S(2)}) collective-permute-start(bf16[8,48,128]{2,1,0:T(8,128)(2,1)} %get-tuple-element.128), channel_id=1, source_target_pairs={{0,32},{32,0},{64,96},{96,64},{1,33},{33,1},{65,97},{97,65},{2,34}... | collective-permute-start | bytes 294920 | tf_op jit(solution)/shard_map/ppermute | solution.py:332
  78.7 14.4 %collective-permute-start.14 = (bf16[8,48,128]{2,1,0:T(8,128)(2,1)}, bf16[8,48,128]{2,1,0:T(8,128)(2,1)}, u32[]{:S(2)}, u32[]{:S(2)}) collective-permute-start(bf16[8,48,128]{2,1,0:T(8,128)(2,1)} %get-tuple-element.129), channel_id=1, source_target_pairs={{0,64},{32,96},{64,0},{96,32},{1,65},{33,97},{65,1},{97,33},{2,66}... | collective-permute-start | bytes 294920 | tf_op jit(solution)/shard_map/ppermute | solution.py:332
  81.2 12.0 %collective-permute-start.15 = (bf16[8,48,128]{2,1,0:T(8,128)(2,1)}, bf16[8,48,128]{2,1,0:T(8,128)(2,1)}, u32[]{:S(2)}, u32[]{:S(2)}) collective-permute-start(bf16[8,48,128]{2,1,0:T(8,128)(2,1)} %get-tuple-element.130), channel_id=1, source_target_pairs={{0,96},{32,64},{64,32},{96,0},{1,97},{33,65},{65,33},{97,1},{2,98}... | collective-permute-start | bytes 294920 | tf_op jit(solution)/shard_map/ppermute | solution.py:332
  81.4 1.0 copy-start.14
  87.0 1.3 copy-start.1
  88.3 1.0 copy-start.10
  90.2 3.0 %copy-start.8 = (bf16[8,192,128]{2,1,0:T(8,128)(2,1)S(1)}, bf16[8,192,128]{2,1,0:T(8,128)(2,1)}, u32[]{:S(2)}) copy-start(bf16[8,192,128]{2,1,0:T(8,128)(2,1)} %copy-done.7) | copy-start | bytes 1179652
  90.2 3.0 %copy-start.32 = (bf16[8,48,128]{2,1,0:T(8,128)(2,1)S(1)}, bf16[8,48,128]{2,1,0:T(8,128)(2,1)}, u32[]{:S(2)}) copy-start(bf16[8,48,128]{2,1,0:T(8,128)(2,1)} %copy-done.31) | copy-start | bytes 294916
  95.1 20.8 %all-to-all-start.1 = ((bf16[8,240,128]{2,1,0:T(8,128)(2,1)}), bf16[8,240,128]{2,1,0:T(8,128)(2,1)S(1)}, u32[]{:S(2)}, u32[]{:S(2)}) async-start(bf16[8,240,128]{2,1,0:T(8,128)(2,1)} %shard_map.128), calls=%async_computation.1 | async-start | bytes 983040 | tf_op jit(solution)/shard_map/all_to_all | solution.py:336
  100.5 4.4 %collective-permute-start.17 = (bf16[16,36,128]{2,1,0:T(8,128)(2,1)}, bf16[16,36,128]{2,1,0:T(8,128)(2,1)S(1)}, u32[]{:S(2)}, u32[]{:S(2)}) collective-permute-start(bf16[16,36,128]{2,1,0:T(8,128)(2,1)} %copy-done.52), channel_id=1, source_target_pairs={{0,32},{32,0},{64,96},{96,64},{1,33},{33,1},{65,97},{97,65},{2,34}... | collective-permute-start | bytes 442376 | tf_op jit(solution)/shard_map/ppermute | solution.py:332
  100.5 10.0 %collective-permute-start.18 = (bf16[16,36,128]{2,1,0:T(8,128)(2,1)}, bf16[16,36,128]{2,1,0:T(8,128)(2,1)S(1)}, u32[]{:S(2)}, u32[]{:S(2)}) collective-permute-start(bf16[16,36,128]{2,1,0:T(8,128)(2,1)} %copy-done.51), channel_id=1, source_target_pairs={{0,64},{32,96},{64,0},{96,32},{1,65},{33,97},{65,1},{97,33},{2,66}... | collective-permute-start | bytes 442376 | tf_op jit(solution)/shard_map/ppermute | solution.py:332
  104.2 9.0 %collective-permute-start.19 = (bf16[16,36,128]{2,1,0:T(8,128)(2,1)}, bf16[16,36,128]{2,1,0:T(8,128)(2,1)S(1)}, u32[]{:S(2)}, u32[]{:S(2)}) collective-permute-start(bf16[16,36,128]{2,1,0:T(8,128)(2,1)} %copy-done.50), channel_id=1, source_target_pairs={{0,96},{32,64},{64,32},{96,0},{1,97},{33,65},{65,33},{97,1},{2,98}... | collective-permute-start | bytes 442376 | tf_op jit(solution)/shard_map/ppermute | solution.py:332
  116.8 12.5 %copy-start.24 = (bf16[16,36,128]{2,1,0:T(8,128)(2,1)S(1)}, bf16[16,36,128]{2,1,0:T(8,128)(2,1)}, u32[]{:S(2)}) copy-start(bf16[16,36,128]{2,1,0:T(8,128)(2,1)} %copy-done.23) | copy-start | bytes 442372
  116.8 12.5 %copy-start.26 = (bf16[16,36,128]{2,1,0:T(8,128)(2,1)S(1)}, bf16[16,36,128]{2,1,0:T(8,128)(2,1)}, u32[]{:S(2)}) copy-start(bf16[16,36,128]{2,1,0:T(8,128)(2,1)} %copy-done.25) | copy-start | bytes 442372
  116.8 12.5 %copy-start.28 = (bf16[16,36,128]{2,1,0:T(8,128)(2,1)S(1)}, bf16[16,36,128]{2,1,0:T(8,128)(2,1)}, u32[]{:S(2)}) copy-start(bf16[16,36,128]{2,1,0:T(8,128)(2,1)} %copy-done.27) | copy-start | bytes 442372
  116.8 12.5 %copy-start.30 = (bf16[16,36,128]{2,1,0:T(8,128)(2,1)S(1)}, bf16[16,36,128]{2,1,0:T(8,128)(2,1)}, u32[]{:S(2)}) copy-start(bf16[16,36,128]{2,1,0:T(8,128)(2,1)} %copy-done.29) | copy-start | bytes 442372
  119.3 18.5 %copy-start.41 = (bf16[256,768]{1,0:T(8,128)(2,1)S(1)}, bf16[256,768]{1,0:T(8,128)(2,1)}, u32[]{:S(2)}) copy-start(bf16[256,768]{1,0:T(8,128)(2,1)} %copy-done.40) | copy-start | bytes 1179652
  119.3 20.6 %copy-start.39 = (bf16[256,768]{1,0:T(8,128)(2,1)S(1)}, bf16[256,768]{1,0:T(8,128)(2,1)}, u32[]{:S(2)}) copy-start(bf16[256,768]{1,0:T(8,128)(2,1)} %copy-done.38) | copy-start | bytes 1179652
  119.3 21.1 %copy-start.37 = (bf16[256,768]{1,0:T(8,128)(2,1)S(1)}, bf16[256,768]{1,0:T(8,128)(2,1)}, u32[]{:S(2)}) copy-start(bf16[256,768]{1,0:T(8,128)(2,1)} %copy-done.36) | copy-start | bytes 1179652
  119.3 42.2 %copy-start.56 = (bf16[256,768]{1,0:T(8,128)(2,1)S(1)}, bf16[256,768]{1,0:T(8,128)(2,1)}, u32[]{:S(2)}) copy-start(bf16[256,768]{1,0:T(8,128)(2,1)} %copy-done.55) | copy-start | bytes 1179652
  119.3 4.3 %collective-permute-start.20 = (bf16[16,36,128]{2,1,0:T(8,128)(2,1)S(1)}, bf16[16,36,128]{2,1,0:T(8,128)(2,1)S(1)}, u32[]{:S(2)}, u32[]{:S(2)}) collective-permute-start(bf16[16,36,128]{2,1,0:T(8,128)(2,1)S(1)} %get-tuple-element.156), channel_id=1, source_target_pairs={{0,32},{32,0},{64,96},{96,64},{1,33},{33,1},{65,97},{97,65},{2,34}... | collective-permute-start | bytes 442376 | tf_op jit(solution)/shard_map/ppermute | solution.py:332
  119.4 8.7 %collective-permute-start.21 = (bf16[16,36,128]{2,1,0:T(8,128)(2,1)S(1)}, bf16[16,36,128]{2,1,0:T(8,128)(2,1)S(1)}, u32[]{:S(2)}, u32[]{:S(2)}) collective-permute-start(bf16[16,36,128]{2,1,0:T(8,128)(2,1)S(1)} %get-tuple-element.157), channel_id=1, source_target_pairs={{0,64},{32,96},{64,0},{96,32},{1,65},{33,97},{65,1},{97,33},{2,66}... | collective-permute-start | bytes 442376 | tf_op jit(solution)/shard_map/ppermute | solution.py:332
  123.1 6.2 %collective-permute-start.22 = (bf16[16,36,128]{2,1,0:T(8,128)(2,1)S(1)}, bf16[16,36,128]{2,1,0:T(8,128)(2,1)S(1)}, u32[]{:S(2)}, u32[]{:S(2)}) collective-permute-start(bf16[16,36,128]{2,1,0:T(8,128)(2,1)S(1)} %get-tuple-element.158), channel_id=1, source_target_pairs={{0,96},{32,64},{64,32},{96,0},{1,97},{33,65},{65,33},{97,1},{2,98}... | collective-permute-start | bytes 442376 | tf_op jit(solution)/shard_map/ppermute | solution.py:332
  130.2 34.4 %all-to-all-start.2 = ((bf16[16,72,128]{2,1,0:T(8,128)(2,1)}), bf16[16,72,128]{2,1,0:T(8,128)(2,1)S(1)}, u32[]{:S(2)}, u32[]{:S(2)}) async-start(bf16[16,72,128]{2,1,0:T(8,128)(2,1)} %shard_map.130), calls=%async_computation.2 | async-start | bytes 589824 | tf_op jit(solution)/shard_map/all_to_all | solution.py:336
  137.8 3.9 %collective-permute-start.23 = (bf16[256,768]{1,0:T(8,128)(2,1)S(1)}, bf16[256,768]{1,0:T(8,128)(2,1)S(1)}, u32[]{:S(2)}, u32[]{:S(2)}) collective-permute-start(bf16[256,768]{1,0:T(8,128)(2,1)S(1)} %copy-done.41), channel_id=1, source_target_pairs={{0,1},{1,0},{2,3},{3,2},{4,5},{5,4},{6,7},{7,6},{8,9},{9,8},{10,11... | collective-permute-start | bytes 1179656 | tf_op jit(solution)/shard_map/ppermute | solution.py:332
  139.9 13.0 %collective-permute-start.24 = (bf16[256,768]{1,0:T(8,128)(2,1)S(1)}, bf16[256,768]{1,0:T(8,128)(2,1)S(1)}, u32[]{:S(2)}, u32[]{:S(2)}) collective-permute-start(bf16[256,768]{1,0:T(8,128)(2,1)S(1)} %copy-done.39), channel_id=1, source_target_pairs={{0,2},{1,3},{2,0},{3,1},{4,6},{5,7},{6,4},{7,5},{8,10},{9,11},{10,... | collective-permute-start | bytes 1179656 | tf_op jit(solution)/shard_map/ppermute | solution.py:332
  140.4 23.6 %copy-start.4 = (bf16[1008,256]{1,0:T(8,128)(2,1)S(1)}, bf16[1008,256]{1,0:T(8,128)(2,1)}, u32[]{:S(2)}) copy-start(bf16[1008,256]{1,0:T(8,128)(2,1)} %copy-done.3) | copy-start | bytes 1548292
  140.4 21.1 %collective-permute-start.25 = (bf16[256,768]{1,0:T(8,128)(2,1)S(1)}, bf16[256,768]{1,0:T(8,128)(2,1)S(1)}, u32[]{:S(2)}, u32[]{:S(2)}) collective-permute-start(bf16[256,768]{1,0:T(8,128)(2,1)S(1)} %copy-done.37), channel_id=1, source_target_pairs={{0,3},{1,2},{2,1},{3,0},{4,7},{5,6},{6,5},{7,4},{8,11},{9,10},{10,... | collective-permute-start | bytes 1179656 | tf_op jit(solution)/shard_map/ppermute | solution.py:332
  165.4 19.6 %all-to-all-start.3 = ((bf16[16,72,128]{2,1,0:T(8,128)(2,1)}), bf16[16,72,128]{2,1,0:T(8,128)(2,1)S(1)}, u32[]{:S(2)}, u32[]{:S(2)}) async-start(bf16[16,72,128]{2,1,0:T(8,128)(2,1)} %shard_map.131), calls=%async_computation.3 | async-start | bytes 589824 | tf_op jit(solution)/shard_map/all_to_all | solution.py:336
  173.9 13.0 %collective-permute-start.26 = (bf16[256,768]{1,0:T(8,128)(2,1)S(1)}, bf16[256,768]{1,0:T(8,128)(2,1)S(1)}, u32[]{:S(2)}, u32[]{:S(2)}) collective-permute-start(bf16[256,768]{1,0:T(8,128)(2,1)S(1)} %get-tuple-element.170), channel_id=1, source_target_pairs={{0,1},{1,0},{2,3},{3,2},{4,5},{5,4},{6,7},{7,6},{8,9},{9,8},{10,11... | collective-permute-start | bytes 1179656 | tf_op jit(solution)/shard_map/ppermute | solution.py:332
  174.7 13.6 %collective-permute-start.27 = (bf16[256,768]{1,0:T(8,128)(2,1)S(1)}, bf16[256,768]{1,0:T(8,128)(2,1)S(1)}, u32[]{:S(2)}, u32[]{:S(2)}) collective-permute-start(bf16[256,768]{1,0:T(8,128)(2,1)S(1)} %get-tuple-element.171), channel_id=1, source_target_pairs={{0,2},{1,3},{2,0},{3,1},{4,6},{5,7},{6,4},{7,5},{8,10},{9,11},{10,... | collective-permute-start | bytes 1179656 | tf_op jit(solution)/shard_map/ppermute | solution.py:332
  174.9 22.1 %collective-permute-start.28 = (bf16[256,768]{1,0:T(8,128)(2,1)S(1)}, bf16[256,768]{1,0:T(8,128)(2,1)S(1)}, u32[]{:S(2)}, u32[]{:S(2)}) collective-permute-start(bf16[256,768]{1,0:T(8,128)(2,1)S(1)} %get-tuple-element.172), channel_id=1, source_target_pairs={{0,3},{1,2},{2,1},{3,0},{4,7},{5,6},{6,5},{7,4},{8,11},{9,10},{10,... | collective-permute-start | bytes 1179656 | tf_op jit(solution)/shard_map/ppermute | solution.py:332
  185.0 14.5 %collective-permute-start.31 = (bf16[16,72,128]{2,1,0:T(8,128)(2,1)S(1)}, bf16[16,72,128]{2,1,0:T(8,128)(2,1)S(1)}, u32[]{:S(2)}, u32[]{:S(2)}) collective-permute-start(bf16[16,72,128]{2,1,0:T(8,128)(2,1)S(1)} %all-to-all-done.3.b0), channel_id=1, source_target_pairs={{0,96},{32,64},{64,32},{96,0},{1,97},{33,65},{65,33},{97,1},{2,98}... | collective-permute-start | bytes 884744 | tf_op jit(solution)/shard_map/ppermute | solution.py:332
  186.9 12.6 %collective-permute-start.30 = (bf16[16,72,128]{2,1,0:T(8,128)(2,1)S(1)}, bf16[16,72,128]{2,1,0:T(8,128)(2,1)S(1)}, u32[]{:S(2)}, u32[]{:S(2)}) collective-permute-start(bf16[16,72,128]{2,1,0:T(8,128)(2,1)S(1)} %all-to-all-done.3.b0), channel_id=1, source_target_pairs={{0,64},{32,96},{64,0},{96,32},{1,65},{33,97},{65,1},{97,33},{2,66}... | collective-permute-start | bytes 884744 | tf_op jit(solution)/shard_map/ppermute | solution.py:332
  186.9 12.6 %collective-permute-start.29 = (bf16[16,72,128]{2,1,0:T(8,128)(2,1)S(1)}, bf16[16,72,128]{2,1,0:T(8,128)(2,1)S(1)}, u32[]{:S(2)}, u32[]{:S(2)}) collective-permute-start(bf16[16,72,128]{2,1,0:T(8,128)(2,1)S(1)} %all-to-all-done.3.b0), channel_id=1, source_target_pairs={{0,32},{32,0},{64,96},{96,64},{1,33},{33,1},{65,97},{97,65},{2,34}... | collective-permute-start | bytes 884744 | tf_op jit(solution)/shard_map/ppermute | solution.py:332
  (29 other events, 21.5 us)

commit v2 on v1

--- a/solution.py
+++ b/solution.py
@@ -230,7 +230,7 @@
     for c in range(64):
         chunks[c // 16, c % 16] = held[36 * c : 36 * c + 36].astype(BF)
     for k in range(4):
-        sends[k][...] = chunks[place[0] ^ k]
+        sends[k][...] = chunks[place[1] ^ k]
 
 
 def put_grad(held, kind, a, value):
@@ -307,7 +307,7 @@
 def place_kernel(place, b0, b1, b2, b3, *refs):
     outs, chunks, wide, held = refs[:4], refs[4], refs[5], refs[6]
     for k, block in enumerate((b0, b1, b2, b3)):
-        chunks[place[0] ^ k] = block[...]
+        chunks[place[1] ^ k] = block[...]
     for c in range(64):
         wide[...] = chunks[c // 16, c % 16].astype(F32)
         for half in range(2):
@@ -340,8 +340,7 @@
 
 
 def per_device(tokens, cotangent, w_query, w_key, w_value, w_out, offsets):
-    where = lax.axis_index(HEAD_AXES).reshape(1).astype(jnp.int32)
-    place = lax.axis_index("x").reshape(1).astype(jnp.int32)
+    where = jnp.stack([lax.axis_index(HEAD_AXES), lax.axis_index("x")]).astype(jnp.int32)
 
     def picked(source, first, rest, index):
         shape = ((192 * first + 64 * rest, WIDTH), BF)
@@ -393,7 +392,7 @@
     third_got = [third_back[0]] + [swap(third_back[j], "x", j) for j in (1, 2, 3)]
     first_got = swap(first_send, "z", 1)
     early = call(early_kernel, [half_chunks] * 4, scratch=halves, smem=1, flops=4 * 1008 * 768 * 128)(
-        place, attended, query_grad, c_first, c_rest, x_first, x_rest
+        where, attended, query_grad, c_first, c_rest, x_first, x_rest
     )
     mixed_slots = call(output_kernel, [slot] * 4, flops=2 * 1008 * 768 * 128)(attended, w_out)
     mixed_slots = to_heads(mixed_slots)
@@ -401,7 +400,7 @@
     third_got, first_got, mixed_slots[0], early[0] = tie((third_got, first_got, mixed_slots[0], early[0]))
     (rest_back,) = call(third_sum_kernel, [rest_shape])(second_back, *third_got)
     rest_got = deal(rest_back, "z")
-    rest_got, early = tie((rest_got, early))
+    rest_got, early, mixed_slots = tie((rest_got, early, mixed_slots))
 
     *late, changes = call(
         change_kernel,
@@ -409,7 +408,7 @@
         scratch=halves,
         smem=1,
         flops=2 * 1008 * 768 * 128,
-    )(place, first_back, first_got, rest_got, query_grad, x_first, x_rest)
+    )(where, first_back, first_got, rest_got, query_grad, x_first, x_rest)
     late = [late[0]] + [swap(late[k], "x", k) for k in (1, 2, 3)]
     change_slots = call(input_kernel, [slot] * 4, flops=2 * 1008 * 768 * 256)(changes, joined)
     spread = call(spread_kernel, [((ROWS, WIDTH), BF)], smem=2, flops=2 * 1024 * 512 * 768)
@@ -425,7 +424,7 @@
         [((192, WIDTH), F32)] * 4,
         scratch=[((4, 16, 72, 128), BF), ((72, 128), F32), ((2, 2304, 128), F32)],
         smem=1,
-    )(place, *blocks)
+    )(where, *blocks)
     return mixed, grad_tokens, grad_query, grad_key, grad_value, grad_out
 
 

time: 204 us -> 186 us (0.912)
  waiting for transfers between devices: 70.6 us -> 60.6 us
  local copies, waits for them, and re-layouts: 29.1 us -> 24.6 us
    ppermute x32, waiting for transfers between devices: 60 us -> 49.8 us  [swap(): return lax.ppermute(value, axis, [(i, i ^ k) for i in range(count)])]
    unnamed x114 -> x116, local copies, waits for them, and re-layouts: 29.1 us -> 24.6 us
  transfers between devices with their start and end apart: 36 -> 36, of which waited for: 16 -> 17; matrix products, arithmetic and copies ran while one was open for 0% -> 0% of each run, Pallas kernels for 8% -> 9%
where the time goes in v2:
time: 186 us; the launch traced here: 185 us
  starting transfers between devices  66.2 us (36%)
  waiting for transfers between devices  60.6 us (33%)
  Pallas kernels  32.3 us (17%)
  local copies, waits for them, and re-layouts  24.6 us (13%)
    ppermute x32, waiting for transfers between devices, swap(): return lax.ppermute(value, axis, [(i, i ^ k) for i in range(count)])  49.8 us
    ppermute x32, starting transfers between devices, swap(): return lax.ppermute(value, axis, [(i, i ^ k) for i in range(count)])  38.6 us
    pallas_call x18, Pallas kernels, run(): pl.pallas_call(body, out_shape=tuple((jax.ShapeDtypeStruct(shape, kind) f...  32.3 us
    all_to_all x4, starting transfers between devices, deal(): return lax.all_to_all(value, axis, 0, 0, tiled=True)  27.6 us
    unnamed x116, local copies, waits for them, and re-layouts  24.6 us
    all_to_all x4, waiting for transfers between devices, deal(): return lax.all_to_all(value, axis, 0, 0, tiled=True)  10.8 us
  transfers between devices with their start and end apart: 36, of which 17 were waited for; matrix products, arithmetic and copies ran while one was open for 0% of the time, Pallas kernels for 9%

profile of v2, /device:TPU:1, one launch (start us, length us, event | category | flops | bytes accessed | tf_op | source)
XLA Modules:
  0.0 184.7 jit_solution(16131844586237617846)
XLA Ops:
  0.7 1.1 copy-done
  2.5 1.2 shard_map.118
  3.8 2.2 %collective-permute-start.1 = (bf16[64,768]{1,0:T(8,128)(2,1)S(1)}, bf16[64,768]{1,0:T(8,128)(2,1)S(1)}, u32[]{:S(2)}, u32[]{:S(2)}) collective-permute-start(bf16[64,768]{1,0:T(8,128)(2,1)S(1)} %get-tuple-element.98), channel_id=1, source_target_pairs={{0,2},{1,3},{2,0},{3,1},{4,6},{5,7},{6,4},{7,5},{8,10},{9,11},{10,... | collective-permute-start | bytes 294920 | tf_op jit(solution)/shard_map/ppermute | solution.py:332
  6.0 2.7 %collective-permute-start.2 = (bf16[64,768]{1,0:T(8,128)(2,1)S(1)}, bf16[64,768]{1,0:T(8,128)(2,1)S(1)}, u32[]{:S(2)}, u32[]{:S(2)}) collective-permute-start(bf16[64,768]{1,0:T(8,128)(2,1)S(1)} %get-tuple-element.99), channel_id=1, source_target_pairs={{0,3},{1,2},{2,1},{3,0},{4,7},{5,6},{6,5},{7,4},{8,11},{9,10},{10,... | collective-permute-start | bytes 294920 | tf_op jit(solution)/shard_map/ppermute | solution.py:332
  8.8 1.4 shard_map.119
  11.6 1.1 collective-permute-done.2.x3
  12.7 1.1 collective-permute-start
  14.0 2.2 %shard_map.120 = (bf16[256,768]{1,0:T(8,128)(2,1)S(1)}, bf16[256,768]{1,0:T(8,128)(2,1)}, bf16[256,768]{1,0:T(8,128)(2,1)}, bf16[256,768]{1,0:T(8,128)(2,1)}) custom-call(s32[3,12]{1,0:T(4,128)S(1)} %copy-done.24, s32[2]{0:T(128)S(1)} %pad_add_fusion.where.place, bf16[512,768]{1,0:T(8,128)(2,1)S(1)} %copy-done.26), custom_call_target="tpu_custom_call" | custom-call | flops 805306368 | bytes 4194304 | tf_op jit(solution)/shard_map/pallas_call | solution.py:77
  16.9 1.3 shard_map.122
  18.8 2.8 %collective-permute-done.4.x2 = bf16[192,768]{1,0:T(8,128)(2,1)S(1)} collective-permute-done((bf16[192,768]{1,0:T(8,128)(2,1)S(1)}, bf16[192,768]{1,0:T(8,128)(2,1)S(1)}, u32[]{:S(2)}, u32[]{:S(2)}) %collective-permute-start.4) | collective-permute-done | bytes 294944 | tf_op jit(solution)/shard_map/ppermute | solution.py:332
  21.6 6.4 %all-to-all-start = ((bf16[8,240,128]{2,1,0:T(8,128)(2,1)}), bf16[8,240,128]{2,1,0:T(8,128)(2,1)S(1)}, u32[]{:S(2)}, u32[]{:S(2)}) async-start(bf16[8,240,128]{2,1,0:T(8,128)(2,1)} %get-tuple-element.127), calls=%async_computation | async-start | bytes 983040 | tf_op jit(solution)/shard_map/all_to_all | solution.py:336
  28.1 1.6 collective-permute-start.3
  29.7 1.0 collective-permute-start.5
  31.6 1.2 collective-permute-start.8
  32.8 6.5 %collective-permute-done.5.x3 = bf16[192,768]{1,0:T(8,128)(2,1)S(1)} collective-permute-done((bf16[192,768]{1,0:T(8,128)(2,1)S(1)}, bf16[192,768]{1,0:T(8,128)(2,1)S(1)}, u32[]{:S(2)}, u32[]{:S(2)}) %collective-permute-start.5) | collective-permute-done | bytes 294944 | tf_op jit(solution)/shard_map/ppermute | solution.py:332
  39.2 1.0 copy-done.6
  40.2 1.2 shard_map.123
  42.1 1.3 collective-permute-start.9
  43.5 2.6 %collective-permute-start.12 = (bf16[8,48,128]{2,1,0:T(8,128)(2,1)S(1)}, bf16[8,48,128]{2,1,0:T(8,128)(2,1)S(1)}, u32[]{:S(2)}, u32[]{:S(2)}) collective-permute-start(bf16[8,48,128]{2,1,0:T(8,128)(2,1)S(1)} %slice.4), channel_id=1, source_target_pairs={{0,96},{32,64},{64,32},{96,0},{1,97},{33,65},{65,33},{97,1},{2,98}... | collective-permute-start | bytes 294920 | tf_op jit(solution)/shard_map/ppermute | solution.py:332
  46.7 1.2 collective-permute-start.10
  47.9 7.5 %collective-permute-done.8.c3 = bf16[256,768]{1,0:T(8,128)(2,1)} collective-permute-done((bf16[256,768]{1,0:T(8,128)(2,1)}, bf16[256,768]{1,0:T(8,128)(2,1)}, u32[]{:S(2)}, u32[]{:S(2)}) %collective-permute-start.8) | collective-permute-done | bytes 393248 | tf_op jit(solution)/shard_map/ppermute | solution.py:332
  55.3 1.0 copy-done.4
  56.3 1.0 copy-done.7
  57.3 1.8 shard_map.124
  59.9 0.9 copy-done.50
  60.8 0.8 copy-done.55
  61.6 9.1 %shard_map.125 = (bf16[1008,128]{1,0:T(8,128)(2,1)S(1)}, bf16[1008,128]{1,0:T(8,128)(2,1)S(1)}, bf16[768,128]{1,0:T(8,128)(2,1)S(1)}, bf16[768,128]{1,0:T(8,128)...) custom-call(s32[3,12]{1,0:T(4,128)S(1)} %copy-done.25, ...), custom_call_target="tpu_custom_call" | custom-call | flops 924844032 | bytes 4194304 | tf_op jit(solution)/shard_map/pallas_call | solution.py:77
  71.4 1.6 collective-permute-start.16
  73.1 1.2 collective-permute-start.13
  74.3 2.5 %collective-permute-start.14 = (bf16[8,48,128]{2,1,0:T(8,128)(2,1)S(1)}, bf16[8,48,128]{2,1,0:T(8,128)(2,1)S(1)}, u32[]{:S(2)}, u32[]{:S(2)}) collective-permute-start(bf16[8,48,128]{2,1,0:T(8,128)(2,1)S(1)} %get-tuple-element.133), channel_id=1, source_target_pairs={{0,64},{32,96},{64,0},{96,32},{1,65},{33,97},{65,1},{97,33},{2,66}... | collective-permute-start | bytes 294920 | tf_op jit(solution)/shard_map/ppermute | solution.py:332
  78.4 1.5 shard_map.127
  81.9 2.0 %collective-permute-done.15.t3 = bf16[8,48,128]{2,1,0:T(8,128)(2,1)S(1)} collective-permute-done((bf16[8,48,128]{2,1,0:T(8,128)(2,1)S(1)}, bf16[8,48,128]{2,1,0:T(8,128)(2,1)S(1)}, u32[]{:S(2)}, u32[]{:S(2)}) %collective-permute-start.15) | collective-permute-done | bytes 98336 | tf_op jit(solution)/shard_map/ppermute | solution.py:332
  84.6 0.8 shard_map.128
  85.4 5.5 %all-to-all-start.1 = ((bf16[8,240,128]{2,1,0:T(8,128)(2,1)}), bf16[8,240,128]{2,1,0:T(8,128)(2,1)S(1)}, u32[]{:S(2)}, u32[]{:S(2)}) async-start(bf16[8,240,128]{2,1,0:T(8,128)(2,1)} %shard_map.128), calls=%async_computation.1 | async-start | bytes 983040 | tf_op jit(solution)/shard_map/all_to_all | solution.py:336
  90.9 0.9 collective-permute-start.20
  91.8 1.0 collective-permute-start.21
  93.6 2.4 %collective-permute-start.18 = (bf16[16,36,128]{2,1,0:T(8,128)(2,1)}, bf16[16,36,128]{2,1,0:T(8,128)(2,1)S(1)}, u32[]{:S(2)}, u32[]{:S(2)}) collective-permute-start(bf16[16,36,128]{2,1,0:T(8,128)(2,1)} %copy-done.52), channel_id=1, source_target_pairs={{0,64},{32,96},{64,0},{96,32},{1,65},{33,97},{65,1},{97,33},{2,66}... | collective-permute-start | bytes 442376 | tf_op jit(solution)/shard_map/ppermute | solution.py:332
  95.9 3.5 %collective-permute-done.17.refs_1_ = bf16[16,36,128]{2,1,0:T(8,128)(2,1)S(1)} collective-permute-done((bf16[16,36,128]{2,1,0:T(8,128)(2,1)}, bf16[16,36,128]{2,1,0:T(8,128)(2,1)S(1)}, u32[]{:S(2)}, u32[]{:S(2)}) %collective-permute-start.17) | collective-permute-done | bytes 147488 | tf_op jit(solution)/shard_map/ppermute | solution.py:332
  100.1 1.2 collective-permute-start.19
  101.3 2.6 %collective-permute-done.18.refs_2_ = bf16[16,36,128]{2,1,0:T(8,128)(2,1)S(1)} collective-permute-done((bf16[16,36,128]{2,1,0:T(8,128)(2,1)}, bf16[16,36,128]{2,1,0:T(8,128)(2,1)S(1)}, u32[]{:S(2)}, u32[]{:S(2)}) %collective-permute-start.18) | collective-permute-done | bytes 147488 | tf_op jit(solution)/shard_map/ppermute | solution.py:332
  104.5 1.7 collective-permute-done.19.refs_3_
  108.3 3.0 %collective-permute-done.22.s3 = bf16[256,768]{1,0:T(8,128)(2,1)S(1)} collective-permute-done((bf16[256,768]{1,0:T(8,128)(2,1)}, bf16[256,768]{1,0:T(8,128)(2,1)S(1)}, u32[]{:S(2)}, u32[]{:S(2)}) %collective-permute-start.22) | collective-permute-done | bytes 393248 | tf_op jit(solution)/shard_map/ppermute | solution.py:332
  112.1 0.9 copy-done.13
  113.0 0.9 copy-done.15
  113.9 1.2 shard_map.129
  116.0 2.4 %collective-permute-start.24 = (bf16[16,36,128]{2,1,0:T(8,128)(2,1)S(1)}, bf16[16,36,128]{2,1,0:T(8,128)(2,1)S(1)}, u32[]{:S(2)}, u32[]{:S(2)}) collective-permute-start(bf16[16,36,128]{2,1,0:T(8,128)(2,1)S(1)} %get-tuple-element.165), channel_id=1, source_target_pairs={{0,64},{32,96},{64,0},{96,32},{1,65},{33,97},{65,1},{97,33},{2,66}... | collective-permute-start | bytes 442376 | tf_op jit(solution)/shard_map/ppermute | solution.py:332
  118.3 1.5 collective-permute-start.25
  119.8 1.7 collective-permute-done.23.refs_5_
  121.6 4.5 %collective-permute-done.24.refs_6_ = bf16[16,36,128]{2,1,0:T(8,128)(2,1)S(1)} collective-permute-done((bf16[16,36,128]{2,1,0:T(8,128)(2,1)S(1)}, bf16[16,36,128]{2,1,0:T(8,128)(2,1)S(1)}, u32[]{:S(2)}, u32[]{:S(2)}) %collective-permute-start.24) | collective-permute-done | bytes 147488 | tf_op jit(solution)/shard_map/ppermute | solution.py:332
  126.0 2.5 %collective-permute-done.25.refs_7_ = bf16[16,36,128]{2,1,0:T(8,128)(2,1)S(1)} collective-permute-done((bf16[16,36,128]{2,1,0:T(8,128)(2,1)S(1)}, bf16[16,36,128]{2,1,0:T(8,128)(2,1)S(1)}, u32[]{:S(2)}, u32[]{:S(2)}) %collective-permute-start.25) | collective-permute-done | bytes 147488 | tf_op jit(solution)/shard_map/ppermute | solution.py:332
  128.5 0.9 shard_map.130
  129.5 9.5 %all-to-all-start.2 = ((bf16[16,72,128]{2,1,0:T(8,128)(2,1)}), bf16[16,72,128]{2,1,0:T(8,128)(2,1)S(1)}, u32[]{:S(2)}, u32[]{:S(2)}) async-start(bf16[16,72,128]{2,1,0:T(8,128)(2,1)} %shard_map.130), calls=%async_computation.2 | async-start | bytes 589824 | tf_op jit(solution)/shard_map/all_to_all | solution.py:336
  142.7 2.4 %shard_map.132 = bf16[512,768]{1,0:T(8,128)(2,1)} custom-call(s32[3,12]{1,0:T(4,128)S(1)} %copy-done.25, s32[2]{0:T(128)S(1)} %pad_add_fusion.where.place, bf16[256,768]{1,0:T(8,128)(2,1)S(1)} %copy-done.57, bf16[256,768]{1,0:T(8,128)(2,1)S(1)} %copy-done.28, bf16[256,768]{1,0:T(8,128)(2,1)S(1)} %copy-done.30, bf16[256,768]{1,0:T(8,128)(2,1)S(1)} %copy-done.32), custom_call_target="tpu_custom_call" | custom-call | flops 805306368 | bytes 4194304 | tf_op jit(solution)/shard_map/pallas_call | solution.py:77
  145.2 4.0 %all-to-all-done.2.got = bf16[16,72,128]{2,1,0:T(8,128)(2,1)S(1)} async-done(((bf16[16,72,128]{2,1,0:T(8,128)(2,1)}), bf16[16,72,128]{2,1,0:T(8,128)(2,1)S(1)}, u32[]{:S(2)}, u32[]{:S(2)}) %all-to-all-start.2) | async-done | bytes 294944 | tf_op jit(solution)/shard_map/all_to_all | solution.py:336
  149.9 6.1 %all-to-all-start.3 = ((bf16[16,72,128]{2,1,0:T(8,128)(2,1)}), bf16[16,72,128]{2,1,0:T(8,128)(2,1)S(1)}, u32[]{:S(2)}, u32[]{:S(2)}) async-start(bf16[16,72,128]{2,1,0:T(8,128)(2,1)} %shard_map.131), calls=%async_computation.3 | async-start | bytes 589824 | tf_op jit(solution)/shard_map/all_to_all | solution.py:336
  156.1 1.6 collective-permute-start.26
  158.1 1.3 collective-permute-start.28
  159.4 6.7 %all-to-all-done.3.b0 = bf16[16,72,128]{2,1,0:T(8,128)(2,1)S(1)} async-done(((bf16[16,72,128]{2,1,0:T(8,128)(2,1)}), bf16[16,72,128]{2,1,0:T(8,128)(2,1)S(1)}, u32[]{:S(2)}, u32[]{:S(2)}) %all-to-all-start.3) | async-done | bytes 294944 | tf_op jit(solution)/shard_map/all_to_all | solution.py:336
  166.2 1.5 collective-permute-start.31
  167.7 1.8 collective-permute-start.29
  169.4 1.7 collective-permute-done.27.s2
  171.1 8.7 %collective-permute-done.28.s3 = bf16[256,768]{1,0:T(8,128)(2,1)S(1)} collective-permute-done((bf16[256,768]{1,0:T(8,128)(2,1)S(1)}, bf16[256,768]{1,0:T(8,128)(2,1)S(1)}, u32[]{:S(2)}, u32[]{:S(2)}) %collective-permute-start.28) | collective-permute-done | bytes 393248 | tf_op jit(solution)/shard_map/ppermute | solution.py:332
  179.8 2.4 %shard_map.134 = bf16[512,768]{1,0:T(8,128)(2,1)} custom-call(s32[3,12]{1,0:T(4,128)S(1)} %copy-done.25, s32[2]{0:T(128)S(1)} %pad_add_fusion.where.place, bf16[256,768]{1,0:T(8,128)(2,1)S(1)} %copy-done.37, bf16[256,768]{1,0:T(8,128)(2,1)S(1)} %collective-permute-done.26.s1, bf16[256,768]{1,0:T(8,128)(2,1)S(1)} %collective-permute-done.27.s2, ...), custom_call_target="tpu_custom_call" | custom-call | flops 805306368 | bytes 4194304 | tf_op jit(solution)/shard_map/pallas_call | solution.py:77
  182.3 2.5 %shard_map.135 = (f32[192,768]{1,0:T(8,128)}, f32[192,768]{1,0:T(8,128)}, f32[192,768]{1,0:T(8,128)}, f32[192,768]{1,0:T(8,128)}) custom-call(s32[2]{0:T(128)S(1)} %pad_add_fusion.where.place, bf16[16,72,128]{2,1,0:T(8,128)(2,1)S(1)} %all-to-all-done.3.b0, bf16[16,72,128]{2,1,0:T(8,128)(2,1)S(1)} %collective-permute-done.29.b1, ...), custom_call_target="tpu_custom_call" | custom-call | bytes 4194304 | tf_op jit(solution)/shard_map/pallas_call | solution.py:77
  (144 shorter events, 22.3 us)
Async XLA Ops:
  0.7 1.1 copy-start
  3.8 10.1 %copy-start.9 = (bf16[192,768]{1,0:T(8,128)(2,1)S(1)}, bf16[192,768]{1,0:T(8,128)(2,1)}, u32[]{:S(2)}) copy-start(bf16[192,768]{1,0:T(8,128)(2,1)} %w_query.1) | copy-start | bytes 884740
  3.8 10.1 %copy-start.10 = (bf16[192,768]{1,0:T(8,128)(2,1)S(1)}, bf16[192,768]{1,0:T(8,128)(2,1)}, u32[]{:S(2)}) copy-start(bf16[192,768]{1,0:T(8,128)(2,1)} %w_key.1) | copy-start | bytes 884740
  3.8 10.1 %copy-start.11 = (bf16[192,768]{1,0:T(8,128)(2,1)S(1)}, bf16[192,768]{1,0:T(8,128)(2,1)}, u32[]{:S(2)}) copy-start(bf16[192,768]{1,0:T(8,128)(2,1)} %w_value.1) | copy-start | bytes 884740
  3.8 7.8 %collective-permute-start.1 = (bf16[64,768]{1,0:T(8,128)(2,1)S(1)}, bf16[64,768]{1,0:T(8,128)(2,1)S(1)}, u32[]{:S(2)}, u32[]{:S(2)}) collective-permute-start(bf16[64,768]{1,0:T(8,128)(2,1)S(1)} %get-tuple-element.98), channel_id=1, source_target_pairs={{0,2},{1,3},{2,0},{3,1},{4,6},{5,7},{6,4},{7,5},{8,10},{9,11},{10,... | collective-permute-start | bytes 294920 | tf_op jit(solution)/shard_map/ppermute | solution.py:332
  6.0 6.7 %collective-permute-start.2 = (bf16[64,768]{1,0:T(8,128)(2,1)S(1)}, bf16[64,768]{1,0:T(8,128)(2,1)S(1)}, u32[]{:S(2)}, u32[]{:S(2)}) collective-permute-start(bf16[64,768]{1,0:T(8,128)(2,1)S(1)} %get-tuple-element.99), channel_id=1, source_target_pairs={{0,3},{1,2},{2,1},{3,0},{4,7},{5,6},{6,5},{7,4},{8,11},{9,10},{10,... | collective-permute-start | bytes 294920 | tf_op jit(solution)/shard_map/ppermute | solution.py:332
  11.6 2.4 %copy-start.26 = (bf16[512,768]{1,0:T(8,128)(2,1)S(1)}, bf16[512,768]{1,0:T(8,128)(2,1)}, u32[]{:S(2)}) copy-start(bf16[512,768]{1,0:T(8,128)(2,1)} %source.5) | copy-start | bytes 2359300
  12.7 8.9 %collective-permute-start.4 = (bf16[192,768]{1,0:T(8,128)(2,1)S(1)}, bf16[192,768]{1,0:T(8,128)(2,1)S(1)}, u32[]{:S(2)}, u32[]{:S(2)}) collective-permute-start(bf16[192,768]{1,0:T(8,128)(2,1)S(1)} %get-tuple-element.116), channel_id=1, source_target_pairs={{0,2},{1,3},{2,0},{3,1},{4,6},{5,7},{6,4},{7,5},{8,10},{9,11},{10,... | collective-permute-start | bytes 884744 | tf_op jit(solution)/shard_map/ppermute | solution.py:332
  12.7 4.2 %collective-permute-start = (bf16[64,768]{1,0:T(8,128)(2,1)S(1)}, bf16[64,768]{1,0:T(8,128)(2,1)S(1)}, u32[]{:S(2)}, u32[]{:S(2)}) collective-permute-start(bf16[64,768]{1,0:T(8,128)(2,1)S(1)} %get-tuple-element.97), channel_id=1, source_target_pairs={{0,1},{1,0},{2,3},{3,2},{4,5},{5,4},{6,7},{7,6},{8,9},{9,8},{10,11... | collective-permute-start | bytes 294920 | tf_op jit(solution)/shard_map/ppermute | solution.py:332
  16.9 11.1 %copy-start.46 = (bf16[192,768]{1,0:T(8,128)(2,1)S(1)}, bf16[192,768]{1,0:T(8,128)(2,1)}, u32[]{:S(2)}) copy-start(bf16[192,768]{1,0:T(8,128)(2,1)} %copy-done.45) | copy-start | bytes 884740
  16.9 12.7 %copy-start.44 = (bf16[192,768]{1,0:T(8,128)(2,1)S(1)}, bf16[192,768]{1,0:T(8,128)(2,1)}, u32[]{:S(2)}) copy-start(bf16[192,768]{1,0:T(8,128)(2,1)} %copy-done.43) | copy-start | bytes 884740
  21.6 11.2 %copy-start.5 = (bf16[192,768]{1,0:T(8,128)(2,1)}, bf16[192,768]{1,0:T(8,128)(2,1)S(1)}, u32[]{:S(2)}) copy-start(bf16[192,768]{1,0:T(8,128)(2,1)S(1)} %collective-permute-done.4.x2) | copy-start | bytes 884740
  21.6 21.8 %all-to-all-start = ((bf16[8,240,128]{2,1,0:T(8,128)(2,1)}), bf16[8,240,128]{2,1,0:T(8,128)(2,1)S(1)}, u32[]{:S(2)}, u32[]{:S(2)}) async-start(bf16[8,240,128]{2,1,0:T(8,128)(2,1)} %get-tuple-element.127), calls=%async_computation | async-start | bytes 983040 | tf_op jit(solution)/shard_map/all_to_all | solution.py:336
  28.1 4.7 %collective-permute-start.3 = (bf16[192,768]{1,0:T(8,128)(2,1)S(1)}, bf16[192,768]{1,0:T(8,128)(2,1)S(1)}, u32[]{:S(2)}, u32[]{:S(2)}) collective-permute-start(bf16[192,768]{1,0:T(8,128)(2,1)S(1)} %copy-done.46), channel_id=1, source_target_pairs={{0,1},{1,0},{2,3},{3,2},{4,5},{5,4},{6,7},{7,6},{8,9},{9,8},{10,11... | collective-permute-start | bytes 884744 | tf_op jit(solution)/shard_map/ppermute | solution.py:332
  29.7 9.6 %collective-permute-start.5 = (bf16[192,768]{1,0:T(8,128)(2,1)S(1)}, bf16[192,768]{1,0:T(8,128)(2,1)S(1)}, u32[]{:S(2)}, u32[]{:S(2)}) collective-permute-start(bf16[192,768]{1,0:T(8,128)(2,1)S(1)} %copy-done.44), channel_id=1, source_target_pairs={{0,3},{1,2},{2,1},{3,0},{4,7},{5,6},{6,5},{7,4},{8,11},{9,10},{10,... | collective-permute-start | bytes 884744 | tf_op jit(solution)/shard_map/ppermute | solution.py:332
  30.6 15.4 %collective-permute-start.6 = (bf16[256,768]{1,0:T(8,128)(2,1)}, bf16[256,768]{1,0:T(8,128)(2,1)}, u32[]{:S(2)}, u32[]{:S(2)}) collective-permute-start(bf16[256,768]{1,0:T(8,128)(2,1)} %get-tuple-element.122), channel_id=1, source_target_pairs={{0,1},{1,0},{2,3},{3,2},{4,5},{5,4},{6,7},{7,6},{8,9},{9,8},{10,11... | collective-permute-start | bytes 1179656 | tf_op jit(solution)/shard_map/ppermute | solution.py:332
  31.0 15.6 %collective-permute-start.7 = (bf16[256,768]{1,0:T(8,128)(2,1)}, bf16[256,768]{1,0:T(8,128)(2,1)}, u32[]{:S(2)}, u32[]{:S(2)}) collective-permute-start(bf16[256,768]{1,0:T(8,128)(2,1)} %get-tuple-element.123), channel_id=1, source_target_pairs={{0,2},{1,3},{2,0},{3,1},{4,6},{5,7},{6,4},{7,5},{8,10},{9,11},{10,... | collective-permute-start | bytes 1179656 | tf_op jit(solution)/shard_map/ppermute | solution.py:332
  31.6 23.8 %collective-permute-start.8 = (bf16[256,768]{1,0:T(8,128)(2,1)}, bf16[256,768]{1,0:T(8,128)(2,1)}, u32[]{:S(2)}, u32[]{:S(2)}) collective-permute-start(bf16[256,768]{1,0:T(8,128)(2,1)} %get-tuple-element.124), channel_id=1, source_target_pairs={{0,3},{1,2},{2,1},{3,0},{4,7},{5,6},{6,5},{7,4},{8,11},{9,10},{10,... | collective-permute-start | bytes 1179656 | tf_op jit(solution)/shard_map/ppermute | solution.py:332
  42.1 17.8 %copy-start.25 = (s32[3,12]{1,0:T(4,128)S(1)}, s32[3,12]{1,0:T(4,128)}, u32[]{:S(2)}) copy-start(s32[3,12]{1,0:T(4,128)} %offs.11) | copy-start | bytes 436
  42.1 17.1 %collective-permute-start.9 = (bf16[768,128]{1,0:T(8,128)(2,1)}, bf16[768,128]{1,0:T(8,128)(2,1)S(1)}, u32[]{:S(2)}, u32[]{:S(2)}) collective-permute-start(bf16[768,128]{1,0:T(8,128)(2,1)} %get-tuple-element.126.first_own), channel_id=1, source_target_pairs={{0,4},{4,0},{8,12},{12,8},{16,20},{20,16},{24,28},{28,24},{1,5},{5... | collective-permute-start | bytes 589832 | tf_op jit(solution)/shard_map/ppermute | solution.py:332
  43.4 16.4 %copy-start.48 = (bf16[768,128]{1,0:T(8,128)(2,1)S(1)}, bf16[768,128]{1,0:T(8,128)(2,1)}, u32[]{:S(2)}) copy-start(bf16[768,128]{1,0:T(8,128)(2,1)} %copy-done.47) | copy-start | bytes 589828
  43.5 16.4 %collective-permute-start.12 = (bf16[8,48,128]{2,1,0:T(8,128)(2,1)S(1)}, bf16[8,48,128]{2,1,0:T(8,128)(2,1)S(1)}, u32[]{:S(2)}, u32[]{:S(2)}) collective-permute-start(bf16[8,48,128]{2,1,0:T(8,128)(2,1)S(1)} %slice.4), channel_id=1, source_target_pairs={{0,96},{32,64},{64,32},{96,0},{1,97},{33,65},{65,33},{97,1},{2,98}... | collective-permute-start | bytes 294920 | tf_op jit(solution)/shard_map/ppermute | solution.py:332
  46.0 13.8 %collective-permute-start.11 = (bf16[8,48,128]{2,1,0:T(8,128)(2,1)S(1)}, bf16[8,48,128]{2,1,0:T(8,128)(2,1)S(1)}, u32[]{:S(2)}, u32[]{:S(2)}) collective-permute-start(bf16[8,48,128]{2,1,0:T(8,128)(2,1)S(1)} %slice.4), channel_id=1, source_target_pairs={{0,64},{32,96},{64,0},{96,32},{1,65},{33,97},{65,1},{97,33},{2,66}... | collective-permute-start | bytes 294920 | tf_op jit(solution)/shard_map/ppermute | solution.py:332
  46.7 13.2 %collective-permute-start.10 = (bf16[8,48,128]{2,1,0:T(8,128)(2,1)S(1)}, bf16[8,48,128]{2,1,0:T(8,128)(2,1)S(1)}, u32[]{:S(2)}, u32[]{:S(2)}) collective-permute-start(bf16[8,48,128]{2,1,0:T(8,128)(2,1)S(1)} %slice.4), channel_id=1, source_target_pairs={{0,32},{32,0},{64,96},{96,64},{1,33},{33,1},{65,97},{97,65},{2,34}... | collective-permute-start | bytes 294920 | tf_op jit(solution)/shard_map/ppermute | solution.py:332
  55.3 1.0 copy-start.4
  61.6 15.3 %copy-start.8 = (bf16[192,768]{1,0:T(8,128)(2,1)S(1)}, bf16[192,768]{1,0:T(8,128)(2,1)}, u32[]{:S(2)}) copy-start(bf16[192,768]{1,0:T(8,128)(2,1)} %w_out.3) | copy-start | bytes 884740
  71.4 12.5 %collective-permute-start.16 = (bf16[768,128]{1,0:T(8,128)(2,1)S(1)}, bf16[768,128]{1,0:T(8,128)(2,1)S(1)}, u32[]{:S(2)}, u32[]{:S(2)}) collective-permute-start(bf16[768,128]{1,0:T(8,128)(2,1)S(1)} %get-tuple-element.135), channel_id=1, source_target_pairs={{0,4},{4,0},{8,12},{12,8},{16,20},{20,16},{24,28},{28,24},{1,5},{5... | collective-permute-start | bytes 589832 | tf_op jit(solution)/shard_map/ppermute | solution.py:332
  73.1 8.8 %collective-permute-start.13 = (bf16[8,48,128]{2,1,0:T(8,128)(2,1)S(1)}, bf16[8,48,128]{2,1,0:T(8,128)(2,1)S(1)}, u32[]{:S(2)}, u32[]{:S(2)}) collective-permute-start(bf16[8,48,128]{2,1,0:T(8,128)(2,1)S(1)} %get-tuple-element.132), channel_id=1, source_target_pairs={{0,32},{32,0},{64,96},{96,64},{1,33},{33,1},{65,97},{97,65},{2,34}... | collective-permute-start | bytes 294920 | tf_op jit(solution)/shard_map/ppermute | solution.py:332
  74.3 7.6 %collective-permute-start.14 = (bf16[8,48,128]{2,1,0:T(8,128)(2,1)S(1)}, bf16[8,48,128]{2,1,0:T(8,128)(2,1)S(1)}, u32[]{:S(2)}, u32[]{:S(2)}) collective-permute-start(bf16[8,48,128]{2,1,0:T(8,128)(2,1)S(1)} %get-tuple-element.133), channel_id=1, source_target_pairs={{0,64},{32,96},{64,0},{96,32},{1,65},{33,97},{65,1},{97,33},{2,66}... | collective-permute-start | bytes 294920 | tf_op jit(solution)/shard_map/ppermute | solution.py:332
  76.7 7.2 %collective-permute-start.15 = (bf16[8,48,128]{2,1,0:T(8,128)(2,1)S(1)}, bf16[8,48,128]{2,1,0:T(8,128)(2,1)S(1)}, u32[]{:S(2)}, u32[]{:S(2)}) collective-permute-start(bf16[8,48,128]{2,1,0:T(8,128)(2,1)S(1)} %get-tuple-element.134), channel_id=1, source_target_pairs={{0,96},{32,64},{64,32},{96,0},{1,97},{33,65},{65,33},{97,1},{2,98}... | collective-permute-start | bytes 294920 | tf_op jit(solution)/shard_map/ppermute | solution.py:332
  78.4 5.5 %copy-start.33 = (bf16[256,768]{1,0:T(8,128)(2,1)}, bf16[256,768]{1,0:T(8,128)(2,1)S(1)}, u32[]{:S(2)}) copy-start(bf16[256,768]{1,0:T(8,128)(2,1)S(1)} %get-tuple-element.155) | copy-start | bytes 1179652
  78.4 6.2 %copy-start.34 = (bf16[256,768]{1,0:T(8,128)(2,1)}, bf16[256,768]{1,0:T(8,128)(2,1)S(1)}, u32[]{:S(2)}) copy-start(bf16[256,768]{1,0:T(8,128)(2,1)S(1)} %get-tuple-element.154) | copy-start | bytes 1179652
  78.4 6.2 %copy-start.35 = (bf16[256,768]{1,0:T(8,128)(2,1)}, bf16[256,768]{1,0:T(8,128)(2,1)S(1)}, u32[]{:S(2)}) copy-start(bf16[256,768]{1,0:T(8,128)(2,1)S(1)} %get-tuple-element.153) | copy-start | bytes 1179652
  81.9 2.7 %copy-start.51 = (bf16[16,36,128]{2,1,0:T(8,128)(2,1)}, bf16[16,36,128]{2,1,0:T(8,128)(2,1)S(1)}, u32[]{:S(2)}) copy-start(bf16[16,36,128]{2,1,0:T(8,128)(2,1)S(1)} %get-tuple-element.151) | copy-start | bytes 442372
  85.4 26.6 %all-to-all-start.1 = ((bf16[8,240,128]{2,1,0:T(8,128)(2,1)}), bf16[8,240,128]{2,1,0:T(8,128)(2,1)S(1)}, u32[]{:S(2)}, u32[]{:S(2)}) async-start(bf16[8,240,128]{2,1,0:T(8,128)(2,1)} %shard_map.128), calls=%async_computation.1 | async-start | bytes 983040 | tf_op jit(solution)/shard_map/all_to_all | solution.py:336
  90.9 15.9 %collective-permute-start.20 = (bf16[256,768]{1,0:T(8,128)(2,1)}, bf16[256,768]{1,0:T(8,128)(2,1)S(1)}, u32[]{:S(2)}, u32[]{:S(2)}) collective-permute-start(bf16[256,768]{1,0:T(8,128)(2,1)} %copy-done.35), channel_id=1, source_target_pairs={{0,1},{1,0},{2,3},{3,2},{4,5},{5,4},{6,7},{7,6},{8,9},{9,8},{10,11... | collective-permute-start | bytes 1179656 | tf_op jit(solution)/shard_map/ppermute | solution.py:332
  91.8 15.7 %collective-permute-start.21 = (bf16[256,768]{1,0:T(8,128)(2,1)}, bf16[256,768]{1,0:T(8,128)(2,1)S(1)}, u32[]{:S(2)}, u32[]{:S(2)}) collective-permute-start(bf16[256,768]{1,0:T(8,128)(2,1)} %copy-done.34), channel_id=1, source_target_pairs={{0,2},{1,3},{2,0},{3,1},{4,6},{5,7},{6,4},{7,5},{8,10},{9,11},{10,... | collective-permute-start | bytes 1179656 | tf_op jit(solution)/shard_map/ppermute | solution.py:332
  92.8 18.5 %collective-permute-start.22 = (bf16[256,768]{1,0:T(8,128)(2,1)}, bf16[256,768]{1,0:T(8,128)(2,1)S(1)}, u32[]{:S(2)}, u32[]{:S(2)}) collective-permute-start(bf16[256,768]{1,0:T(8,128)(2,1)} %copy-done.33), channel_id=1, source_target_pairs={{0,3},{1,2},{2,1},{3,0},{4,7},{5,6},{6,5},{7,4},{8,11},{9,10},{10,... | collective-permute-start | bytes 1179656 | tf_op jit(solution)/shard_map/ppermute | solution.py:332
  93.6 5.9 %collective-permute-start.17 = (bf16[16,36,128]{2,1,0:T(8,128)(2,1)}, bf16[16,36,128]{2,1,0:T(8,128)(2,1)S(1)}, u32[]{:S(2)}, u32[]{:S(2)}) collective-permute-start(bf16[16,36,128]{2,1,0:T(8,128)(2,1)} %copy-done.53), channel_id=1, source_target_pairs={{0,32},{32,0},{64,96},{96,64},{1,33},{33,1},{65,97},{97,65},{2,34}... | collective-permute-start | bytes 442376 | tf_op jit(solution)/shard_map/ppermute | solution.py:332
  93.6 10.3 %collective-permute-start.18 = (bf16[16,36,128]{2,1,0:T(8,128)(2,1)}, bf16[16,36,128]{2,1,0:T(8,128)(2,1)S(1)}, u32[]{:S(2)}, u32[]{:S(2)}) collective-permute-start(bf16[16,36,128]{2,1,0:T(8,128)(2,1)} %copy-done.52), channel_id=1, source_target_pairs={{0,64},{32,96},{64,0},{96,32},{1,65},{33,97},{65,1},{97,33},{2,66}... | collective-permute-start | bytes 442376 | tf_op jit(solution)/shard_map/ppermute | solution.py:332
  100.1 6.1 %collective-permute-start.19 = (bf16[16,36,128]{2,1,0:T(8,128)(2,1)}, bf16[16,36,128]{2,1,0:T(8,128)(2,1)S(1)}, u32[]{:S(2)}, u32[]{:S(2)}) collective-permute-start(bf16[16,36,128]{2,1,0:T(8,128)(2,1)} %copy-done.51), channel_id=1, source_target_pairs={{0,96},{32,64},{64,32},{96,0},{1,97},{33,65},{65,33},{97,1},{2,98}... | collective-permute-start | bytes 442376 | tf_op jit(solution)/shard_map/ppermute | solution.py:332
  113.9 14.6 %copy-start.17 = (bf16[16,36,128]{2,1,0:T(8,128)(2,1)S(1)}, bf16[16,36,128]{2,1,0:T(8,128)(2,1)}, u32[]{:S(2)}) copy-start(bf16[16,36,128]{2,1,0:T(8,128)(2,1)} %copy-done.16) | copy-start | bytes 442372
  113.9 14.6 %copy-start.19 = (bf16[16,36,128]{2,1,0:T(8,128)(2,1)S(1)}, bf16[16,36,128]{2,1,0:T(8,128)(2,1)}, u32[]{:S(2)}) copy-start(bf16[16,36,128]{2,1,0:T(8,128)(2,1)} %copy-done.18) | copy-start | bytes 442372
  113.9 14.6 %copy-start.21 = (bf16[16,36,128]{2,1,0:T(8,128)(2,1)S(1)}, bf16[16,36,128]{2,1,0:T(8,128)(2,1)}, u32[]{:S(2)}) copy-start(bf16[16,36,128]{2,1,0:T(8,128)(2,1)} %copy-done.20) | copy-start | bytes 442372
  113.9 14.6 %copy-start.23 = (bf16[16,36,128]{2,1,0:T(8,128)(2,1)S(1)}, bf16[16,36,128]{2,1,0:T(8,128)(2,1)}, u32[]{:S(2)}) copy-start(bf16[16,36,128]{2,1,0:T(8,128)(2,1)} %copy-done.22) | copy-start | bytes 442372
  116.0 23.1 %copy-start.2 = (bf16[1008,256]{1,0:T(8,128)(2,1)S(1)}, bf16[1008,256]{1,0:T(8,128)(2,1)}, u32[]{:S(2)}) copy-start(bf16[1008,256]{1,0:T(8,128)(2,1)} %copy-done.1) | copy-start | bytes 1548292
  116.0 5.6 %collective-permute-start.23 = (bf16[16,36,128]{2,1,0:T(8,128)(2,1)S(1)}, bf16[16,36,128]{2,1,0:T(8,128)(2,1)S(1)}, u32[]{:S(2)}, u32[]{:S(2)}) collective-permute-start(bf16[16,36,128]{2,1,0:T(8,128)(2,1)S(1)} %get-tuple-element.164), channel_id=1, source_target_pairs={{0,32},{32,0},{64,96},{96,64},{1,33},{33,1},{65,97},{97,65},{2,34}... | collective-permute-start | bytes 442376 | tf_op jit(solution)/shard_map/ppermute | solution.py:332
  116.0 10.0 %collective-permute-start.24 = (bf16[16,36,128]{2,1,0:T(8,128)(2,1)S(1)}, bf16[16,36,128]{2,1,0:T(8,128)(2,1)S(1)}, u32[]{:S(2)}, u32[]{:S(2)}) collective-permute-start(bf16[16,36,128]{2,1,0:T(8,128)(2,1)S(1)} %get-tuple-element.165), channel_id=1, source_target_pairs={{0,64},{32,96},{64,0},{96,32},{1,65},{33,97},{65,1},{97,33},{2,66}... | collective-permute-start | bytes 442376 | tf_op jit(solution)/shard_map/ppermute | solution.py:332
  118.3 10.2 %collective-permute-start.25 = (bf16[16,36,128]{2,1,0:T(8,128)(2,1)S(1)}, bf16[16,36,128]{2,1,0:T(8,128)(2,1)S(1)}, u32[]{:S(2)}, u32[]{:S(2)}) collective-permute-start(bf16[16,36,128]{2,1,0:T(8,128)(2,1)S(1)} %get-tuple-element.166), channel_id=1, source_target_pairs={{0,96},{32,64},{64,32},{96,0},{1,97},{33,65},{65,33},{97,1},{2,98}... | collective-permute-start | bytes 442376 | tf_op jit(solution)/shard_map/ppermute | solution.py:332
  129.5 13.2 %copy-start.28 = (bf16[256,768]{1,0:T(8,128)(2,1)S(1)}, bf16[256,768]{1,0:T(8,128)(2,1)}, u32[]{:S(2)}) copy-start(bf16[256,768]{1,0:T(8,128)(2,1)} %copy-done.27) | copy-start | bytes 1179652
  129.5 13.2 %copy-start.30 = (bf16[256,768]{1,0:T(8,128)(2,1)S(1)}, bf16[256,768]{1,0:T(8,128)(2,1)}, u32[]{:S(2)}) copy-start(bf16[256,768]{1,0:T(8,128)(2,1)} %copy-done.29) | copy-start | bytes 1179652
  129.5 13.2 %copy-start.32 = (bf16[256,768]{1,0:T(8,128)(2,1)S(1)}, bf16[256,768]{1,0:T(8,128)(2,1)}, u32[]{:S(2)}) copy-start(bf16[256,768]{1,0:T(8,128)(2,1)} %copy-done.31) | copy-start | bytes 1179652
  129.5 19.7 %all-to-all-start.2 = ((bf16[16,72,128]{2,1,0:T(8,128)(2,1)}), bf16[16,72,128]{2,1,0:T(8,128)(2,1)S(1)}, u32[]{:S(2)}, u32[]{:S(2)}) async-start(bf16[16,72,128]{2,1,0:T(8,128)(2,1)} %shard_map.130), calls=%async_computation.2 | async-start | bytes 589824 | tf_op jit(solution)/shard_map/all_to_all | solution.py:336
  139.0 3.7 %copy-start.57 = (bf16[256,768]{1,0:T(8,128)(2,1)S(1)}, bf16[256,768]{1,0:T(8,128)(2,1)}, u32[]{:S(2)}) copy-start(bf16[256,768]{1,0:T(8,128)(2,1)} %copy-done.56) | copy-start | bytes 1179652
  145.2 12.5 %copy-start.41 = (bf16[256,768]{1,0:T(8,128)(2,1)S(1)}, bf16[256,768]{1,0:T(8,128)(2,1)}, u32[]{:S(2)}) copy-start(bf16[256,768]{1,0:T(8,128)(2,1)} %copy-done.40) | copy-start | bytes 1179652
  145.2 12.9 %copy-start.39 = (bf16[256,768]{1,0:T(8,128)(2,1)S(1)}, bf16[256,768]{1,0:T(8,128)(2,1)}, u32[]{:S(2)}) copy-start(bf16[256,768]{1,0:T(8,128)(2,1)} %copy-done.38) | copy-start | bytes 1179652
  145.2 34.6 %copy-start.37 = (bf16[256,768]{1,0:T(8,128)(2,1)S(1)}, bf16[256,768]{1,0:T(8,128)(2,1)}, u32[]{:S(2)}) copy-start(bf16[256,768]{1,0:T(8,128)(2,1)} %copy-done.36) | copy-start | bytes 1179652
  149.9 16.2 %all-to-all-start.3 = ((bf16[16,72,128]{2,1,0:T(8,128)(2,1)}), bf16[16,72,128]{2,1,0:T(8,128)(2,1)S(1)}, u32[]{:S(2)}, u32[]{:S(2)}) async-start(bf16[16,72,128]{2,1,0:T(8,128)(2,1)} %shard_map.131), calls=%async_computation.3 | async-start | bytes 589824 | tf_op jit(solution)/shard_map/all_to_all | solution.py:336
  156.1 11.6 %collective-permute-start.26 = (bf16[256,768]{1,0:T(8,128)(2,1)}, bf16[256,768]{1,0:T(8,128)(2,1)S(1)}, u32[]{:S(2)}, u32[]{:S(2)}) collective-permute-start(bf16[256,768]{1,0:T(8,128)(2,1)} %copy-done.42), channel_id=1, source_target_pairs={{0,1},{1,0},{2,3},{3,2},{4,5},{5,4},{6,7},{7,6},{8,9},{9,8},{10,11... | collective-permute-start | bytes 1179656 | tf_op jit(solution)/shard_map/ppermute | solution.py:332
  157.7 13.4 %collective-permute-start.27 = (bf16[256,768]{1,0:T(8,128)(2,1)S(1)}, bf16[256,768]{1,0:T(8,128)(2,1)S(1)}, u32[]{:S(2)}, u32[]{:S(2)}) collective-permute-start(bf16[256,768]{1,0:T(8,128)(2,1)S(1)} %copy-done.41), channel_id=1, source_target_pairs={{0,2},{1,3},{2,0},{3,1},{4,6},{5,7},{6,4},{7,5},{8,10},{9,11},{10,... | collective-permute-start | bytes 1179656 | tf_op jit(solution)/shard_map/ppermute | solution.py:332
  158.1 21.7 %collective-permute-start.28 = (bf16[256,768]{1,0:T(8,128)(2,1)S(1)}, bf16[256,768]{1,0:T(8,128)(2,1)S(1)}, u32[]{:S(2)}, u32[]{:S(2)}) collective-permute-start(bf16[256,768]{1,0:T(8,128)(2,1)S(1)} %copy-done.39), channel_id=1, source_target_pairs={{0,3},{1,2},{2,1},{3,0},{4,7},{5,6},{6,5},{7,4},{8,11},{9,10},{10,... | collective-permute-start | bytes 1179656 | tf_op jit(solution)/shard_map/ppermute | solution.py:332
  166.2 16.1 %collective-permute-start.31 = (bf16[16,72,128]{2,1,0:T(8,128)(2,1)S(1)}, bf16[16,72,128]{2,1,0:T(8,128)(2,1)S(1)}, u32[]{:S(2)}, u32[]{:S(2)}) collective-permute-start(bf16[16,72,128]{2,1,0:T(8,128)(2,1)S(1)} %all-to-all-done.3.b0), channel_id=1, source_target_pairs={{0,96},{32,64},{64,32},{96,0},{1,97},{33,65},{65,33},{97,1},{2,98}... | collective-permute-start | bytes 884744 | tf_op jit(solution)/shard_map/ppermute | solution.py:332
  167.7 14.6 %collective-permute-start.30 = (bf16[16,72,128]{2,1,0:T(8,128)(2,1)S(1)}, bf16[16,72,128]{2,1,0:T(8,128)(2,1)S(1)}, u32[]{:S(2)}, u32[]{:S(2)}) collective-permute-start(bf16[16,72,128]{2,1,0:T(8,128)(2,1)S(1)} %all-to-all-done.3.b0), channel_id=1, source_target_pairs={{0,64},{32,96},{64,0},{96,32},{1,65},{33,97},{65,1},{97,33},{2,66}... | collective-permute-start | bytes 884744 | tf_op jit(solution)/shard_map/ppermute | solution.py:332
  167.7 14.6 %collective-permute-start.29 = (bf16[16,72,128]{2,1,0:T(8,128)(2,1)S(1)}, bf16[16,72,128]{2,1,0:T(8,128)(2,1)S(1)}, u32[]{:S(2)}, u32[]{:S(2)}) collective-permute-start(bf16[16,72,128]{2,1,0:T(8,128)(2,1)S(1)} %all-to-all-done.3.b0), channel_id=1, source_target_pairs={{0,32},{32,0},{64,96},{96,64},{1,33},{33,1},{65,97},{97,65},{2,34}... | collective-permute-start | bytes 884744 | tf_op jit(solution)/shard_map/ppermute | solution.py:332
  (30 other events, 22.4 us)

commit v3 on v2

--- a/solution.py
+++ b/solution.py
@@ -190,13 +190,16 @@
     for a in range(3):
         base = PER_HEAD * a
         q, g = rows_of(query_first, query_rest, a), grads[base : base + PER_HEAD]
-        same = jnp.where(
-            position(iota((PER_HEAD, 1), 0), a) == position(iota((1, PER_HEAD), 1), a), 1.0, 0.0
-        ).astype(F32)
+        same = ones_where(position(iota((PER_HEAD, 1), 0), a) == position(iota((1, PER_HEAD), 1), a))
 
         def over_levels(column):
-            wide = jnp.broadcast_to(column, (PER_HEAD, 128))
-            return jnp.dot(same, wide, precision=lax.Precision.HIGHEST, preferred_element_type=F32)[:, 0:1]
+            high = column.astype(BF).astype(F32)
+            middle = (column - high).astype(BF).astype(F32)
+            lane = iota((PER_HEAD, 128), 1)
+            parts = jnp.where(
+                lane == 0, high, jnp.where(lane == 1, middle, jnp.where(lane == 2, column - high - middle, 0.0))
+            )
+            return jnp.sum(nn(same, parts.astype(BF)), 1, keepdims=True)
 
         expo = [
             jnp.exp(nt(q[low:high], keys[3 * level + a]) * SCALE) for level, (low, high) in enumerate(SPANS)
@@ -400,7 +403,7 @@
     third_got, first_got, mixed_slots[0], early[0] = tie((third_got, first_got, mixed_slots[0], early[0]))
     (rest_back,) = call(third_sum_kernel, [rest_shape])(second_back, *third_got)
     rest_got = deal(rest_back, "z")
-    rest_got, early, mixed_slots = tie((rest_got, early, mixed_slots))
+    rest_got, early = tie((rest_got, early))
 
     *late, changes = call(
         change_kernel,
@@ -412,9 +415,10 @@
     late = [late[0]] + [swap(late[k], "x", k) for k in (1, 2, 3)]
     change_slots = call(input_kernel, [slot] * 4, flops=2 * 1008 * 768 * 256)(changes, joined)
     spread = call(spread_kernel, [((ROWS, WIDTH), BF)], smem=2, flops=2 * 1024 * 512 * 768)
-    (mixed,) = spread(offsets, where, *mixed_slots)
+    late, mixed_slots = tie((late, mixed_slots))
     (parts,) = call(x_sum_kernel, [full_chunks], scratch=[((72, 128), F32)])(*early, *late)
     (part,) = call(yz_sum_kernel, [full_chunks])(deal(parts, YZ_AXES))
+    (mixed,) = spread(offsets, where, *mixed_slots)
     part, mixed, change_slots = tie((part, mixed, change_slots))
     block, change_slots = deal(part, YZ_AXES), to_heads(change_slots)
     blocks = [block] + [swap(block, "x", k) for k in (1, 2, 3)]

time: 186 us -> 176 us (0.946)
  local copies, waits for them, and re-layouts: 24.6 us -> 20.2 us
  waiting for transfers between devices: 60.6 us -> 57 us
    ppermute x32, waiting for transfers between devices: 49.8 us -> 43.6 us  [swap(): return lax.ppermute(value, axis, [(i, i ^ k) for i in range(count)])]
    unnamed x116 -> x94, local copies, waits for them, and re-layouts: 24.6 us -> 20.2 us
    all_to_all x4, waiting for transfers between devices: 10.8 us -> 13.4 us  [deal(): return lax.all_to_all(value, axis, 0, 0, tiled=True)]
  transfers between devices with their start and end apart: 36 -> 36, of which waited for: 17 -> 17; matrix products, arithmetic and copies ran while one was open for 0% -> 0% of each run, Pallas kernels for 9% -> 10%
where the time goes in v3:
time: 176 us; the launch traced here: 175 us
  starting transfers between devices  65.9 us (37%)
  waiting for transfers between devices  57 us (32%)
  Pallas kernels  31 us (18%)
  local copies, waits for them, and re-layouts  20.2 us (11%)
    ppermute x32, waiting for transfers between devices, swap(): return lax.ppermute(value, axis, [(i, i ^ k) for i in range(count)])  43.6 us
    ppermute x32, starting transfers between devices, swap(): return lax.ppermute(value, axis, [(i, i ^ k) for i in range(count)])  39.8 us
    pallas_call x18, Pallas kernels, run(): pl.pallas_call(body, out_shape=tuple((jax.ShapeDtypeStruct(shape, kind) f...  31 us
    all_to_all x4, starting transfers between devices, deal(): return lax.all_to_all(value, axis, 0, 0, tiled=True)  26 us
    unnamed x94, local copies, waits for them, and re-layouts  20.2 us
    all_to_all x4, waiting for transfers between devices, deal(): return lax.all_to_all(value, axis, 0, 0, tiled=True)  13.4 us
  transfers between devices with their start and end apart: 36, of which 17 were waited for; matrix products, arithmetic and copies ran while one was open for 0% of the time, Pallas kernels for 10%

profile of v3, /device:TPU:1, one launch (start us, length us, event | category | flops | bytes accessed | tf_op | source)
XLA Modules:
  0.0 175.1 jit_solution(1368802711723815292)
XLA Ops:
  0.7 1.1 copy-done
  2.5 1.2 shard_map.118
  3.8 2.2 %collective-permute-start.1 = (bf16[64,768]{1,0:T(8,128)(2,1)S(1)}, bf16[64,768]{1,0:T(8,128)(2,1)S(1)}, u32[]{:S(2)}, u32[]{:S(2)}) collective-permute-start(bf16[64,768]{1,0:T(8,128)(2,1)S(1)} %get-tuple-element.102), channel_id=1, source_target_pairs={{0,2},{1,3},{2,0},{3,1},{4,6},{5,7},{6,4},{7,5},{8,10},{9,11},{10,... | collective-permute-start | bytes 294920 | tf_op jit(solution)/shard_map/ppermute | solution.py:335
  6.0 2.7 %collective-permute-start.2 = (bf16[64,768]{1,0:T(8,128)(2,1)S(1)}, bf16[64,768]{1,0:T(8,128)(2,1)S(1)}, u32[]{:S(2)}, u32[]{:S(2)}) collective-permute-start(bf16[64,768]{1,0:T(8,128)(2,1)S(1)} %get-tuple-element.103), channel_id=1, source_target_pairs={{0,3},{1,2},{2,1},{3,0},{4,7},{5,6},{6,5},{7,4},{8,11},{9,10},{10,... | collective-permute-start | bytes 294920 | tf_op jit(solution)/shard_map/ppermute | solution.py:335
  8.8 1.4 shard_map.119
  11.6 1.1 collective-permute-done.2.x3
  12.7 1.1 collective-permute-start
  14.0 2.2 %shard_map.120 = (bf16[256,768]{1,0:T(8,128)(2,1)S(1)}, bf16[256,768]{1,0:T(8,128)(2,1)}, bf16[256,768]{1,0:T(8,128)(2,1)}, bf16[256,768]{1,0:T(8,128)(2,1)}) custom-call(s32[3,12]{1,0:T(4,128)S(1)} %copy-done.24, s32[2]{0:T(128)S(1)} %pad_add_fusion.where.place, bf16[512,768]{1,0:T(8,128)(2,1)S(1)} %copy-done.26), custom_call_target="tpu_custom_call" | custom-call | flops 805306368 | bytes 4194304 | tf_op jit(solution)/shard_map/pallas_call | solution.py:77
  16.9 1.3 shard_map.122
  18.8 2.8 %collective-permute-done.4.x2 = bf16[192,768]{1,0:T(8,128)(2,1)S(1)} collective-permute-done((bf16[192,768]{1,0:T(8,128)(2,1)S(1)}, bf16[192,768]{1,0:T(8,128)(2,1)S(1)}, u32[]{:S(2)}, u32[]{:S(2)}) %collective-permute-start.4) | collective-permute-done | bytes 294944 | tf_op jit(solution)/shard_map/ppermute | solution.py:335
  21.6 6.4 %all-to-all-start = ((bf16[8,240,128]{2,1,0:T(8,128)(2,1)}), bf16[8,240,128]{2,1,0:T(8,128)(2,1)S(1)}, u32[]{:S(2)}, u32[]{:S(2)}) async-start(bf16[8,240,128]{2,1,0:T(8,128)(2,1)} %get-tuple-element.131), calls=%async_computation | async-start | bytes 983040 | tf_op jit(solution)/shard_map/all_to_all | solution.py:339
  28.1 1.6 collective-permute-start.3
  29.7 1.0 collective-permute-start.5
  31.6 1.2 collective-permute-start.8
  32.8 6.5 %collective-permute-done.5.x3 = bf16[192,768]{1,0:T(8,128)(2,1)S(1)} collective-permute-done((bf16[192,768]{1,0:T(8,128)(2,1)S(1)}, bf16[192,768]{1,0:T(8,128)(2,1)S(1)}, u32[]{:S(2)}, u32[]{:S(2)}) %collective-permute-start.5) | collective-permute-done | bytes 294944 | tf_op jit(solution)/shard_map/ppermute | solution.py:335
  39.2 1.0 copy-done.6
  40.2 1.2 shard_map.123
  42.0 1.3 collective-permute-start.9
  43.5 2.6 %collective-permute-start.12 = (bf16[8,48,128]{2,1,0:T(8,128)(2,1)S(1)}, bf16[8,48,128]{2,1,0:T(8,128)(2,1)S(1)}, u32[]{:S(2)}, u32[]{:S(2)}) collective-permute-start(bf16[8,48,128]{2,1,0:T(8,128)(2,1)S(1)} %slice.4), channel_id=1, source_target_pairs={{0,96},{32,64},{64,32},{96,0},{1,97},{33,65},{65,33},{97,1},{2,98}... | collective-permute-start | bytes 294920 | tf_op jit(solution)/shard_map/ppermute | solution.py:335
  46.7 1.2 collective-permute-start.10
  47.9 7.5 %collective-permute-done.8.c3 = bf16[256,768]{1,0:T(8,128)(2,1)} collective-permute-done((bf16[256,768]{1,0:T(8,128)(2,1)}, bf16[256,768]{1,0:T(8,128)(2,1)}, u32[]{:S(2)}, u32[]{:S(2)}) %collective-permute-start.8) | collective-permute-done | bytes 393248 | tf_op jit(solution)/shard_map/ppermute | solution.py:335
  55.3 1.0 copy-done.4
  56.3 1.0 copy-done.7
  57.3 1.8 %shard_map.124 = (bf16[768,768]{1,0:T(8,128)(2,1)S(1)}, bf16[240,768]{1,0:T(8,128)(2,1)S(1)}, bf16[1008,128]{1,0:T(8,128)(2,1)S(1)}) custom-call(bf16[256,768]{1,0:T(8,128)(2,1)S(1)} %copy-done.4, bf16[256,768]{1,0:T(8,128)(2,1)} %collective-permute-done.6.c1, bf16[256,768]{1,0:T(8,128)(2,1)} %collective-permute-done.7.c2, ...), custom_call_target="tpu_custom_call" | custom-call | flops 198180864 | bytes 4194304 | tf_op jit(solution)/shard_map/pallas_call | solution.py:77
  59.9 0.9 copy-done.39
  60.8 0.8 copy-done.44
  61.6 7.2 %shard_map.125 = (bf16[1008,128]{1,0:T(8,128)(2,1)S(1)}, bf16[1008,128]{1,0:T(8,128)(2,1)S(1)}, bf16[768,128]{1,0:T(8,128)(2,1)S(1)}, bf16[768,128]{1,0:T(8,128)...) custom-call(s32[3,12]{1,0:T(4,128)S(1)} %copy-done.25, ...), custom_call_target="tpu_custom_call" | custom-call | flops 924844032 | bytes 4194304 | tf_op jit(solution)/shard_map/pallas_call | solution.py:77
  69.5 1.7 collective-permute-start.16
  71.1 1.2 collective-permute-start.13
  72.3 2.5 %collective-permute-start.14 = (bf16[8,48,128]{2,1,0:T(8,128)(2,1)S(1)}, bf16[8,48,128]{2,1,0:T(8,128)(2,1)S(1)}, u32[]{:S(2)}, u32[]{:S(2)}) collective-permute-start(bf16[8,48,128]{2,1,0:T(8,128)(2,1)S(1)} %get-tuple-element.137), channel_id=1, source_target_pairs={{0,64},{32,96},{64,0},{96,32},{1,65},{33,97},{65,1},{97,33},{2,66}... | collective-permute-start | bytes 294920 | tf_op jit(solution)/shard_map/ppermute | solution.py:335
  76.5 1.5 shard_map.127
  80.0 1.9 %collective-permute-done.15.t3 = bf16[8,48,128]{2,1,0:T(8,128)(2,1)S(1)} collective-permute-done((bf16[8,48,128]{2,1,0:T(8,128)(2,1)S(1)}, bf16[8,48,128]{2,1,0:T(8,128)(2,1)S(1)}, u32[]{:S(2)}, u32[]{:S(2)}) %collective-permute-start.15) | collective-permute-done | bytes 98336 | tf_op jit(solution)/shard_map/ppermute | solution.py:335
  82.6 0.8 shard_map.128
  83.5 5.5 %all-to-all-start.1 = ((bf16[8,240,128]{2,1,0:T(8,128)(2,1)}), bf16[8,240,128]{2,1,0:T(8,128)(2,1)S(1)}, u32[]{:S(2)}, u32[]{:S(2)}) async-start(bf16[8,240,128]{2,1,0:T(8,128)(2,1)} %shard_map.128), calls=%async_computation.1 | async-start | bytes 983040 | tf_op jit(solution)/shard_map/all_to_all | solution.py:339
  89.0 0.9 collective-permute-start.23
  89.9 1.0 collective-permute-start.24
  90.9 0.9 collective-permute-start.25
  91.7 2.6 %collective-permute-start.18 = (bf16[16,36,128]{2,1,0:T(8,128)(2,1)}, bf16[16,36,128]{2,1,0:T(8,128)(2,1)S(1)}, u32[]{:S(2)}, u32[]{:S(2)}) collective-permute-start(bf16[16,36,128]{2,1,0:T(8,128)(2,1)} %copy-done.41), channel_id=1, source_target_pairs={{0,64},{32,96},{64,0},{96,32},{1,65},{33,97},{65,1},{97,33},{2,66}... | collective-permute-start | bytes 442376 | tf_op jit(solution)/shard_map/ppermute | solution.py:335
  94.3 1.7 collective-permute-done.17.refs_1_
  96.6 1.2 collective-permute-start.19
  97.8 2.5 %collective-permute-done.18.refs_2_ = bf16[16,36,128]{2,1,0:T(8,128)(2,1)S(1)} collective-permute-done((bf16[16,36,128]{2,1,0:T(8,128)(2,1)}, bf16[16,36,128]{2,1,0:T(8,128)(2,1)S(1)}, u32[]{:S(2)}, u32[]{:S(2)}) %collective-permute-start.18) | collective-permute-done | bytes 147488 | tf_op jit(solution)/shard_map/ppermute | solution.py:335
  101.0 1.3 collective-permute-done.19.refs_3_
  102.9 3.3 %all-to-all-done.1.rests = bf16[8,240,128]{2,1,0:T(8,128)(2,1)S(1)} async-done(((bf16[8,240,128]{2,1,0:T(8,128)(2,1)}), bf16[8,240,128]{2,1,0:T(8,128)(2,1)S(1)}, u32[]{:S(2)}, u32[]{:S(2)}) %all-to-all-start.1) | async-done | bytes 491552 | tf_op jit(solution)/shard_map/all_to_all | solution.py:339
  106.2 0.9 copy-done.13
  107.1 0.9 copy-done.15
  108.1 1.2 shard_map.129
  110.3 3.7 %collective-permute-start.22 = (bf16[16,36,128]{2,1,0:T(8,128)(2,1)S(1)}, bf16[16,36,128]{2,1,0:T(8,128)(2,1)S(1)}, u32[]{:S(2)}, u32[]{:S(2)}) collective-permute-start(bf16[16,36,128]{2,1,0:T(8,128)(2,1)S(1)} %get-tuple-element.166), channel_id=1, source_target_pairs={{0,96},{32,64},{64,32},{96,0},{1,97},{33,65},{65,33},{97,1},{2,98}... | collective-permute-start | bytes 442376 | tf_op jit(solution)/shard_map/ppermute | solution.py:335
  114.0 1.4 collective-permute-done.20.refs_5_
  115.4 2.4 %collective-permute-done.21.refs_6_ = bf16[16,36,128]{2,1,0:T(8,128)(2,1)S(1)} collective-permute-done((bf16[16,36,128]{2,1,0:T(8,128)(2,1)S(1)}, bf16[16,36,128]{2,1,0:T(8,128)(2,1)S(1)}, u32[]{:S(2)}, u32[]{:S(2)}) %collective-permute-start.21) | collective-permute-done | bytes 147488 | tf_op jit(solution)/shard_map/ppermute | solution.py:335
  117.8 2.8 %collective-permute-done.22.refs_7_ = bf16[16,36,128]{2,1,0:T(8,128)(2,1)S(1)} collective-permute-done((bf16[16,36,128]{2,1,0:T(8,128)(2,1)S(1)}, bf16[16,36,128]{2,1,0:T(8,128)(2,1)S(1)}, u32[]{:S(2)}, u32[]{:S(2)}) %collective-permute-start.22) | collective-permute-done | bytes 147488 | tf_op jit(solution)/shard_map/ppermute | solution.py:335
  120.7 0.9 shard_map.130
  121.6 8.2 %all-to-all-start.2 = ((bf16[16,72,128]{2,1,0:T(8,128)(2,1)}), bf16[16,72,128]{2,1,0:T(8,128)(2,1)S(1)}, u32[]{:S(2)}, u32[]{:S(2)}) async-start(bf16[16,72,128]{2,1,0:T(8,128)(2,1)} %shard_map.130), calls=%async_computation.2 | async-start | bytes 589824 | tf_op jit(solution)/shard_map/all_to_all | solution.py:339
  131.3 3.1 %shard_map.132 = bf16[512,768]{1,0:T(8,128)(2,1)} custom-call(s32[3,12]{1,0:T(4,128)S(1)} %copy-done.25, s32[2]{0:T(128)S(1)} %pad_add_fusion.where.place, bf16[256,768]{1,0:T(8,128)(2,1)S(1)} %copy-done.46, bf16[256,768]{1,0:T(8,128)(2,1)} %collective-permute-done.23.s1, bf16[256,768]{1,0:T(8,128)(2,1)} %collective-permute-done.24.s2, ...), custom_call_target="tpu_custom_call" | custom-call | flops 805306368 | bytes 4194304 | tf_op jit(solution)/shard_map/pallas_call | solution.py:77
  134.4 4.8 %all-to-all-done.2.got = bf16[16,72,128]{2,1,0:T(8,128)(2,1)S(1)} async-done(((bf16[16,72,128]{2,1,0:T(8,128)(2,1)}), bf16[16,72,128]{2,1,0:T(8,128)(2,1)S(1)}, u32[]{:S(2)}, u32[]{:S(2)}) %all-to-all-start.2) | async-done | bytes 294944 | tf_op jit(solution)/shard_map/all_to_all | solution.py:339
  140.0 6.0 %all-to-all-start.3 = ((bf16[16,72,128]{2,1,0:T(8,128)(2,1)}), bf16[16,72,128]{2,1,0:T(8,128)(2,1)S(1)}, u32[]{:S(2)}, u32[]{:S(2)}) async-start(bf16[16,72,128]{2,1,0:T(8,128)(2,1)} %shard_map.131), calls=%async_computation.3 | async-start | bytes 589824 | tf_op jit(solution)/shard_map/all_to_all | solution.py:339
  146.0 2.5 %collective-permute-start.26 = (bf16[256,768]{1,0:T(8,128)(2,1)S(1)}, bf16[256,768]{1,0:T(8,128)(2,1)S(1)}, u32[]{:S(2)}, u32[]{:S(2)}) collective-permute-start(bf16[256,768]{1,0:T(8,128)(2,1)S(1)} %copy-done.31), channel_id=1, source_target_pairs={{0,1},{1,0},{2,3},{3,2},{4,5},{5,4},{6,7},{7,6},{8,9},{9,8},{10,11... | collective-permute-start | bytes 1179656 | tf_op jit(solution)/shard_map/ppermute | solution.py:335
  148.9 1.3 collective-permute-start.28
  150.2 5.2 %all-to-all-done.3.b0 = bf16[16,72,128]{2,1,0:T(8,128)(2,1)S(1)} async-done(((bf16[16,72,128]{2,1,0:T(8,128)(2,1)}), bf16[16,72,128]{2,1,0:T(8,128)(2,1)S(1)}, u32[]{:S(2)}, u32[]{:S(2)}) %all-to-all-start.3) | async-done | bytes 294944 | tf_op jit(solution)/shard_map/all_to_all | solution.py:339
  155.4 1.6 collective-permute-start.31
  157.4 1.3 collective-permute-start.29
  158.7 2.7 %collective-permute-done.27.s2 = bf16[256,768]{1,0:T(8,128)(2,1)S(1)} collective-permute-done((bf16[256,768]{1,0:T(8,128)(2,1)S(1)}, bf16[256,768]{1,0:T(8,128)(2,1)S(1)}, u32[]{:S(2)}, u32[]{:S(2)}) %collective-permute-start.27) | collective-permute-done | bytes 393248 | tf_op jit(solution)/shard_map/ppermute | solution.py:335
  161.3 8.9 %collective-permute-done.28.s3 = bf16[256,768]{1,0:T(8,128)(2,1)S(1)} collective-permute-done((bf16[256,768]{1,0:T(8,128)(2,1)S(1)}, bf16[256,768]{1,0:T(8,128)(2,1)S(1)}, u32[]{:S(2)}, u32[]{:S(2)}) %collective-permute-start.28) | collective-permute-done | bytes 393248 | tf_op jit(solution)/shard_map/ppermute | solution.py:335
  170.2 2.4 %shard_map.134 = bf16[512,768]{1,0:T(8,128)(2,1)} custom-call(s32[3,12]{1,0:T(4,128)S(1)} %copy-done.25, s32[2]{0:T(128)S(1)} %pad_add_fusion.where.place, bf16[256,768]{1,0:T(8,128)(2,1)S(1)} %get-tuple-element.185.s0, bf16[256,768]{1,0:T(8,128)(2,1)S(1)} %collective-permute-done.26.s1, bf16[256,768]{1,0:T(8,128)(2,1)S(1)} %collective-permute-done.27.s2, ...), custom_call_target="tpu_custom_call" | custom-call | flops 805306368 | bytes 4194304 | tf_op jit(solution)/shard_map/pallas_call | solution.py:77
  172.7 2.5 %shard_map.135 = (f32[192,768]{1,0:T(8,128)}, f32[192,768]{1,0:T(8,128)}, f32[192,768]{1,0:T(8,128)}, f32[192,768]{1,0:T(8,128)}) custom-call(s32[2]{0:T(128)S(1)} %pad_add_fusion.where.place, bf16[16,72,128]{2,1,0:T(8,128)(2,1)S(1)} %all-to-all-done.3.b0, bf16[16,72,128]{2,1,0:T(8,128)(2,1)S(1)} %collective-permute-done.29.b1, ...), custom_call_target="tpu_custom_call" | custom-call | bytes 4194304 | tf_op jit(solution)/shard_map/pallas_call | solution.py:77
  (122 shorter events, 17.7 us)
Async XLA Ops:
  0.7 1.1 copy-start
  3.8 10.1 %copy-start.9 = (bf16[192,768]{1,0:T(8,128)(2,1)S(1)}, bf16[192,768]{1,0:T(8,128)(2,1)}, u32[]{:S(2)}) copy-start(bf16[192,768]{1,0:T(8,128)(2,1)} %w_query.1) | copy-start | bytes 884740
  3.8 10.1 %copy-start.10 = (bf16[192,768]{1,0:T(8,128)(2,1)S(1)}, bf16[192,768]{1,0:T(8,128)(2,1)}, u32[]{:S(2)}) copy-start(bf16[192,768]{1,0:T(8,128)(2,1)} %w_key.1) | copy-start | bytes 884740
  3.8 10.1 %copy-start.11 = (bf16[192,768]{1,0:T(8,128)(2,1)S(1)}, bf16[192,768]{1,0:T(8,128)(2,1)}, u32[]{:S(2)}) copy-start(bf16[192,768]{1,0:T(8,128)(2,1)} %w_value.1) | copy-start | bytes 884740
  3.8 7.8 %collective-permute-start.1 = (bf16[64,768]{1,0:T(8,128)(2,1)S(1)}, bf16[64,768]{1,0:T(8,128)(2,1)S(1)}, u32[]{:S(2)}, u32[]{:S(2)}) collective-permute-start(bf16[64,768]{1,0:T(8,128)(2,1)S(1)} %get-tuple-element.102), channel_id=1, source_target_pairs={{0,2},{1,3},{2,0},{3,1},{4,6},{5,7},{6,4},{7,5},{8,10},{9,11},{10,... | collective-permute-start | bytes 294920 | tf_op jit(solution)/shard_map/ppermute | solution.py:335
  6.0 6.7 %collective-permute-start.2 = (bf16[64,768]{1,0:T(8,128)(2,1)S(1)}, bf16[64,768]{1,0:T(8,128)(2,1)S(1)}, u32[]{:S(2)}, u32[]{:S(2)}) collective-permute-start(bf16[64,768]{1,0:T(8,128)(2,1)S(1)} %get-tuple-element.103), channel_id=1, source_target_pairs={{0,3},{1,2},{2,1},{3,0},{4,7},{5,6},{6,5},{7,4},{8,11},{9,10},{10,... | collective-permute-start | bytes 294920 | tf_op jit(solution)/shard_map/ppermute | solution.py:335
  11.5 2.4 %copy-start.26 = (bf16[512,768]{1,0:T(8,128)(2,1)S(1)}, bf16[512,768]{1,0:T(8,128)(2,1)}, u32[]{:S(2)}) copy-start(bf16[512,768]{1,0:T(8,128)(2,1)} %source.5) | copy-start | bytes 2359300
  12.7 8.9 %collective-permute-start.4 = (bf16[192,768]{1,0:T(8,128)(2,1)S(1)}, bf16[192,768]{1,0:T(8,128)(2,1)S(1)}, u32[]{:S(2)}, u32[]{:S(2)}) collective-permute-start(bf16[192,768]{1,0:T(8,128)(2,1)S(1)} %get-tuple-element.120), channel_id=1, source_target_pairs={{0,2},{1,3},{2,0},{3,1},{4,6},{5,7},{6,4},{7,5},{8,10},{9,11},{10,... | collective-permute-start | bytes 884744 | tf_op jit(solution)/shard_map/ppermute | solution.py:335
  12.7 4.2 %collective-permute-start = (bf16[64,768]{1,0:T(8,128)(2,1)S(1)}, bf16[64,768]{1,0:T(8,128)(2,1)S(1)}, u32[]{:S(2)}, u32[]{:S(2)}) collective-permute-start(bf16[64,768]{1,0:T(8,128)(2,1)S(1)} %get-tuple-element.101), channel_id=1, source_target_pairs={{0,1},{1,0},{2,3},{3,2},{4,5},{5,4},{6,7},{7,6},{8,9},{9,8},{10,11... | collective-permute-start | bytes 294920 | tf_op jit(solution)/shard_map/ppermute | solution.py:335
  16.9 11.1 %copy-start.35 = (bf16[192,768]{1,0:T(8,128)(2,1)S(1)}, bf16[192,768]{1,0:T(8,128)(2,1)}, u32[]{:S(2)}) copy-start(bf16[192,768]{1,0:T(8,128)(2,1)} %copy-done.34) | copy-start | bytes 884740
  16.9 12.7 %copy-start.33 = (bf16[192,768]{1,0:T(8,128)(2,1)S(1)}, bf16[192,768]{1,0:T(8,128)(2,1)}, u32[]{:S(2)}) copy-start(bf16[192,768]{1,0:T(8,128)(2,1)} %copy-done.32) | copy-start | bytes 884740
  21.6 11.2 %copy-start.5 = (bf16[192,768]{1,0:T(8,128)(2,1)}, bf16[192,768]{1,0:T(8,128)(2,1)S(1)}, u32[]{:S(2)}) copy-start(bf16[192,768]{1,0:T(8,128)(2,1)S(1)} %collective-permute-done.4.x2) | copy-start | bytes 884740
  21.6 21.8 %all-to-all-start = ((bf16[8,240,128]{2,1,0:T(8,128)(2,1)}), bf16[8,240,128]{2,1,0:T(8,128)(2,1)S(1)}, u32[]{:S(2)}, u32[]{:S(2)}) async-start(bf16[8,240,128]{2,1,0:T(8,128)(2,1)} %get-tuple-element.131), calls=%async_computation | async-start | bytes 983040 | tf_op jit(solution)/shard_map/all_to_all | solution.py:339
  28.1 4.7 %collective-permute-start.3 = (bf16[192,768]{1,0:T(8,128)(2,1)S(1)}, bf16[192,768]{1,0:T(8,128)(2,1)S(1)}, u32[]{:S(2)}, u32[]{:S(2)}) collective-permute-start(bf16[192,768]{1,0:T(8,128)(2,1)S(1)} %copy-done.35), channel_id=1, source_target_pairs={{0,1},{1,0},{2,3},{3,2},{4,5},{5,4},{6,7},{7,6},{8,9},{9,8},{10,11... | collective-permute-start | bytes 884744 | tf_op jit(solution)/shard_map/ppermute | solution.py:335
  29.7 9.6 %collective-permute-start.5 = (bf16[192,768]{1,0:T(8,128)(2,1)S(1)}, bf16[192,768]{1,0:T(8,128)(2,1)S(1)}, u32[]{:S(2)}, u32[]{:S(2)}) collective-permute-start(bf16[192,768]{1,0:T(8,128)(2,1)S(1)} %copy-done.33), channel_id=1, source_target_pairs={{0,3},{1,2},{2,1},{3,0},{4,7},{5,6},{6,5},{7,4},{8,11},{9,10},{10,... | collective-permute-start | bytes 884744 | tf_op jit(solution)/shard_map/ppermute | solution.py:335
  30.6 15.4 %collective-permute-start.6 = (bf16[256,768]{1,0:T(8,128)(2,1)}, bf16[256,768]{1,0:T(8,128)(2,1)}, u32[]{:S(2)}, u32[]{:S(2)}) collective-permute-start(bf16[256,768]{1,0:T(8,128)(2,1)} %get-tuple-element.126), channel_id=1, source_target_pairs={{0,1},{1,0},{2,3},{3,2},{4,5},{5,4},{6,7},{7,6},{8,9},{9,8},{10,11... | collective-permute-start | bytes 1179656 | tf_op jit(solution)/shard_map/ppermute | solution.py:335
  31.0 15.6 %collective-permute-start.7 = (bf16[256,768]{1,0:T(8,128)(2,1)}, bf16[256,768]{1,0:T(8,128)(2,1)}, u32[]{:S(2)}, u32[]{:S(2)}) collective-permute-start(bf16[256,768]{1,0:T(8,128)(2,1)} %get-tuple-element.127), channel_id=1, source_target_pairs={{0,2},{1,3},{2,0},{3,1},{4,6},{5,7},{6,4},{7,5},{8,10},{9,11},{10,... | collective-permute-start | bytes 1179656 | tf_op jit(solution)/shard_map/ppermute | solution.py:335
  31.6 23.8 %collective-permute-start.8 = (bf16[256,768]{1,0:T(8,128)(2,1)}, bf16[256,768]{1,0:T(8,128)(2,1)}, u32[]{:S(2)}, u32[]{:S(2)}) collective-permute-start(bf16[256,768]{1,0:T(8,128)(2,1)} %get-tuple-element.128), channel_id=1, source_target_pairs={{0,3},{1,2},{2,1},{3,0},{4,7},{5,6},{6,5},{7,4},{8,11},{9,10},{10,... | collective-permute-start | bytes 1179656 | tf_op jit(solution)/shard_map/ppermute | solution.py:335
  39.2 1.0 copy-start.6
  42.0 17.8 %copy-start.25 = (s32[3,12]{1,0:T(4,128)S(1)}, s32[3,12]{1,0:T(4,128)}, u32[]{:S(2)}) copy-start(s32[3,12]{1,0:T(4,128)} %offs.11) | copy-start | bytes 436
  42.0 17.1 %collective-permute-start.9 = (bf16[768,128]{1,0:T(8,128)(2,1)}, bf16[768,128]{1,0:T(8,128)(2,1)S(1)}, u32[]{:S(2)}, u32[]{:S(2)}) collective-permute-start(bf16[768,128]{1,0:T(8,128)(2,1)} %get-tuple-element.130.first_own), channel_id=1, source_target_pairs={{0,4},{4,0},{8,12},{12,8},{16,20},{20,16},{24,28},{28,24},{1,5},{5... | collective-permute-start | bytes 589832 | tf_op jit(solution)/shard_map/ppermute | solution.py:335
  43.4 16.4 %copy-start.37 = (bf16[768,128]{1,0:T(8,128)(2,1)S(1)}, bf16[768,128]{1,0:T(8,128)(2,1)}, u32[]{:S(2)}) copy-start(bf16[768,128]{1,0:T(8,128)(2,1)} %copy-done.36) | copy-start | bytes 589828
  43.5 16.4 %collective-permute-start.12 = (bf16[8,48,128]{2,1,0:T(8,128)(2,1)S(1)}, bf16[8,48,128]{2,1,0:T(8,128)(2,1)S(1)}, u32[]{:S(2)}, u32[]{:S(2)}) collective-permute-start(bf16[8,48,128]{2,1,0:T(8,128)(2,1)S(1)} %slice.4), channel_id=1, source_target_pairs={{0,96},{32,64},{64,32},{96,0},{1,97},{33,65},{65,33},{97,1},{2,98}... | collective-permute-start | bytes 294920 | tf_op jit(solution)/shard_map/ppermute | solution.py:335
  46.0 13.8 %collective-permute-start.11 = (bf16[8,48,128]{2,1,0:T(8,128)(2,1)S(1)}, bf16[8,48,128]{2,1,0:T(8,128)(2,1)S(1)}, u32[]{:S(2)}, u32[]{:S(2)}) collective-permute-start(bf16[8,48,128]{2,1,0:T(8,128)(2,1)S(1)} %slice.4), channel_id=1, source_target_pairs={{0,64},{32,96},{64,0},{96,32},{1,65},{33,97},{65,1},{97,33},{2,66}... | collective-permute-start | bytes 294920 | tf_op jit(solution)/shard_map/ppermute | solution.py:335
  46.7 13.2 %collective-permute-start.10 = (bf16[8,48,128]{2,1,0:T(8,128)(2,1)S(1)}, bf16[8,48,128]{2,1,0:T(8,128)(2,1)S(1)}, u32[]{:S(2)}, u32[]{:S(2)}) collective-permute-start(bf16[8,48,128]{2,1,0:T(8,128)(2,1)S(1)} %slice.4), channel_id=1, source_target_pairs={{0,32},{32,0},{64,96},{96,64},{1,33},{33,1},{65,97},{97,65},{2,34}... | collective-permute-start | bytes 294920 | tf_op jit(solution)/shard_map/ppermute | solution.py:335
  55.3 1.0 copy-start.4
  56.3 1.0 copy-start.7
  59.9 0.9 copy-start.39
  61.6 13.4 %copy-start.8 = (bf16[192,768]{1,0:T(8,128)(2,1)S(1)}, bf16[192,768]{1,0:T(8,128)(2,1)}, u32[]{:S(2)}) copy-start(bf16[192,768]{1,0:T(8,128)(2,1)} %w_out.3) | copy-start | bytes 884740
  69.5 12.5 %collective-permute-start.16 = (bf16[768,128]{1,0:T(8,128)(2,1)S(1)}, bf16[768,128]{1,0:T(8,128)(2,1)S(1)}, u32[]{:S(2)}, u32[]{:S(2)}) collective-permute-start(bf16[768,128]{1,0:T(8,128)(2,1)S(1)} %get-tuple-element.139), channel_id=1, source_target_pairs={{0,4},{4,0},{8,12},{12,8},{16,20},{20,16},{24,28},{28,24},{1,5},{5... | collective-permute-start | bytes 589832 | tf_op jit(solution)/shard_map/ppermute | solution.py:335
  71.1 8.9 %collective-permute-start.13 = (bf16[8,48,128]{2,1,0:T(8,128)(2,1)S(1)}, bf16[8,48,128]{2,1,0:T(8,128)(2,1)S(1)}, u32[]{:S(2)}, u32[]{:S(2)}) collective-permute-start(bf16[8,48,128]{2,1,0:T(8,128)(2,1)S(1)} %get-tuple-element.136), channel_id=1, source_target_pairs={{0,32},{32,0},{64,96},{96,64},{1,33},{33,1},{65,97},{97,65},{2,34}... | collective-permute-start | bytes 294920 | tf_op jit(solution)/shard_map/ppermute | solution.py:335
  72.3 7.7 %collective-permute-start.14 = (bf16[8,48,128]{2,1,0:T(8,128)(2,1)S(1)}, bf16[8,48,128]{2,1,0:T(8,128)(2,1)S(1)}, u32[]{:S(2)}, u32[]{:S(2)}) collective-permute-start(bf16[8,48,128]{2,1,0:T(8,128)(2,1)S(1)} %get-tuple-element.137), channel_id=1, source_target_pairs={{0,64},{32,96},{64,0},{96,32},{1,65},{33,97},{65,1},{97,33},{2,66}... | collective-permute-start | bytes 294920 | tf_op jit(solution)/shard_map/ppermute | solution.py:335
  74.8 7.2 %collective-permute-start.15 = (bf16[8,48,128]{2,1,0:T(8,128)(2,1)S(1)}, bf16[8,48,128]{2,1,0:T(8,128)(2,1)S(1)}, u32[]{:S(2)}, u32[]{:S(2)}) collective-permute-start(bf16[8,48,128]{2,1,0:T(8,128)(2,1)S(1)} %get-tuple-element.138), channel_id=1, source_target_pairs={{0,96},{32,64},{64,32},{96,0},{1,97},{33,65},{65,33},{97,1},{2,98}... | collective-permute-start | bytes 294920 | tf_op jit(solution)/shard_map/ppermute | solution.py:335
  76.5 5.5 %copy-start.27 = (bf16[256,768]{1,0:T(8,128)(2,1)}, bf16[256,768]{1,0:T(8,128)(2,1)S(1)}, u32[]{:S(2)}) copy-start(bf16[256,768]{1,0:T(8,128)(2,1)S(1)} %get-tuple-element.170) | copy-start | bytes 1179652
  76.5 6.2 %copy-start.28 = (bf16[256,768]{1,0:T(8,128)(2,1)}, bf16[256,768]{1,0:T(8,128)(2,1)S(1)}, u32[]{:S(2)}) copy-start(bf16[256,768]{1,0:T(8,128)(2,1)S(1)} %get-tuple-element.169) | copy-start | bytes 1179652
  76.5 6.2 %copy-start.29 = (bf16[256,768]{1,0:T(8,128)(2,1)}, bf16[256,768]{1,0:T(8,128)(2,1)S(1)}, u32[]{:S(2)}) copy-start(bf16[256,768]{1,0:T(8,128)(2,1)S(1)} %get-tuple-element.168) | copy-start | bytes 1179652
  80.0 2.6 %copy-start.40 = (bf16[16,36,128]{2,1,0:T(8,128)(2,1)}, bf16[16,36,128]{2,1,0:T(8,128)(2,1)S(1)}, u32[]{:S(2)}) copy-start(bf16[16,36,128]{2,1,0:T(8,128)(2,1)S(1)} %get-tuple-element.155) | copy-start | bytes 442372
  83.5 22.7 %all-to-all-start.1 = ((bf16[8,240,128]{2,1,0:T(8,128)(2,1)}), bf16[8,240,128]{2,1,0:T(8,128)(2,1)S(1)}, u32[]{:S(2)}, u32[]{:S(2)}) async-start(bf16[8,240,128]{2,1,0:T(8,128)(2,1)} %shard_map.128), calls=%async_computation.1 | async-start | bytes 983040 | tf_op jit(solution)/shard_map/all_to_all | solution.py:339
  89.0 21.4 %collective-permute-start.23 = (bf16[256,768]{1,0:T(8,128)(2,1)}, bf16[256,768]{1,0:T(8,128)(2,1)}, u32[]{:S(2)}, u32[]{:S(2)}) collective-permute-start(bf16[256,768]{1,0:T(8,128)(2,1)} %copy-done.29), channel_id=1, source_target_pairs={{0,1},{1,0},{2,3},{3,2},{4,5},{5,4},{6,7},{7,6},{8,9},{9,8},{10,11... | collective-permute-start | bytes 1179656 | tf_op jit(solution)/shard_map/ppermute | solution.py:335
  89.9 6.1 %collective-permute-start.17 = (bf16[16,36,128]{2,1,0:T(8,128)(2,1)}, bf16[16,36,128]{2,1,0:T(8,128)(2,1)S(1)}, u32[]{:S(2)}, u32[]{:S(2)}) collective-permute-start(bf16[16,36,128]{2,1,0:T(8,128)(2,1)} %copy-done.42), channel_id=1, source_target_pairs={{0,32},{32,0},{64,96},{96,64},{1,33},{33,1},{65,97},{97,65},{2,34}... | collective-permute-start | bytes 442376 | tf_op jit(solution)/shard_map/ppermute | solution.py:335
  89.9 24.1 %collective-permute-start.24 = (bf16[256,768]{1,0:T(8,128)(2,1)}, bf16[256,768]{1,0:T(8,128)(2,1)}, u32[]{:S(2)}, u32[]{:S(2)}) collective-permute-start(bf16[256,768]{1,0:T(8,128)(2,1)} %copy-done.28), channel_id=1, source_target_pairs={{0,2},{1,3},{2,0},{3,1},{4,6},{5,7},{6,4},{7,5},{8,10},{9,11},{10,... | collective-permute-start | bytes 1179656 | tf_op jit(solution)/shard_map/ppermute | solution.py:335
  90.9 23.1 %collective-permute-start.25 = (bf16[256,768]{1,0:T(8,128)(2,1)}, bf16[256,768]{1,0:T(8,128)(2,1)}, u32[]{:S(2)}, u32[]{:S(2)}) collective-permute-start(bf16[256,768]{1,0:T(8,128)(2,1)} %copy-done.27), channel_id=1, source_target_pairs={{0,3},{1,2},{2,1},{3,0},{4,7},{5,6},{6,5},{7,4},{8,11},{9,10},{10,... | collective-permute-start | bytes 1179656 | tf_op jit(solution)/shard_map/ppermute | solution.py:335
  91.7 8.6 %collective-permute-start.18 = (bf16[16,36,128]{2,1,0:T(8,128)(2,1)}, bf16[16,36,128]{2,1,0:T(8,128)(2,1)S(1)}, u32[]{:S(2)}, u32[]{:S(2)}) collective-permute-start(bf16[16,36,128]{2,1,0:T(8,128)(2,1)} %copy-done.41), channel_id=1, source_target_pairs={{0,64},{32,96},{64,0},{96,32},{1,65},{33,97},{65,1},{97,33},{2,66}... | collective-permute-start | bytes 442376 | tf_op jit(solution)/shard_map/ppermute | solution.py:335
  96.6 5.6 %collective-permute-start.19 = (bf16[16,36,128]{2,1,0:T(8,128)(2,1)}, bf16[16,36,128]{2,1,0:T(8,128)(2,1)S(1)}, u32[]{:S(2)}, u32[]{:S(2)}) collective-permute-start(bf16[16,36,128]{2,1,0:T(8,128)(2,1)} %copy-done.40), channel_id=1, source_target_pairs={{0,96},{32,64},{64,32},{96,0},{1,97},{33,65},{65,33},{97,1},{2,98}... | collective-permute-start | bytes 442376 | tf_op jit(solution)/shard_map/ppermute | solution.py:335
  106.2 0.9 copy-start.13
  107.1 0.9 copy-start.15
  108.1 12.6 %copy-start.17 = (bf16[16,36,128]{2,1,0:T(8,128)(2,1)S(1)}, bf16[16,36,128]{2,1,0:T(8,128)(2,1)}, u32[]{:S(2)}) copy-start(bf16[16,36,128]{2,1,0:T(8,128)(2,1)} %copy-done.16) | copy-start | bytes 442372
  108.1 12.6 %copy-start.19 = (bf16[16,36,128]{2,1,0:T(8,128)(2,1)S(1)}, bf16[16,36,128]{2,1,0:T(8,128)(2,1)}, u32[]{:S(2)}) copy-start(bf16[16,36,128]{2,1,0:T(8,128)(2,1)} %copy-done.18) | copy-start | bytes 442372
  108.1 12.6 %copy-start.21 = (bf16[16,36,128]{2,1,0:T(8,128)(2,1)S(1)}, bf16[16,36,128]{2,1,0:T(8,128)(2,1)}, u32[]{:S(2)}) copy-start(bf16[16,36,128]{2,1,0:T(8,128)(2,1)} %copy-done.20) | copy-start | bytes 442372
  108.1 12.6 %copy-start.23 = (bf16[16,36,128]{2,1,0:T(8,128)(2,1)S(1)}, bf16[16,36,128]{2,1,0:T(8,128)(2,1)}, u32[]{:S(2)}) copy-start(bf16[16,36,128]{2,1,0:T(8,128)(2,1)} %copy-done.22) | copy-start | bytes 442372
  110.1 19.7 %copy-start.2 = (bf16[1008,256]{1,0:T(8,128)(2,1)S(1)}, bf16[1008,256]{1,0:T(8,128)(2,1)}, u32[]{:S(2)}) copy-start(bf16[1008,256]{1,0:T(8,128)(2,1)} %copy-done.1) | copy-start | bytes 1548292
  110.1 5.3 %collective-permute-start.20 = (bf16[16,36,128]{2,1,0:T(8,128)(2,1)S(1)}, bf16[16,36,128]{2,1,0:T(8,128)(2,1)S(1)}, u32[]{:S(2)}, u32[]{:S(2)}) collective-permute-start(bf16[16,36,128]{2,1,0:T(8,128)(2,1)S(1)} %get-tuple-element.164), channel_id=1, source_target_pairs={{0,32},{32,0},{64,96},{96,64},{1,33},{33,1},{65,97},{97,65},{2,34}... | collective-permute-start | bytes 442376 | tf_op jit(solution)/shard_map/ppermute | solution.py:335
  110.1 7.7 %collective-permute-start.21 = (bf16[16,36,128]{2,1,0:T(8,128)(2,1)S(1)}, bf16[16,36,128]{2,1,0:T(8,128)(2,1)S(1)}, u32[]{:S(2)}, u32[]{:S(2)}) collective-permute-start(bf16[16,36,128]{2,1,0:T(8,128)(2,1)S(1)} %get-tuple-element.165), channel_id=1, source_target_pairs={{0,64},{32,96},{64,0},{96,32},{1,65},{33,97},{65,1},{97,33},{2,66}... | collective-permute-start | bytes 442376 | tf_op jit(solution)/shard_map/ppermute | solution.py:335
  110.3 10.4 %collective-permute-start.22 = (bf16[16,36,128]{2,1,0:T(8,128)(2,1)S(1)}, bf16[16,36,128]{2,1,0:T(8,128)(2,1)S(1)}, u32[]{:S(2)}, u32[]{:S(2)}) collective-permute-start(bf16[16,36,128]{2,1,0:T(8,128)(2,1)S(1)} %get-tuple-element.166), channel_id=1, source_target_pairs={{0,96},{32,64},{64,32},{96,0},{1,97},{33,65},{65,33},{97,1},{2,98}... | collective-permute-start | bytes 442376 | tf_op jit(solution)/shard_map/ppermute | solution.py:335
  121.6 17.6 %all-to-all-start.2 = ((bf16[16,72,128]{2,1,0:T(8,128)(2,1)}), bf16[16,72,128]{2,1,0:T(8,128)(2,1)S(1)}, u32[]{:S(2)}, u32[]{:S(2)}) async-start(bf16[16,72,128]{2,1,0:T(8,128)(2,1)} %shard_map.130), calls=%async_computation.2 | async-start | bytes 589824 | tf_op jit(solution)/shard_map/all_to_all | solution.py:339
  129.8 1.5 copy-start.46
  134.4 11.6 %copy-start.31 = (bf16[256,768]{1,0:T(8,128)(2,1)S(1)}, bf16[256,768]{1,0:T(8,128)(2,1)}, u32[]{:S(2)}) copy-start(bf16[256,768]{1,0:T(8,128)(2,1)} %copy-done.30) | copy-start | bytes 1179652
  140.0 15.4 %all-to-all-start.3 = ((bf16[16,72,128]{2,1,0:T(8,128)(2,1)}), bf16[16,72,128]{2,1,0:T(8,128)(2,1)S(1)}, u32[]{:S(2)}, u32[]{:S(2)}) async-start(bf16[16,72,128]{2,1,0:T(8,128)(2,1)} %shard_map.131), calls=%async_computation.3 | async-start | bytes 589824 | tf_op jit(solution)/shard_map/all_to_all | solution.py:339
  146.0 11.4 %collective-permute-start.26 = (bf16[256,768]{1,0:T(8,128)(2,1)S(1)}, bf16[256,768]{1,0:T(8,128)(2,1)S(1)}, u32[]{:S(2)}, u32[]{:S(2)}) collective-permute-start(bf16[256,768]{1,0:T(8,128)(2,1)S(1)} %copy-done.31), channel_id=1, source_target_pairs={{0,1},{1,0},{2,3},{3,2},{4,5},{5,4},{6,7},{7,6},{8,9},{9,8},{10,11... | collective-permute-start | bytes 1179656 | tf_op jit(solution)/shard_map/ppermute | solution.py:335
  148.5 12.9 %collective-permute-start.27 = (bf16[256,768]{1,0:T(8,128)(2,1)S(1)}, bf16[256,768]{1,0:T(8,128)(2,1)S(1)}, u32[]{:S(2)}, u32[]{:S(2)}) collective-permute-start(bf16[256,768]{1,0:T(8,128)(2,1)S(1)} %get-tuple-element.187), channel_id=1, source_target_pairs={{0,2},{1,3},{2,0},{3,1},{4,6},{5,7},{6,4},{7,5},{8,10},{9,11},{10,... | collective-permute-start | bytes 1179656 | tf_op jit(solution)/shard_map/ppermute | solution.py:335
  148.9 21.3 %collective-permute-start.28 = (bf16[256,768]{1,0:T(8,128)(2,1)S(1)}, bf16[256,768]{1,0:T(8,128)(2,1)S(1)}, u32[]{:S(2)}, u32[]{:S(2)}) collective-permute-start(bf16[256,768]{1,0:T(8,128)(2,1)S(1)} %get-tuple-element.188), channel_id=1, source_target_pairs={{0,3},{1,2},{2,1},{3,0},{4,7},{5,6},{6,5},{7,4},{8,11},{9,10},{10,... | collective-permute-start | bytes 1179656 | tf_op jit(solution)/shard_map/ppermute | solution.py:335
  155.4 17.2 %collective-permute-start.31 = (bf16[16,72,128]{2,1,0:T(8,128)(2,1)S(1)}, bf16[16,72,128]{2,1,0:T(8,128)(2,1)S(1)}, u32[]{:S(2)}, u32[]{:S(2)}) collective-permute-start(bf16[16,72,128]{2,1,0:T(8,128)(2,1)S(1)} %all-to-all-done.3.b0), channel_id=1, source_target_pairs={{0,96},{32,64},{64,32},{96,0},{1,97},{33,65},{65,33},{97,1},{2,98}... | collective-permute-start | bytes 884744 | tf_op jit(solution)/shard_map/ppermute | solution.py:335
  157.0 15.7 %collective-permute-start.30 = (bf16[16,72,128]{2,1,0:T(8,128)(2,1)S(1)}, bf16[16,72,128]{2,1,0:T(8,128)(2,1)S(1)}, u32[]{:S(2)}, u32[]{:S(2)}) collective-permute-start(bf16[16,72,128]{2,1,0:T(8,128)(2,1)S(1)} %all-to-all-done.3.b0), channel_id=1, source_target_pairs={{0,64},{32,96},{64,0},{96,32},{1,65},{33,97},{65,1},{97,33},{2,66}... | collective-permute-start | bytes 884744 | tf_op jit(solution)/shard_map/ppermute | solution.py:335
  157.4 15.3 %collective-permute-start.29 = (bf16[16,72,128]{2,1,0:T(8,128)(2,1)S(1)}, bf16[16,72,128]{2,1,0:T(8,128)(2,1)S(1)}, u32[]{:S(2)}, u32[]{:S(2)}) collective-permute-start(bf16[16,72,128]{2,1,0:T(8,128)(2,1)S(1)} %all-to-all-done.3.b0), channel_id=1, source_target_pairs={{0,32},{32,0},{64,96},{96,64},{1,33},{33,1},{65,97},{97,65},{2,34}... | collective-permute-start | bytes 884744 | tf_op jit(solution)/shard_map/ppermute | solution.py:335
  (19 other events, 13.3 us)

commit v4 on v3

--- a/solution.py
+++ b/solution.py
@@ -400,7 +400,7 @@
     mixed_slots = call(output_kernel, [slot] * 4, flops=2 * 1008 * 768 * 128)(attended, w_out)
     mixed_slots = to_heads(mixed_slots)
     early = [early[0]] + [swap(early[k], "x", k) for k in (1, 2, 3)]
-    third_got, first_got, mixed_slots[0], early[0] = tie((third_got, first_got, mixed_slots[0], early[0]))
+    third_got, first_got, early[0] = tie((third_got, first_got, early[0]))
     (rest_back,) = call(third_sum_kernel, [rest_shape])(second_back, *third_got)
     rest_got = deal(rest_back, "z")
     rest_got, early = tie((rest_got, early))

time: 176 us -> 180 us (1.023)
  waiting for transfers between devices: 57 us -> 61.8 us
    ppermute x32, waiting for transfers between devices: 43.6 us -> 51.1 us  [swap(): return lax.ppermute(value, axis, [(i, i ^ k) for i in range(count)])]
    all_to_all x4, waiting for transfers between devices: 13.4 us -> 10.7 us  [deal(): return lax.all_to_all(value, axis, 0, 0, tiled=True)]
    unnamed x94 -> x92, local copies, waits for them, and re-layouts: 20.2 us -> 18.7 us
where the time goes in v4:
time: 180 us
  starting transfers between devices  65.9 us (37%)
  waiting for transfers between devices  61.8 us (34%)
  Pallas kernels  32 us (18%)
  local copies, waits for them, and re-layouts  18.7 us (10%)
    ppermute x32, waiting for transfers between devices, swap(): return lax.ppermute(value, axis, [(i, i ^ k) for i in range(count)])  51.1 us
    ppermute x32, starting transfers between devices, swap(): return lax.ppermute(value, axis, [(i, i ^ k) for i in range(count)])  38.2 us
    pallas_call x18, Pallas kernels, run(): pl.pallas_call(body, out_shape=tuple((jax.ShapeDtypeStruct(shape, kind) f...  32 us
    all_to_all x4, starting transfers between devices, deal(): return lax.all_to_all(value, axis, 0, 0, tiled=True)  27.7 us
    unnamed x92, local copies, waits for them, and re-layouts  18.7 us
    all_to_all x4, waiting for transfers between devices, deal(): return lax.all_to_all(value, axis, 0, 0, tiled=True)  10.7 us
  transfers between devices with their start and end apart: 36, of which 17 were waited for; matrix products, arithmetic and copies ran while one was open for 0% of the time, Pallas kernels for 10%

profile of v4, /device:TPU:1, one launch (start us, length us, event | category | flops | bytes accessed | tf_op | source)
XLA Modules:
  0.0 179.5 jit_solution(8596300163374342328)
XLA Ops:
  0.7 1.1 copy-done
  2.5 1.2 shard_map.118
  3.8 2.2 %collective-permute-start.1 = (bf16[64,768]{1,0:T(8,128)(2,1)S(1)}, bf16[64,768]{1,0:T(8,128)(2,1)S(1)}, u32[]{:S(2)}, u32[]{:S(2)}) collective-permute-start(bf16[64,768]{1,0:T(8,128)(2,1)S(1)} %get-tuple-element.101), channel_id=1, source_target_pairs={{0,2},{1,3},{2,0},{3,1},{4,6},{5,7},{6,4},{7,5},{8,10},{9,11},{10,... | collective-permute-start | bytes 294920 | tf_op jit(solution)/shard_map/ppermute | solution.py:335
  6.0 2.7 %collective-permute-start.2 = (bf16[64,768]{1,0:T(8,128)(2,1)S(1)}, bf16[64,768]{1,0:T(8,128)(2,1)S(1)}, u32[]{:S(2)}, u32[]{:S(2)}) collective-permute-start(bf16[64,768]{1,0:T(8,128)(2,1)S(1)} %get-tuple-element.102), channel_id=1, source_target_pairs={{0,3},{1,2},{2,1},{3,0},{4,7},{5,6},{6,5},{7,4},{8,11},{9,10},{10,... | collective-permute-start | bytes 294920 | tf_op jit(solution)/shard_map/ppermute | solution.py:335
  8.8 1.4 shard_map.119
  11.6 1.1 collective-permute-done.2.x3
  12.7 1.1 collective-permute-start
  14.0 2.2 %shard_map.120 = (bf16[256,768]{1,0:T(8,128)(2,1)S(1)}, bf16[256,768]{1,0:T(8,128)(2,1)}, bf16[256,768]{1,0:T(8,128)(2,1)}, bf16[256,768]{1,0:T(8,128)(2,1)}) custom-call(s32[3,12]{1,0:T(4,128)S(1)} %copy-done.26, s32[2]{0:T(128)S(1)} %pad_add_fusion.where.place, bf16[512,768]{1,0:T(8,128)(2,1)S(1)} %copy-done.28), custom_call_target="tpu_custom_call" | custom-call | flops 805306368 | bytes 4194304 | tf_op jit(solution)/shard_map/pallas_call | solution.py:77
  16.9 1.3 shard_map.122
  18.8 2.8 %collective-permute-done.4.x2 = bf16[192,768]{1,0:T(8,128)(2,1)S(1)} collective-permute-done((bf16[192,768]{1,0:T(8,128)(2,1)S(1)}, bf16[192,768]{1,0:T(8,128)(2,1)S(1)}, u32[]{:S(2)}, u32[]{:S(2)}) %collective-permute-start.4) | collective-permute-done | bytes 294944 | tf_op jit(solution)/shard_map/ppermute | solution.py:335
  21.6 6.4 %all-to-all-start = ((bf16[8,240,128]{2,1,0:T(8,128)(2,1)}), bf16[8,240,128]{2,1,0:T(8,128)(2,1)S(1)}, u32[]{:S(2)}, u32[]{:S(2)}) async-start(bf16[8,240,128]{2,1,0:T(8,128)(2,1)} %get-tuple-element.130), calls=%async_computation | async-start | bytes 983040 | tf_op jit(solution)/shard_map/all_to_all | solution.py:339
  28.1 1.6 collective-permute-start.3
  29.7 1.0 collective-permute-start.5
  31.6 1.2 collective-permute-start.8
  32.8 6.5 %collective-permute-done.5.x3 = bf16[192,768]{1,0:T(8,128)(2,1)S(1)} collective-permute-done((bf16[192,768]{1,0:T(8,128)(2,1)S(1)}, bf16[192,768]{1,0:T(8,128)(2,1)S(1)}, u32[]{:S(2)}, u32[]{:S(2)}) %collective-permute-start.5) | collective-permute-done | bytes 294944 | tf_op jit(solution)/shard_map/ppermute | solution.py:335
  39.2 1.0 copy-done.6
  40.2 1.2 shard_map.123
  42.1 1.3 collective-permute-start.9
  43.5 2.6 %collective-permute-start.12 = (bf16[8,48,128]{2,1,0:T(8,128)(2,1)S(1)}, bf16[8,48,128]{2,1,0:T(8,128)(2,1)S(1)}, u32[]{:S(2)}, u32[]{:S(2)}) collective-permute-start(bf16[8,48,128]{2,1,0:T(8,128)(2,1)S(1)} %slice.4), channel_id=1, source_target_pairs={{0,96},{32,64},{64,32},{96,0},{1,97},{33,65},{65,33},{97,1},{2,98}... | collective-permute-start | bytes 294920 | tf_op jit(solution)/shard_map/ppermute | solution.py:335
  46.7 1.2 collective-permute-start.10
  47.9 7.5 %collective-permute-done.8.c3 = bf16[256,768]{1,0:T(8,128)(2,1)} collective-permute-done((bf16[256,768]{1,0:T(8,128)(2,1)}, bf16[256,768]{1,0:T(8,128)(2,1)}, u32[]{:S(2)}, u32[]{:S(2)}) %collective-permute-start.8) | collective-permute-done | bytes 393248 | tf_op jit(solution)/shard_map/ppermute | solution.py:335
  55.3 1.0 copy-done.4
  56.3 1.0 copy-done.7
  57.3 1.8 %shard_map.124 = (bf16[768,768]{1,0:T(8,128)(2,1)S(1)}, bf16[240,768]{1,0:T(8,128)(2,1)S(1)}, bf16[1008,128]{1,0:T(8,128)(2,1)S(1)}) custom-call(bf16[256,768]{1,0:T(8,128)(2,1)S(1)} %copy-done.4, bf16[256,768]{1,0:T(8,128)(2,1)} %collective-permute-done.6.c1, bf16[256,768]{1,0:T(8,128)(2,1)} %collective-permute-done.7.c2, ...), custom_call_target="tpu_custom_call" | custom-call | flops 198180864 | bytes 4194304 | tf_op jit(solution)/shard_map/pallas_call | solution.py:77
  59.9 0.9 copy-done.38
  60.8 0.8 copy-done.43
  61.6 7.1 %shard_map.125 = (bf16[1008,128]{1,0:T(8,128)(2,1)S(1)}, bf16[1008,128]{1,0:T(8,128)(2,1)S(1)}, bf16[768,128]{1,0:T(8,128)(2,1)S(1)}, bf16[768,128]{1,0:T(8,128)...) custom-call(s32[3,12]{1,0:T(4,128)S(1)} %copy-done.27, ...), custom_call_target="tpu_custom_call" | custom-call | flops 924844032 | bytes 4194304 | tf_op jit(solution)/shard_map/pallas_call | solution.py:77
  68.8 1.7 collective-permute-start.16
  70.5 1.2 collective-permute-start.13
  71.7 2.5 %collective-permute-start.14 = (bf16[8,48,128]{2,1,0:T(8,128)(2,1)S(1)}, bf16[8,48,128]{2,1,0:T(8,128)(2,1)S(1)}, u32[]{:S(2)}, u32[]{:S(2)}) collective-permute-start(bf16[8,48,128]{2,1,0:T(8,128)(2,1)S(1)} %get-tuple-element.136), channel_id=1, source_target_pairs={{0,64},{32,96},{64,0},{96,32},{1,65},{33,97},{65,1},{97,33},{2,66}... | collective-permute-start | bytes 294920 | tf_op jit(solution)/shard_map/ppermute | solution.py:335
  74.4 1.5 shard_map.126
  76.0 2.8 %collective-permute-done.14.t2 = bf16[8,48,128]{2,1,0:T(8,128)(2,1)S(1)} collective-permute-done((bf16[8,48,128]{2,1,0:T(8,128)(2,1)S(1)}, bf16[8,48,128]{2,1,0:T(8,128)(2,1)S(1)}, u32[]{:S(2)}, u32[]{:S(2)}) %collective-permute-start.14) | collective-permute-done | bytes 98336 | tf_op jit(solution)/shard_map/ppermute | solution.py:335
  78.8 2.6 %collective-permute-done.15.t3 = bf16[8,48,128]{2,1,0:T(8,128)(2,1)S(1)} collective-permute-done((bf16[8,48,128]{2,1,0:T(8,128)(2,1)S(1)}, bf16[8,48,128]{2,1,0:T(8,128)(2,1)S(1)}, u32[]{:S(2)}, u32[]{:S(2)}) %collective-permute-start.15) | collective-permute-done | bytes 98336 | tf_op jit(solution)/shard_map/ppermute | solution.py:335
  81.4 0.9 shard_map.127
  82.2 5.5 %all-to-all-start.1 = ((bf16[8,240,128]{2,1,0:T(8,128)(2,1)}), bf16[8,240,128]{2,1,0:T(8,128)(2,1)S(1)}, u32[]{:S(2)}, u32[]{:S(2)}) async-start(bf16[8,240,128]{2,1,0:T(8,128)(2,1)} %shard_map.127), calls=%async_computation.1 | async-start | bytes 983040 | tf_op jit(solution)/shard_map/all_to_all | solution.py:339
  87.7 1.0 copy-done.8
  88.7 0.9 copy-done.13
  89.6 1.7 shard_map.129
  92.1 0.9 collective-permute-start.23
  93.0 1.0 collective-permute-start.24
  94.6 1.8 %collective-permute-start.18 = (bf16[16,36,128]{2,1,0:T(8,128)(2,1)}, bf16[16,36,128]{2,1,0:T(8,128)(2,1)S(1)}, u32[]{:S(2)}, u32[]{:S(2)}) collective-permute-start(bf16[16,36,128]{2,1,0:T(8,128)(2,1)} %copy-done.40), channel_id=1, source_target_pairs={{0,64},{32,96},{64,0},{96,32},{1,65},{33,97},{65,1},{97,33},{2,66}... | collective-permute-start | bytes 442376 | tf_op jit(solution)/shard_map/ppermute | solution.py:335
  96.5 2.7 %collective-permute-done.17.refs_1_ = bf16[16,36,128]{2,1,0:T(8,128)(2,1)S(1)} collective-permute-done((bf16[16,36,128]{2,1,0:T(8,128)(2,1)}, bf16[16,36,128]{2,1,0:T(8,128)(2,1)S(1)}, u32[]{:S(2)}, u32[]{:S(2)}) %collective-permute-start.17) | collective-permute-done | bytes 147488 | tf_op jit(solution)/shard_map/ppermute | solution.py:335
  100.2 2.5 %collective-permute-done.18.refs_2_ = bf16[16,36,128]{2,1,0:T(8,128)(2,1)S(1)} collective-permute-done((bf16[16,36,128]{2,1,0:T(8,128)(2,1)}, bf16[16,36,128]{2,1,0:T(8,128)(2,1)S(1)}, u32[]{:S(2)}, u32[]{:S(2)}) %collective-permute-start.18) | collective-permute-done | bytes 147488 | tf_op jit(solution)/shard_map/ppermute | solution.py:335
  103.3 2.5 %collective-permute-done.19.refs_3_ = bf16[16,36,128]{2,1,0:T(8,128)(2,1)S(1)} collective-permute-done((bf16[16,36,128]{2,1,0:T(8,128)(2,1)}, bf16[16,36,128]{2,1,0:T(8,128)(2,1)S(1)}, u32[]{:S(2)}, u32[]{:S(2)}) %collective-permute-start.19) | collective-permute-done | bytes 147488 | tf_op jit(solution)/shard_map/ppermute | solution.py:335
  106.5 0.9 copy-done.15
  107.4 0.9 copy-done.17
  108.4 1.2 shard_map.128
  110.4 2.0 %collective-permute-start.20 = (bf16[16,36,128]{2,1,0:T(8,128)(2,1)S(1)}, bf16[16,36,128]{2,1,0:T(8,128)(2,1)S(1)}, u32[]{:S(2)}, u32[]{:S(2)}) collective-permute-start(bf16[16,36,128]{2,1,0:T(8,128)(2,1)S(1)} %get-tuple-element.162), channel_id=1, source_target_pairs={{0,32},{32,0},{64,96},{96,64},{1,33},{33,1},{65,97},{97,65},{2,34}... | collective-permute-start | bytes 442376 | tf_op jit(solution)/shard_map/ppermute | solution.py:335
  112.4 1.6 collective-permute-start.21
  115.6 5.2 %collective-permute-done.21.refs_6_ = bf16[16,36,128]{2,1,0:T(8,128)(2,1)S(1)} collective-permute-done((bf16[16,36,128]{2,1,0:T(8,128)(2,1)S(1)}, bf16[16,36,128]{2,1,0:T(8,128)(2,1)S(1)}, u32[]{:S(2)}, u32[]{:S(2)}) %collective-permute-start.21) | collective-permute-done | bytes 147488 | tf_op jit(solution)/shard_map/ppermute | solution.py:335
  120.8 2.8 %collective-permute-done.22.refs_7_ = bf16[16,36,128]{2,1,0:T(8,128)(2,1)S(1)} collective-permute-done((bf16[16,36,128]{2,1,0:T(8,128)(2,1)S(1)}, bf16[16,36,128]{2,1,0:T(8,128)(2,1)S(1)}, u32[]{:S(2)}, u32[]{:S(2)}) %collective-permute-start.22) | collective-permute-done | bytes 147488 | tf_op jit(solution)/shard_map/ppermute | solution.py:335
  123.6 0.9 shard_map.130
  124.5 9.4 %all-to-all-start.2 = ((bf16[16,72,128]{2,1,0:T(8,128)(2,1)}), bf16[16,72,128]{2,1,0:T(8,128)(2,1)S(1)}, u32[]{:S(2)}, u32[]{:S(2)}) async-start(bf16[16,72,128]{2,1,0:T(8,128)(2,1)} %shard_map.130), calls=%async_computation.2 | async-start | bytes 589824 | tf_op jit(solution)/shard_map/all_to_all | solution.py:339
  135.4 3.1 %shard_map.132 = bf16[512,768]{1,0:T(8,128)(2,1)} custom-call(s32[3,12]{1,0:T(4,128)S(1)} %copy-done.27, s32[2]{0:T(128)S(1)} %pad_add_fusion.where.place, bf16[256,768]{1,0:T(8,128)(2,1)S(1)} %copy-done.45, bf16[256,768]{1,0:T(8,128)(2,1)} %collective-permute-done.23.s1, bf16[256,768]{1,0:T(8,128)(2,1)} %collective-permute-done.24.s2, ...), custom_call_target="tpu_custom_call" | custom-call | flops 805306368 | bytes 4194304 | tf_op jit(solution)/shard_map/pallas_call | solution.py:77
  138.5 4.9 %all-to-all-done.2.got = bf16[16,72,128]{2,1,0:T(8,128)(2,1)S(1)} async-done(((bf16[16,72,128]{2,1,0:T(8,128)(2,1)}), bf16[16,72,128]{2,1,0:T(8,128)(2,1)S(1)}, u32[]{:S(2)}, u32[]{:S(2)}) %all-to-all-start.2) | async-done | bytes 294944 | tf_op jit(solution)/shard_map/all_to_all | solution.py:339
  144.3 6.4 %all-to-all-start.3 = ((bf16[16,72,128]{2,1,0:T(8,128)(2,1)}), bf16[16,72,128]{2,1,0:T(8,128)(2,1)S(1)}, u32[]{:S(2)}, u32[]{:S(2)}) async-start(bf16[16,72,128]{2,1,0:T(8,128)(2,1)} %shard_map.131), calls=%async_computation.3 | async-start | bytes 589824 | tf_op jit(solution)/shard_map/all_to_all | solution.py:339
  150.7 2.0 %collective-permute-start.26 = (bf16[256,768]{1,0:T(8,128)(2,1)S(1)}, bf16[256,768]{1,0:T(8,128)(2,1)S(1)}, u32[]{:S(2)}, u32[]{:S(2)}) collective-permute-start(bf16[256,768]{1,0:T(8,128)(2,1)S(1)} %copy-done.30), channel_id=1, source_target_pairs={{0,1},{1,0},{2,3},{3,2},{4,5},{5,4},{6,7},{7,6},{8,9},{9,8},{10,11... | collective-permute-start | bytes 1179656 | tf_op jit(solution)/shard_map/ppermute | solution.py:335
  153.0 1.3 collective-permute-start.28
  154.3 5.7 %all-to-all-done.3.b0 = bf16[16,72,128]{2,1,0:T(8,128)(2,1)S(1)} async-done(((bf16[16,72,128]{2,1,0:T(8,128)(2,1)}), bf16[16,72,128]{2,1,0:T(8,128)(2,1)S(1)}, u32[]{:S(2)}, u32[]{:S(2)}) %all-to-all-start.3) | async-done | bytes 294944 | tf_op jit(solution)/shard_map/all_to_all | solution.py:339
  160.5 2.8 %collective-permute-start.29 = (bf16[16,72,128]{2,1,0:T(8,128)(2,1)S(1)}, bf16[16,72,128]{2,1,0:T(8,128)(2,1)S(1)}, u32[]{:S(2)}, u32[]{:S(2)}) collective-permute-start(bf16[16,72,128]{2,1,0:T(8,128)(2,1)S(1)} %all-to-all-done.3.b0), channel_id=1, source_target_pairs={{0,32},{32,0},{64,96},{96,64},{1,33},{33,1},{65,97},{97,65},{2,34}... | collective-permute-start | bytes 884744 | tf_op jit(solution)/shard_map/ppermute | solution.py:335
  163.3 2.5 %collective-permute-done.27.s2 = bf16[256,768]{1,0:T(8,128)(2,1)S(1)} collective-permute-done((bf16[256,768]{1,0:T(8,128)(2,1)S(1)}, bf16[256,768]{1,0:T(8,128)(2,1)S(1)}, u32[]{:S(2)}, u32[]{:S(2)}) %collective-permute-start.27) | collective-permute-done | bytes 393248 | tf_op jit(solution)/shard_map/ppermute | solution.py:335
  165.9 8.7 %collective-permute-done.28.s3 = bf16[256,768]{1,0:T(8,128)(2,1)S(1)} collective-permute-done((bf16[256,768]{1,0:T(8,128)(2,1)S(1)}, bf16[256,768]{1,0:T(8,128)(2,1)S(1)}, u32[]{:S(2)}, u32[]{:S(2)}) %collective-permute-start.28) | collective-permute-done | bytes 393248 | tf_op jit(solution)/shard_map/ppermute | solution.py:335
  174.6 2.4 %shard_map.134 = bf16[512,768]{1,0:T(8,128)(2,1)} custom-call(s32[3,12]{1,0:T(4,128)S(1)} %copy-done.27, s32[2]{0:T(128)S(1)} %pad_add_fusion.where.place, bf16[256,768]{1,0:T(8,128)(2,1)S(1)} %get-tuple-element.183.s0, bf16[256,768]{1,0:T(8,128)(2,1)S(1)} %collective-permute-done.26.s1, bf16[256,768]{1,0:T(8,128)(2,1)S(1)} %collective-permute-done.27.s2, ...), custom_call_target="tpu_custom_call" | custom-call | flops 805306368 | bytes 4194304 | tf_op jit(solution)/shard_map/pallas_call | solution.py:77
  177.1 2.5 %shard_map.135 = (f32[192,768]{1,0:T(8,128)}, f32[192,768]{1,0:T(8,128)}, f32[192,768]{1,0:T(8,128)}, f32[192,768]{1,0:T(8,128)}) custom-call(s32[2]{0:T(128)S(1)} %pad_add_fusion.where.place, bf16[16,72,128]{2,1,0:T(8,128)(2,1)S(1)} %all-to-all-done.3.b0, bf16[16,72,128]{2,1,0:T(8,128)(2,1)S(1)} %collective-permute-done.29.b1, ...), custom_call_target="tpu_custom_call" | custom-call | bytes 4194304 | tf_op jit(solution)/shard_map/pallas_call | solution.py:77
  (120 shorter events, 16.1 us)
Async XLA Ops:
  0.7 1.1 copy-start
  3.8 10.1 %copy-start.9 = (bf16[192,768]{1,0:T(8,128)(2,1)S(1)}, bf16[192,768]{1,0:T(8,128)(2,1)}, u32[]{:S(2)}) copy-start(bf16[192,768]{1,0:T(8,128)(2,1)} %w_query.1) | copy-start | bytes 884740
  3.8 10.1 %copy-start.10 = (bf16[192,768]{1,0:T(8,128)(2,1)S(1)}, bf16[192,768]{1,0:T(8,128)(2,1)}, u32[]{:S(2)}) copy-start(bf16[192,768]{1,0:T(8,128)(2,1)} %w_key.1) | copy-start | bytes 884740
  3.8 10.1 %copy-start.11 = (bf16[192,768]{1,0:T(8,128)(2,1)S(1)}, bf16[192,768]{1,0:T(8,128)(2,1)}, u32[]{:S(2)}) copy-start(bf16[192,768]{1,0:T(8,128)(2,1)} %w_value.1) | copy-start | bytes 884740
  3.8 7.8 %collective-permute-start.1 = (bf16[64,768]{1,0:T(8,128)(2,1)S(1)}, bf16[64,768]{1,0:T(8,128)(2,1)S(1)}, u32[]{:S(2)}, u32[]{:S(2)}) collective-permute-start(bf16[64,768]{1,0:T(8,128)(2,1)S(1)} %get-tuple-element.101), channel_id=1, source_target_pairs={{0,2},{1,3},{2,0},{3,1},{4,6},{5,7},{6,4},{7,5},{8,10},{9,11},{10,... | collective-permute-start | bytes 294920 | tf_op jit(solution)/shard_map/ppermute | solution.py:335
  6.0 6.7 %collective-permute-start.2 = (bf16[64,768]{1,0:T(8,128)(2,1)S(1)}, bf16[64,768]{1,0:T(8,128)(2,1)S(1)}, u32[]{:S(2)}, u32[]{:S(2)}) collective-permute-start(bf16[64,768]{1,0:T(8,128)(2,1)S(1)} %get-tuple-element.102), channel_id=1, source_target_pairs={{0,3},{1,2},{2,1},{3,0},{4,7},{5,6},{6,5},{7,4},{8,11},{9,10},{10,... | collective-permute-start | bytes 294920 | tf_op jit(solution)/shard_map/ppermute | solution.py:335
  11.6 2.4 %copy-start.28 = (bf16[512,768]{1,0:T(8,128)(2,1)S(1)}, bf16[512,768]{1,0:T(8,128)(2,1)}, u32[]{:S(2)}) copy-start(bf16[512,768]{1,0:T(8,128)(2,1)} %source.5) | copy-start | bytes 2359300
  12.7 8.9 %collective-permute-start.4 = (bf16[192,768]{1,0:T(8,128)(2,1)S(1)}, bf16[192,768]{1,0:T(8,128)(2,1)S(1)}, u32[]{:S(2)}, u32[]{:S(2)}) collective-permute-start(bf16[192,768]{1,0:T(8,128)(2,1)S(1)} %get-tuple-element.119), channel_id=1, source_target_pairs={{0,2},{1,3},{2,0},{3,1},{4,6},{5,7},{6,4},{7,5},{8,10},{9,11},{10,... | collective-permute-start | bytes 884744 | tf_op jit(solution)/shard_map/ppermute | solution.py:335
  12.7 4.2 %collective-permute-start = (bf16[64,768]{1,0:T(8,128)(2,1)S(1)}, bf16[64,768]{1,0:T(8,128)(2,1)S(1)}, u32[]{:S(2)}, u32[]{:S(2)}) collective-permute-start(bf16[64,768]{1,0:T(8,128)(2,1)S(1)} %get-tuple-element.100), channel_id=1, source_target_pairs={{0,1},{1,0},{2,3},{3,2},{4,5},{5,4},{6,7},{7,6},{8,9},{9,8},{10,11... | collective-permute-start | bytes 294920 | tf_op jit(solution)/shard_map/ppermute | solution.py:335
  16.9 11.1 %copy-start.34 = (bf16[192,768]{1,0:T(8,128)(2,1)S(1)}, bf16[192,768]{1,0:T(8,128)(2,1)}, u32[]{:S(2)}) copy-start(bf16[192,768]{1,0:T(8,128)(2,1)} %copy-done.33) | copy-start | bytes 884740
  16.9 12.7 %copy-start.32 = (bf16[192,768]{1,0:T(8,128)(2,1)S(1)}, bf16[192,768]{1,0:T(8,128)(2,1)}, u32[]{:S(2)}) copy-start(bf16[192,768]{1,0:T(8,128)(2,1)} %copy-done.31) | copy-start | bytes 884740
  21.6 11.2 %copy-start.5 = (bf16[192,768]{1,0:T(8,128)(2,1)}, bf16[192,768]{1,0:T(8,128)(2,1)S(1)}, u32[]{:S(2)}) copy-start(bf16[192,768]{1,0:T(8,128)(2,1)S(1)} %collective-permute-done.4.x2) | copy-start | bytes 884740
  21.6 21.8 %all-to-all-start = ((bf16[8,240,128]{2,1,0:T(8,128)(2,1)}), bf16[8,240,128]{2,1,0:T(8,128)(2,1)S(1)}, u32[]{:S(2)}, u32[]{:S(2)}) async-start(bf16[8,240,128]{2,1,0:T(8,128)(2,1)} %get-tuple-element.130), calls=%async_computation | async-start | bytes 983040 | tf_op jit(solution)/shard_map/all_to_all | solution.py:339
  28.1 4.7 %collective-permute-start.3 = (bf16[192,768]{1,0:T(8,128)(2,1)S(1)}, bf16[192,768]{1,0:T(8,128)(2,1)S(1)}, u32[]{:S(2)}, u32[]{:S(2)}) collective-permute-start(bf16[192,768]{1,0:T(8,128)(2,1)S(1)} %copy-done.34), channel_id=1, source_target_pairs={{0,1},{1,0},{2,3},{3,2},{4,5},{5,4},{6,7},{7,6},{8,9},{9,8},{10,11... | collective-permute-start | bytes 884744 | tf_op jit(solution)/shard_map/ppermute | solution.py:335
  29.7 9.6 %collective-permute-start.5 = (bf16[192,768]{1,0:T(8,128)(2,1)S(1)}, bf16[192,768]{1,0:T(8,128)(2,1)S(1)}, u32[]{:S(2)}, u32[]{:S(2)}) collective-permute-start(bf16[192,768]{1,0:T(8,128)(2,1)S(1)} %copy-done.32), channel_id=1, source_target_pairs={{0,3},{1,2},{2,1},{3,0},{4,7},{5,6},{6,5},{7,4},{8,11},{9,10},{10,... | collective-permute-start | bytes 884744 | tf_op jit(solution)/shard_map/ppermute | solution.py:335
  30.6 15.4 %collective-permute-start.6 = (bf16[256,768]{1,0:T(8,128)(2,1)}, bf16[256,768]{1,0:T(8,128)(2,1)}, u32[]{:S(2)}, u32[]{:S(2)}) collective-permute-start(bf16[256,768]{1,0:T(8,128)(2,1)} %get-tuple-element.125), channel_id=1, source_target_pairs={{0,1},{1,0},{2,3},{3,2},{4,5},{5,4},{6,7},{7,6},{8,9},{9,8},{10,11... | collective-permute-start | bytes 1179656 | tf_op jit(solution)/shard_map/ppermute | solution.py:335
  31.0 15.6 %collective-permute-start.7 = (bf16[256,768]{1,0:T(8,128)(2,1)}, bf16[256,768]{1,0:T(8,128)(2,1)}, u32[]{:S(2)}, u32[]{:S(2)}) collective-permute-start(bf16[256,768]{1,0:T(8,128)(2,1)} %get-tuple-element.126), channel_id=1, source_target_pairs={{0,2},{1,3},{2,0},{3,1},{4,6},{5,7},{6,4},{7,5},{8,10},{9,11},{10,... | collective-permute-start | bytes 1179656 | tf_op jit(solution)/shard_map/ppermute | solution.py:335
  31.6 23.8 %collective-permute-start.8 = (bf16[256,768]{1,0:T(8,128)(2,1)}, bf16[256,768]{1,0:T(8,128)(2,1)}, u32[]{:S(2)}, u32[]{:S(2)}) collective-permute-start(bf16[256,768]{1,0:T(8,128)(2,1)} %get-tuple-element.127), channel_id=1, source_target_pairs={{0,3},{1,2},{2,1},{3,0},{4,7},{5,6},{6,5},{7,4},{8,11},{9,10},{10,... | collective-permute-start | bytes 1179656 | tf_op jit(solution)/shard_map/ppermute | solution.py:335
  39.2 1.0 copy-start.6
  42.0 17.8 %copy-start.27 = (s32[3,12]{1,0:T(4,128)S(1)}, s32[3,12]{1,0:T(4,128)}, u32[]{:S(2)}) copy-start(s32[3,12]{1,0:T(4,128)} %offs.11) | copy-start | bytes 436
  42.1 17.1 %collective-permute-start.9 = (bf16[768,128]{1,0:T(8,128)(2,1)}, bf16[768,128]{1,0:T(8,128)(2,1)S(1)}, u32[]{:S(2)}, u32[]{:S(2)}) collective-permute-start(bf16[768,128]{1,0:T(8,128)(2,1)} %get-tuple-element.129.first_own), channel_id=1, source_target_pairs={{0,4},{4,0},{8,12},{12,8},{16,20},{20,16},{24,28},{28,24},{1,5},{5... | collective-permute-start | bytes 589832 | tf_op jit(solution)/shard_map/ppermute | solution.py:335
  43.4 16.4 %copy-start.36 = (bf16[768,128]{1,0:T(8,128)(2,1)S(1)}, bf16[768,128]{1,0:T(8,128)(2,1)}, u32[]{:S(2)}) copy-start(bf16[768,128]{1,0:T(8,128)(2,1)} %copy-done.35) | copy-start | bytes 589828
  43.5 16.4 %collective-permute-start.12 = (bf16[8,48,128]{2,1,0:T(8,128)(2,1)S(1)}, bf16[8,48,128]{2,1,0:T(8,128)(2,1)S(1)}, u32[]{:S(2)}, u32[]{:S(2)}) collective-permute-start(bf16[8,48,128]{2,1,0:T(8,128)(2,1)S(1)} %slice.4), channel_id=1, source_target_pairs={{0,96},{32,64},{64,32},{96,0},{1,97},{33,65},{65,33},{97,1},{2,98}... | collective-permute-start | bytes 294920 | tf_op jit(solution)/shard_map/ppermute | solution.py:335
  46.0 13.8 %collective-permute-start.11 = (bf16[8,48,128]{2,1,0:T(8,128)(2,1)S(1)}, bf16[8,48,128]{2,1,0:T(8,128)(2,1)S(1)}, u32[]{:S(2)}, u32[]{:S(2)}) collective-permute-start(bf16[8,48,128]{2,1,0:T(8,128)(2,1)S(1)} %slice.4), channel_id=1, source_target_pairs={{0,64},{32,96},{64,0},{96,32},{1,65},{33,97},{65,1},{97,33},{2,66}... | collective-permute-start | bytes 294920 | tf_op jit(solution)/shard_map/ppermute | solution.py:335
  46.7 13.2 %collective-permute-start.10 = (bf16[8,48,128]{2,1,0:T(8,128)(2,1)S(1)}, bf16[8,48,128]{2,1,0:T(8,128)(2,1)S(1)}, u32[]{:S(2)}, u32[]{:S(2)}) collective-permute-start(bf16[8,48,128]{2,1,0:T(8,128)(2,1)S(1)} %slice.4), channel_id=1, source_target_pairs={{0,32},{32,0},{64,96},{96,64},{1,33},{33,1},{65,97},{97,65},{2,34}... | collective-permute-start | bytes 294920 | tf_op jit(solution)/shard_map/ppermute | solution.py:335
  55.3 1.0 copy-start.4
  56.3 1.0 copy-start.7
  68.8 7.1 %copy-start.12 = (bf16[1008,128]{1,0:T(8,128)(2,1)}, bf16[1008,128]{1,0:T(8,128)(2,1)S(1)}, u32[]{:S(2)}) copy-start(bf16[1008,128]{1,0:T(8,128)(2,1)S(1)} %get-tuple-element.139.attended) | copy-start | bytes 774148
  68.8 7.1 %copy-start.14 = (bf16[768,128]{1,0:T(8,128)(2,1)}, bf16[768,128]{1,0:T(8,128)(2,1)S(1)}, u32[]{:S(2)}) copy-start(bf16[768,128]{1,0:T(8,128)(2,1)S(1)} %get-tuple-element.158.first_own) | copy-start | bytes 589828
  68.8 12.6 %collective-permute-start.16 = (bf16[768,128]{1,0:T(8,128)(2,1)S(1)}, bf16[768,128]{1,0:T(8,128)(2,1)S(1)}, u32[]{:S(2)}, u32[]{:S(2)}) collective-permute-start(bf16[768,128]{1,0:T(8,128)(2,1)S(1)} %get-tuple-element.138), channel_id=1, source_target_pairs={{0,4},{4,0},{8,12},{12,8},{16,20},{20,16},{24,28},{28,24},{1,5},{5... | collective-permute-start | bytes 589832 | tf_op jit(solution)/shard_map/ppermute | solution.py:335
  70.5 5.4 %collective-permute-start.13 = (bf16[8,48,128]{2,1,0:T(8,128)(2,1)S(1)}, bf16[8,48,128]{2,1,0:T(8,128)(2,1)S(1)}, u32[]{:S(2)}, u32[]{:S(2)}) collective-permute-start(bf16[8,48,128]{2,1,0:T(8,128)(2,1)S(1)} %get-tuple-element.135), channel_id=1, source_target_pairs={{0,32},{32,0},{64,96},{96,64},{1,33},{33,1},{65,97},{97,65},{2,34}... | collective-permute-start | bytes 294920 | tf_op jit(solution)/shard_map/ppermute | solution.py:335
  71.7 7.0 %collective-permute-start.14 = (bf16[8,48,128]{2,1,0:T(8,128)(2,1)S(1)}, bf16[8,48,128]{2,1,0:T(8,128)(2,1)S(1)}, u32[]{:S(2)}, u32[]{:S(2)}) collective-permute-start(bf16[8,48,128]{2,1,0:T(8,128)(2,1)S(1)} %get-tuple-element.136), channel_id=1, source_target_pairs={{0,64},{32,96},{64,0},{96,32},{1,65},{33,97},{65,1},{97,33},{2,66}... | collective-permute-start | bytes 294920 | tf_op jit(solution)/shard_map/ppermute | solution.py:335
  74.2 7.2 %collective-permute-start.15 = (bf16[8,48,128]{2,1,0:T(8,128)(2,1)S(1)}, bf16[8,48,128]{2,1,0:T(8,128)(2,1)S(1)}, u32[]{:S(2)}, u32[]{:S(2)}) collective-permute-start(bf16[8,48,128]{2,1,0:T(8,128)(2,1)S(1)} %get-tuple-element.137), channel_id=1, source_target_pairs={{0,96},{32,64},{64,32},{96,0},{1,97},{33,65},{65,33},{97,1},{2,98}... | collective-permute-start | bytes 294920 | tf_op jit(solution)/shard_map/ppermute | solution.py:335
  75.9 5.4 %copy-start.39 = (bf16[16,36,128]{2,1,0:T(8,128)(2,1)}, bf16[16,36,128]{2,1,0:T(8,128)(2,1)S(1)}, u32[]{:S(2)}) copy-start(bf16[16,36,128]{2,1,0:T(8,128)(2,1)S(1)} %get-tuple-element.153) | copy-start | bytes 442372
  75.9 5.4 %copy-start.40 = (bf16[16,36,128]{2,1,0:T(8,128)(2,1)}, bf16[16,36,128]{2,1,0:T(8,128)(2,1)S(1)}, u32[]{:S(2)}) copy-start(bf16[16,36,128]{2,1,0:T(8,128)(2,1)S(1)} %get-tuple-element.152) | copy-start | bytes 442372
  75.9 5.4 %copy-start.41 = (bf16[16,36,128]{2,1,0:T(8,128)(2,1)}, bf16[16,36,128]{2,1,0:T(8,128)(2,1)S(1)}, u32[]{:S(2)}) copy-start(bf16[16,36,128]{2,1,0:T(8,128)(2,1)S(1)} %get-tuple-element.151) | copy-start | bytes 442372
  76.0 6.3 %copy-start.18 = (bf16[16,36,128]{2,1,0:T(8,128)(2,1)}, bf16[16,36,128]{2,1,0:T(8,128)(2,1)S(1)}, u32[]{:S(2)}) copy-start(bf16[16,36,128]{2,1,0:T(8,128)(2,1)S(1)} %get-tuple-element.154.refs_0_) | copy-start | bytes 442372
  82.2 24.3 %all-to-all-start.1 = ((bf16[8,240,128]{2,1,0:T(8,128)(2,1)}), bf16[8,240,128]{2,1,0:T(8,128)(2,1)S(1)}, u32[]{:S(2)}, u32[]{:S(2)}) async-start(bf16[8,240,128]{2,1,0:T(8,128)(2,1)} %shard_map.127), calls=%async_computation.1 | async-start | bytes 983040 | tf_op jit(solution)/shard_map/all_to_all | solution.py:339
  87.7 1.0 copy-start.8
  88.7 0.9 copy-start.13
  92.1 22.0 %collective-permute-start.23 = (bf16[256,768]{1,0:T(8,128)(2,1)}, bf16[256,768]{1,0:T(8,128)(2,1)}, u32[]{:S(2)}, u32[]{:S(2)}) collective-permute-start(bf16[256,768]{1,0:T(8,128)(2,1)} %get-tuple-element.166), channel_id=1, source_target_pairs={{0,1},{1,0},{2,3},{3,2},{4,5},{5,4},{6,7},{7,6},{8,9},{9,8},{10,11... | collective-permute-start | bytes 1179656 | tf_op jit(solution)/shard_map/ppermute | solution.py:335
  93.0 6.1 %collective-permute-start.17 = (bf16[16,36,128]{2,1,0:T(8,128)(2,1)}, bf16[16,36,128]{2,1,0:T(8,128)(2,1)S(1)}, u32[]{:S(2)}, u32[]{:S(2)}) collective-permute-start(bf16[16,36,128]{2,1,0:T(8,128)(2,1)} %copy-done.41), channel_id=1, source_target_pairs={{0,32},{32,0},{64,96},{96,64},{1,33},{33,1},{65,97},{97,65},{2,34}... | collective-permute-start | bytes 442376 | tf_op jit(solution)/shard_map/ppermute | solution.py:335
  93.0 21.8 %collective-permute-start.24 = (bf16[256,768]{1,0:T(8,128)(2,1)}, bf16[256,768]{1,0:T(8,128)(2,1)}, u32[]{:S(2)}, u32[]{:S(2)}) collective-permute-start(bf16[256,768]{1,0:T(8,128)(2,1)} %get-tuple-element.167), channel_id=1, source_target_pairs={{0,2},{1,3},{2,0},{3,1},{4,6},{5,7},{6,4},{7,5},{8,10},{9,11},{10,... | collective-permute-start | bytes 1179656 | tf_op jit(solution)/shard_map/ppermute | solution.py:335
  94.0 20.8 %collective-permute-start.25 = (bf16[256,768]{1,0:T(8,128)(2,1)}, bf16[256,768]{1,0:T(8,128)(2,1)}, u32[]{:S(2)}, u32[]{:S(2)}) collective-permute-start(bf16[256,768]{1,0:T(8,128)(2,1)} %get-tuple-element.168), channel_id=1, source_target_pairs={{0,3},{1,2},{2,1},{3,0},{4,7},{5,6},{6,5},{7,4},{8,11},{9,10},{10,... | collective-permute-start | bytes 1179656 | tf_op jit(solution)/shard_map/ppermute | solution.py:335
  94.6 8.0 %collective-permute-start.18 = (bf16[16,36,128]{2,1,0:T(8,128)(2,1)}, bf16[16,36,128]{2,1,0:T(8,128)(2,1)S(1)}, u32[]{:S(2)}, u32[]{:S(2)}) collective-permute-start(bf16[16,36,128]{2,1,0:T(8,128)(2,1)} %copy-done.40), channel_id=1, source_target_pairs={{0,64},{32,96},{64,0},{96,32},{1,65},{33,97},{65,1},{97,33},{2,66}... | collective-permute-start | bytes 442376 | tf_op jit(solution)/shard_map/ppermute | solution.py:335
  99.8 6.1 %collective-permute-start.19 = (bf16[16,36,128]{2,1,0:T(8,128)(2,1)}, bf16[16,36,128]{2,1,0:T(8,128)(2,1)S(1)}, u32[]{:S(2)}, u32[]{:S(2)}) collective-permute-start(bf16[16,36,128]{2,1,0:T(8,128)(2,1)} %copy-done.39), channel_id=1, source_target_pairs={{0,96},{32,64},{64,32},{96,0},{1,97},{33,65},{65,33},{97,1},{2,98}... | collective-permute-start | bytes 442376 | tf_op jit(solution)/shard_map/ppermute | solution.py:335
  108.4 15.2 %copy-start.19 = (bf16[16,36,128]{2,1,0:T(8,128)(2,1)S(1)}, bf16[16,36,128]{2,1,0:T(8,128)(2,1)}, u32[]{:S(2)}) copy-start(bf16[16,36,128]{2,1,0:T(8,128)(2,1)} %copy-done.18) | copy-start | bytes 442372
  108.4 15.2 %copy-start.21 = (bf16[16,36,128]{2,1,0:T(8,128)(2,1)S(1)}, bf16[16,36,128]{2,1,0:T(8,128)(2,1)}, u32[]{:S(2)}) copy-start(bf16[16,36,128]{2,1,0:T(8,128)(2,1)} %copy-done.20) | copy-start | bytes 442372
  108.4 15.2 %copy-start.23 = (bf16[16,36,128]{2,1,0:T(8,128)(2,1)S(1)}, bf16[16,36,128]{2,1,0:T(8,128)(2,1)}, u32[]{:S(2)}) copy-start(bf16[16,36,128]{2,1,0:T(8,128)(2,1)} %copy-done.22) | copy-start | bytes 442372
  108.4 15.2 %copy-start.25 = (bf16[16,36,128]{2,1,0:T(8,128)(2,1)S(1)}, bf16[16,36,128]{2,1,0:T(8,128)(2,1)}, u32[]{:S(2)}) copy-start(bf16[16,36,128]{2,1,0:T(8,128)(2,1)} %copy-done.24) | copy-start | bytes 442372
  110.4 23.5 %copy-start.2 = (bf16[1008,256]{1,0:T(8,128)(2,1)S(1)}, bf16[1008,256]{1,0:T(8,128)(2,1)}, u32[]{:S(2)}) copy-start(bf16[1008,256]{1,0:T(8,128)(2,1)} %copy-done.1) | copy-start | bytes 1548292
  110.4 5.2 %collective-permute-start.20 = (bf16[16,36,128]{2,1,0:T(8,128)(2,1)S(1)}, bf16[16,36,128]{2,1,0:T(8,128)(2,1)S(1)}, u32[]{:S(2)}, u32[]{:S(2)}) collective-permute-start(bf16[16,36,128]{2,1,0:T(8,128)(2,1)S(1)} %get-tuple-element.162), channel_id=1, source_target_pairs={{0,32},{32,0},{64,96},{96,64},{1,33},{33,1},{65,97},{97,65},{2,34}... | collective-permute-start | bytes 442376 | tf_op jit(solution)/shard_map/ppermute | solution.py:335
  112.4 8.4 %collective-permute-start.21 = (bf16[16,36,128]{2,1,0:T(8,128)(2,1)S(1)}, bf16[16,36,128]{2,1,0:T(8,128)(2,1)S(1)}, u32[]{:S(2)}, u32[]{:S(2)}) collective-permute-start(bf16[16,36,128]{2,1,0:T(8,128)(2,1)S(1)} %get-tuple-element.163), channel_id=1, source_target_pairs={{0,64},{32,96},{64,0},{96,32},{1,65},{33,97},{65,1},{97,33},{2,66}... | collective-permute-start | bytes 442376 | tf_op jit(solution)/shard_map/ppermute | solution.py:335
  114.0 9.6 %collective-permute-start.22 = (bf16[16,36,128]{2,1,0:T(8,128)(2,1)S(1)}, bf16[16,36,128]{2,1,0:T(8,128)(2,1)S(1)}, u32[]{:S(2)}, u32[]{:S(2)}) collective-permute-start(bf16[16,36,128]{2,1,0:T(8,128)(2,1)S(1)} %get-tuple-element.164), channel_id=1, source_target_pairs={{0,96},{32,64},{64,32},{96,0},{1,97},{33,65},{65,33},{97,1},{2,98}... | collective-permute-start | bytes 442376 | tf_op jit(solution)/shard_map/ppermute | solution.py:335
  124.5 18.9 %all-to-all-start.2 = ((bf16[16,72,128]{2,1,0:T(8,128)(2,1)}), bf16[16,72,128]{2,1,0:T(8,128)(2,1)S(1)}, u32[]{:S(2)}, u32[]{:S(2)}) async-start(bf16[16,72,128]{2,1,0:T(8,128)(2,1)} %shard_map.130), calls=%async_computation.2 | async-start | bytes 589824 | tf_op jit(solution)/shard_map/all_to_all | solution.py:339
  134.0 1.5 copy-start.45
  138.5 12.1 %copy-start.30 = (bf16[256,768]{1,0:T(8,128)(2,1)S(1)}, bf16[256,768]{1,0:T(8,128)(2,1)}, u32[]{:S(2)}) copy-start(bf16[256,768]{1,0:T(8,128)(2,1)} %copy-done.29) | copy-start | bytes 1179652
  144.3 15.8 %all-to-all-start.3 = ((bf16[16,72,128]{2,1,0:T(8,128)(2,1)}), bf16[16,72,128]{2,1,0:T(8,128)(2,1)S(1)}, u32[]{:S(2)}, u32[]{:S(2)}) async-start(bf16[16,72,128]{2,1,0:T(8,128)(2,1)} %shard_map.131), calls=%async_computation.3 | async-start | bytes 589824 | tf_op jit(solution)/shard_map/all_to_all | solution.py:339
  150.7 9.8 %collective-permute-start.26 = (bf16[256,768]{1,0:T(8,128)(2,1)S(1)}, bf16[256,768]{1,0:T(8,128)(2,1)S(1)}, u32[]{:S(2)}, u32[]{:S(2)}) collective-permute-start(bf16[256,768]{1,0:T(8,128)(2,1)S(1)} %copy-done.30), channel_id=1, source_target_pairs={{0,1},{1,0},{2,3},{3,2},{4,5},{5,4},{6,7},{7,6},{8,9},{9,8},{10,11... | collective-permute-start | bytes 1179656 | tf_op jit(solution)/shard_map/ppermute | solution.py:335
  152.6 13.2 %collective-permute-start.27 = (bf16[256,768]{1,0:T(8,128)(2,1)S(1)}, bf16[256,768]{1,0:T(8,128)(2,1)S(1)}, u32[]{:S(2)}, u32[]{:S(2)}) collective-permute-start(bf16[256,768]{1,0:T(8,128)(2,1)S(1)} %get-tuple-element.185), channel_id=1, source_target_pairs={{0,2},{1,3},{2,0},{3,1},{4,6},{5,7},{6,4},{7,5},{8,10},{9,11},{10,... | collective-permute-start | bytes 1179656 | tf_op jit(solution)/shard_map/ppermute | solution.py:335
  153.0 21.6 %collective-permute-start.28 = (bf16[256,768]{1,0:T(8,128)(2,1)S(1)}, bf16[256,768]{1,0:T(8,128)(2,1)S(1)}, u32[]{:S(2)}, u32[]{:S(2)}) collective-permute-start(bf16[256,768]{1,0:T(8,128)(2,1)S(1)} %get-tuple-element.186), channel_id=1, source_target_pairs={{0,3},{1,2},{2,1},{3,0},{4,7},{5,6},{6,5},{7,4},{8,11},{9,10},{10,... | collective-permute-start | bytes 1179656 | tf_op jit(solution)/shard_map/ppermute | solution.py:335
  160.1 17.0 %collective-permute-start.31 = (bf16[16,72,128]{2,1,0:T(8,128)(2,1)S(1)}, bf16[16,72,128]{2,1,0:T(8,128)(2,1)S(1)}, u32[]{:S(2)}, u32[]{:S(2)}) collective-permute-start(bf16[16,72,128]{2,1,0:T(8,128)(2,1)S(1)} %all-to-all-done.3.b0), channel_id=1, source_target_pairs={{0,96},{32,64},{64,32},{96,0},{1,97},{33,65},{65,33},{97,1},{2,98}... | collective-permute-start | bytes 884744 | tf_op jit(solution)/shard_map/ppermute | solution.py:335
  160.1 17.0 %collective-permute-start.30 = (bf16[16,72,128]{2,1,0:T(8,128)(2,1)S(1)}, bf16[16,72,128]{2,1,0:T(8,128)(2,1)S(1)}, u32[]{:S(2)}, u32[]{:S(2)}) collective-permute-start(bf16[16,72,128]{2,1,0:T(8,128)(2,1)S(1)} %all-to-all-done.3.b0), channel_id=1, source_target_pairs={{0,64},{32,96},{64,0},{96,32},{1,65},{33,97},{65,1},{97,33},{2,66}... | collective-permute-start | bytes 884744 | tf_op jit(solution)/shard_map/ppermute | solution.py:335
  160.5 16.5 %collective-permute-start.29 = (bf16[16,72,128]{2,1,0:T(8,128)(2,1)S(1)}, bf16[16,72,128]{2,1,0:T(8,128)(2,1)S(1)}, u32[]{:S(2)}, u32[]{:S(2)}) collective-permute-start(bf16[16,72,128]{2,1,0:T(8,128)(2,1)S(1)} %all-to-all-done.3.b0), channel_id=1, source_target_pairs={{0,32},{32,0},{64,96},{96,64},{1,33},{33,1},{65,97},{97,65},{2,34}... | collective-permute-start | bytes 884744 | tf_op jit(solution)/shard_map/ppermute | solution.py:335
  (18 other events, 13.6 us)

commit v5 on v3

--- a/solution.py
+++ b/solution.py
@@ -230,8 +230,8 @@
 
 
 def put_chunks(place, held, chunks, sends):
-    for c in range(64):
-        chunks[c // 16, c % 16] = held[36 * c : 36 * c + 36].astype(BF)
+    for c in range(4):
+        chunks[c] = held[576 * c : 576 * c + 576].astype(BF)
     for k in range(4):
         sends[k][...] = chunks[place[1] ^ k]
 
@@ -294,10 +294,12 @@
 
 
 def x_sum_kernel(*refs):
-    out, held = refs[8], refs[9]
+    out, total, held = refs[8:]
+    for half in range(2):
+        total[half] = total_of([part[...] for part in refs[4 * half : 4 * half + 4]], 4)
     for y in range(16):
         for half in range(2):
-            held[36 * half : 36 * half + 36] = total_of([part[y] for part in refs[4 * half : 4 * half + 4]], 4)
+            held[36 * half : 36 * half + 36] = total[half, 36 * y : 36 * y + 36]
         out[y] = held[...].astype(BF)
 
 
@@ -362,8 +364,8 @@
     token_first, grad_rows = to_heads(token_first), to_heads(grad_rows)
     token_rest, token_first[0], grad_rows[0], joined = tie((token_rest, token_first[0], grad_rows[0], joined))
 
-    half_chunks, full_chunks = ((16, 36, 128), BF), ((16, 72, 128), BF)
-    halves = [((2304, 128), F32), ((4, 16, 36, 128), BF)]
+    half_chunks, full_chunks = ((576, 128), BF), ((16, 72, 128), BF)
+    halves = [((2304, 128), F32), ((4, 576, 128), BF)]
     wide, half, short = ((3 * PER_HEAD, 128), BF), ((768, 128), BF), ((240, 128), BF)
     rest_shape, second_shape, third_shape = ((8, 240, 128), BF), ((8, 192, 128), BF), ((8, 48, 128), BF)
     whole_first, whole_rest = ((768, WIDTH), BF), ((240, WIDTH), BF)
@@ -415,8 +417,8 @@
     late = [late[0]] + [swap(late[k], "x", k) for k in (1, 2, 3)]
     change_slots = call(input_kernel, [slot] * 4, flops=2 * 1008 * 768 * 256)(changes, joined)
     spread = call(spread_kernel, [((ROWS, WIDTH), BF)], smem=2, flops=2 * 1024 * 512 * 768)
-    late, mixed_slots = tie((late, mixed_slots))
-    (parts,) = call(x_sum_kernel, [full_chunks], scratch=[((72, 128), F32)])(*early, *late)
+    late, mixed_slots, change_slots = tie((late, mixed_slots, change_slots))
+    (parts,) = call(x_sum_kernel, [full_chunks], scratch=[((2, 576, 128), F32), ((72, 128), F32)])(*early, *late)
     (part,) = call(yz_sum_kernel, [full_chunks])(deal(parts, YZ_AXES))
     (mixed,) = spread(offsets, where, *mixed_slots)
     part, mixed, change_slots = tie((part, mixed, change_slots))

time: 176 us -> 174 us (0.989)
    all_to_all x4, waiting for transfers between devices: 13.4 us -> 16 us  [deal(): return lax.all_to_all(value, axis, 0, 0, tiled=True)]
    unnamed x94 -> x86, local copies, waits for them, and re-layouts: 20.2 us -> 18.6 us
where the time goes in v5:
time: 174 us; the launch traced here: 173 us
  starting transfers between devices  64.9 us (37%)
  waiting for transfers between devices  57.9 us (33%)
  Pallas kernels  30.9 us (18%)
  local copies, waits for them, and re-layouts  18.6 us (11%)
    ppermute x32, waiting for transfers between devices, swap(): return lax.ppermute(value, axis, [(i, i ^ k) for i in range(count)])  41.9 us
    ppermute x32, starting transfers between devices, swap(): return lax.ppermute(value, axis, [(i, i ^ k) for i in range(count)])  39.1 us
    pallas_call x18, Pallas kernels, run(): pl.pallas_call(body, out_shape=tuple((jax.ShapeDtypeStruct(shape, kind) f...  30.9 us
    all_to_all x4, starting transfers between devices, deal(): return lax.all_to_all(value, axis, 0, 0, tiled=True)  25.9 us
    unnamed x86, local copies, waits for them, and re-layouts  18.6 us
    all_to_all x4, waiting for transfers between devices, deal(): return lax.all_to_all(value, axis, 0, 0, tiled=True)  16 us
  transfers between devices with their start and end apart: 36, of which 17 were waited for; matrix products, arithmetic and copies ran while one was open for 0% of the time, Pallas kernels for 10%

profile of v5, /device:TPU:1, one launch (start us, length us, event | category | flops | bytes accessed | tf_op | source)
XLA Modules:
  0.0 173.5 jit_solution(4691046956662798134)
XLA Ops:
  0.7 1.1 copy-done
  2.5 1.2 shard_map.118
  3.8 2.2 %collective-permute-start.1 = (bf16[64,768]{1,0:T(8,128)(2,1)S(1)}, bf16[64,768]{1,0:T(8,128)(2,1)S(1)}, u32[]{:S(2)}, u32[]{:S(2)}) collective-permute-start(bf16[64,768]{1,0:T(8,128)(2,1)S(1)} %get-tuple-element.106), channel_id=1, source_target_pairs={{0,2},{1,3},{2,0},{3,1},{4,6},{5,7},{6,4},{7,5},{8,10},{9,11},{10,... | collective-permute-start | bytes 294920 | tf_op jit(solution)/shard_map/ppermute | solution.py:337
  6.0 2.7 %collective-permute-start.2 = (bf16[64,768]{1,0:T(8,128)(2,1)S(1)}, bf16[64,768]{1,0:T(8,128)(2,1)S(1)}, u32[]{:S(2)}, u32[]{:S(2)}) collective-permute-start(bf16[64,768]{1,0:T(8,128)(2,1)S(1)} %get-tuple-element.107), channel_id=1, source_target_pairs={{0,3},{1,2},{2,1},{3,0},{4,7},{5,6},{6,5},{7,4},{8,11},{9,10},{10,... | collective-permute-start | bytes 294920 | tf_op jit(solution)/shard_map/ppermute | solution.py:337
  8.8 1.4 shard_map.119
  11.6 1.1 collective-permute-done.2.x3
  12.7 1.1 collective-permute-start
  14.0 2.2 %shard_map.120 = (bf16[256,768]{1,0:T(8,128)(2,1)S(1)}, bf16[256,768]{1,0:T(8,128)(2,1)}, bf16[256,768]{1,0:T(8,128)(2,1)}, bf16[256,768]{1,0:T(8,128)(2,1)}) custom-call(s32[3,12]{1,0:T(4,128)S(1)} %copy-done.22, s32[2]{0:T(128)S(1)} %pad_add_fusion.where.place, bf16[512,768]{1,0:T(8,128)(2,1)S(1)} %copy-done.24), custom_call_target="tpu_custom_call" | custom-call | flops 805306368 | bytes 4194304 | tf_op jit(solution)/shard_map/pallas_call | solution.py:77
  16.9 1.3 shard_map.122
  18.8 2.8 %collective-permute-done.4.x2 = bf16[192,768]{1,0:T(8,128)(2,1)S(1)} collective-permute-done((bf16[192,768]{1,0:T(8,128)(2,1)S(1)}, bf16[192,768]{1,0:T(8,128)(2,1)S(1)}, u32[]{:S(2)}, u32[]{:S(2)}) %collective-permute-start.4) | collective-permute-done | bytes 294944 | tf_op jit(solution)/shard_map/ppermute | solution.py:337
  21.6 6.4 %all-to-all-start = ((bf16[8,240,128]{2,1,0:T(8,128)(2,1)}), bf16[8,240,128]{2,1,0:T(8,128)(2,1)S(1)}, u32[]{:S(2)}, u32[]{:S(2)}) async-start(bf16[8,240,128]{2,1,0:T(8,128)(2,1)} %get-tuple-element.135), calls=%async_computation | async-start | bytes 983040 | tf_op jit(solution)/shard_map/all_to_all | solution.py:341
  28.1 1.6 collective-permute-start.3
  29.7 1.0 collective-permute-start.5
  31.6 1.2 collective-permute-start.8
  32.8 6.5 %collective-permute-done.5.x3 = bf16[192,768]{1,0:T(8,128)(2,1)S(1)} collective-permute-done((bf16[192,768]{1,0:T(8,128)(2,1)S(1)}, bf16[192,768]{1,0:T(8,128)(2,1)S(1)}, u32[]{:S(2)}, u32[]{:S(2)}) %collective-permute-start.5) | collective-permute-done | bytes 294944 | tf_op jit(solution)/shard_map/ppermute | solution.py:337
  39.2 1.0 copy-done.4
  40.2 1.2 shard_map.123
  42.1 1.3 collective-permute-start.9
  43.5 2.6 %collective-permute-start.12 = (bf16[8,48,128]{2,1,0:T(8,128)(2,1)S(1)}, bf16[8,48,128]{2,1,0:T(8,128)(2,1)S(1)}, u32[]{:S(2)}, u32[]{:S(2)}) collective-permute-start(bf16[8,48,128]{2,1,0:T(8,128)(2,1)S(1)} %slice.4), channel_id=1, source_target_pairs={{0,96},{32,64},{64,32},{96,0},{1,97},{33,65},{65,33},{97,1},{2,98}... | collective-permute-start | bytes 294920 | tf_op jit(solution)/shard_map/ppermute | solution.py:337
  46.7 1.2 collective-permute-start.10
  47.9 7.5 %collective-permute-done.8.c3 = bf16[256,768]{1,0:T(8,128)(2,1)} collective-permute-done((bf16[256,768]{1,0:T(8,128)(2,1)}, bf16[256,768]{1,0:T(8,128)(2,1)}, u32[]{:S(2)}, u32[]{:S(2)}) %collective-permute-start.8) | collective-permute-done | bytes 393248 | tf_op jit(solution)/shard_map/ppermute | solution.py:337
  55.3 1.0 copy-done.2
  56.3 1.0 copy-done.5
  57.3 1.8 %shard_map.124 = (bf16[768,768]{1,0:T(8,128)(2,1)S(1)}, bf16[240,768]{1,0:T(8,128)(2,1)S(1)}, bf16[1008,128]{1,0:T(8,128)(2,1)S(1)}) custom-call(bf16[256,768]{1,0:T(8,128)(2,1)S(1)} %copy-done.2, bf16[256,768]{1,0:T(8,128)(2,1)} %collective-permute-done.6.c1, bf16[256,768]{1,0:T(8,128)(2,1)} %collective-permute-done.7.c2, ...), custom_call_target="tpu_custom_call" | custom-call | flops 198180864 | bytes 4194304 | tf_op jit(solution)/shard_map/pallas_call | solution.py:77
  59.9 0.9 copy-done.35
  60.8 0.8 copy-done.40
  61.6 7.2 %shard_map.125 = (bf16[1008,128]{1,0:T(8,128)(2,1)S(1)}, bf16[1008,128]{1,0:T(8,128)(2,1)S(1)}, bf16[768,128]{1,0:T(8,128)(2,1)S(1)}, bf16[768,128]{1,0:T(8,128)...) custom-call(s32[3,12]{1,0:T(4,128)S(1)} %copy-done.23, ...), custom_call_target="tpu_custom_call" | custom-call | flops 924844032 | bytes 4194304 | tf_op jit(solution)/shard_map/pallas_call | solution.py:77
  69.5 1.7 collective-permute-start.16
  71.1 1.2 collective-permute-start.13
  72.3 2.5 %collective-permute-start.14 = (bf16[8,48,128]{2,1,0:T(8,128)(2,1)S(1)}, bf16[8,48,128]{2,1,0:T(8,128)(2,1)S(1)}, u32[]{:S(2)}, u32[]{:S(2)}) collective-permute-start(bf16[8,48,128]{2,1,0:T(8,128)(2,1)S(1)} %get-tuple-element.141), channel_id=1, source_target_pairs={{0,64},{32,96},{64,0},{96,32},{1,65},{33,97},{65,1},{97,33},{2,66}... | collective-permute-start | bytes 294920 | tf_op jit(solution)/shard_map/ppermute | solution.py:337
  76.5 1.4 shard_map.127
  79.9 2.1 %collective-permute-done.15.t3 = bf16[8,48,128]{2,1,0:T(8,128)(2,1)S(1)} collective-permute-done((bf16[8,48,128]{2,1,0:T(8,128)(2,1)S(1)}, bf16[8,48,128]{2,1,0:T(8,128)(2,1)S(1)}, u32[]{:S(2)}, u32[]{:S(2)}) %collective-permute-start.15) | collective-permute-done | bytes 98336 | tf_op jit(solution)/shard_map/ppermute | solution.py:337
  82.7 0.8 shard_map.128
  83.5 5.5 %all-to-all-start.1 = ((bf16[8,240,128]{2,1,0:T(8,128)(2,1)}), bf16[8,240,128]{2,1,0:T(8,128)(2,1)S(1)}, u32[]{:S(2)}, u32[]{:S(2)}) async-start(bf16[8,240,128]{2,1,0:T(8,128)(2,1)} %shard_map.128), calls=%async_computation.1 | async-start | bytes 983040 | tf_op jit(solution)/shard_map/all_to_all | solution.py:341
  89.0 0.9 collective-permute-start.23
  89.9 1.0 collective-permute-start.24
  90.9 0.9 collective-permute-start.25
  91.7 2.4 %collective-permute-start.18 = (bf16[576,128]{1,0:T(8,128)(2,1)}, bf16[576,128]{1,0:T(8,128)(2,1)S(1)}, u32[]{:S(2)}, u32[]{:S(2)}) collective-permute-start(bf16[576,128]{1,0:T(8,128)(2,1)} %copy-done.37), channel_id=1, source_target_pairs={{0,64},{32,96},{64,0},{96,32},{1,65},{33,97},{65,1},{97,33},{2,66}... | collective-permute-start | bytes 442376 | tf_op jit(solution)/shard_map/ppermute | solution.py:337
  94.2 1.5 collective-permute-done.17.refs_1_
  96.3 1.1 collective-permute-start.19
  97.4 2.1 %collective-permute-done.18.refs_2_ = bf16[576,128]{1,0:T(8,128)(2,1)S(1)} collective-permute-done((bf16[576,128]{1,0:T(8,128)(2,1)}, bf16[576,128]{1,0:T(8,128)(2,1)S(1)}, u32[]{:S(2)}, u32[]{:S(2)}) %collective-permute-start.18) | collective-permute-done | bytes 147488 | tf_op jit(solution)/shard_map/ppermute | solution.py:337
  100.1 1.6 collective-permute-done.19.refs_3_
  102.4 3.9 %all-to-all-done.1.rests = bf16[8,240,128]{2,1,0:T(8,128)(2,1)S(1)} async-done(((bf16[8,240,128]{2,1,0:T(8,128)(2,1)}), bf16[8,240,128]{2,1,0:T(8,128)(2,1)S(1)}, u32[]{:S(2)}, u32[]{:S(2)}) %all-to-all-start.1) | async-done | bytes 491552 | tf_op jit(solution)/shard_map/all_to_all | solution.py:341
  106.2 0.9 copy-done.11
  107.2 0.9 copy-done.13
  108.1 1.1 shard_map.129
  109.5 3.7 %collective-permute-start.22 = (bf16[576,128]{1,0:T(8,128)(2,1)S(1)}, bf16[576,128]{1,0:T(8,128)(2,1)S(1)}, u32[]{:S(2)}, u32[]{:S(2)}) collective-permute-start(bf16[576,128]{1,0:T(8,128)(2,1)S(1)} %get-tuple-element.170), channel_id=1, source_target_pairs={{0,96},{32,64},{64,32},{96,0},{1,97},{33,65},{65,33},{97,1},{2,98}... | collective-permute-start | bytes 442376 | tf_op jit(solution)/shard_map/ppermute | solution.py:337
  114.3 2.5 %collective-permute-done.21.refs_6_ = bf16[576,128]{1,0:T(8,128)(2,1)S(1)} collective-permute-done((bf16[576,128]{1,0:T(8,128)(2,1)S(1)}, bf16[576,128]{1,0:T(8,128)(2,1)S(1)}, u32[]{:S(2)}, u32[]{:S(2)}) %collective-permute-start.21) | collective-permute-done | bytes 147488 | tf_op jit(solution)/shard_map/ppermute | solution.py:337
  116.7 2.7 %collective-permute-done.22.refs_7_ = bf16[576,128]{1,0:T(8,128)(2,1)S(1)} collective-permute-done((bf16[576,128]{1,0:T(8,128)(2,1)S(1)}, bf16[576,128]{1,0:T(8,128)(2,1)S(1)}, u32[]{:S(2)}, u32[]{:S(2)}) %collective-permute-start.22) | collective-permute-done | bytes 147488 | tf_op jit(solution)/shard_map/ppermute | solution.py:337
  119.4 1.0 shard_map.131
  120.5 7.4 %all-to-all-start.2 = ((bf16[16,72,128]{2,1,0:T(8,128)(2,1)}), bf16[16,72,128]{2,1,0:T(8,128)(2,1)S(1)}, u32[]{:S(2)}, u32[]{:S(2)}) async-start(bf16[16,72,128]{2,1,0:T(8,128)(2,1)} %shard_map.131), calls=%async_computation.2 | async-start | bytes 589824 | tf_op jit(solution)/shard_map/all_to_all | solution.py:341
  127.9 3.1 %shard_map.133 = bf16[512,768]{1,0:T(8,128)(2,1)} custom-call(s32[3,12]{1,0:T(4,128)S(1)} %copy-done.23, s32[2]{0:T(128)S(1)} %pad_add_fusion.where.place, bf16[256,768]{1,0:T(8,128)(2,1)S(1)} %copy-done.42, bf16[256,768]{1,0:T(8,128)(2,1)} %collective-permute-done.23.s1, bf16[256,768]{1,0:T(8,128)(2,1)} %collective-permute-done.24.s2, ...), custom_call_target="tpu_custom_call" | custom-call | flops 805306368 | bytes 4194304 | tf_op jit(solution)/shard_map/pallas_call | solution.py:77
  131.0 6.3 %all-to-all-done.2.got = bf16[16,72,128]{2,1,0:T(8,128)(2,1)S(1)} async-done(((bf16[16,72,128]{2,1,0:T(8,128)(2,1)}), bf16[16,72,128]{2,1,0:T(8,128)(2,1)S(1)}, u32[]{:S(2)}, u32[]{:S(2)}) %all-to-all-start.2) | async-done | bytes 294944 | tf_op jit(solution)/shard_map/all_to_all | solution.py:341
  137.3 0.8 shard_map.132
  138.1 6.6 %all-to-all-start.3 = ((bf16[16,72,128]{2,1,0:T(8,128)(2,1)}), bf16[16,72,128]{2,1,0:T(8,128)(2,1)S(1)}, u32[]{:S(2)}, u32[]{:S(2)}) async-start(bf16[16,72,128]{2,1,0:T(8,128)(2,1)} %shard_map.132), calls=%async_computation.3 | async-start | bytes 589824 | tf_op jit(solution)/shard_map/all_to_all | solution.py:341
  144.7 1.9 %collective-permute-start.26 = (bf16[256,768]{1,0:T(8,128)(2,1)S(1)}, bf16[256,768]{1,0:T(8,128)(2,1)S(1)}, u32[]{:S(2)}, u32[]{:S(2)}) collective-permute-start(bf16[256,768]{1,0:T(8,128)(2,1)S(1)} %get-tuple-element.194), channel_id=1, source_target_pairs={{0,1},{1,0},{2,3},{3,2},{4,5},{5,4},{6,7},{7,6},{8,9},{9,8},{10,11... | collective-permute-start | bytes 1179656 | tf_op jit(solution)/shard_map/ppermute | solution.py:337
  147.0 1.3 collective-permute-start.28
  148.3 5.8 %all-to-all-done.3.b0 = bf16[16,72,128]{2,1,0:T(8,128)(2,1)S(1)} async-done(((bf16[16,72,128]{2,1,0:T(8,128)(2,1)}), bf16[16,72,128]{2,1,0:T(8,128)(2,1)S(1)}, u32[]{:S(2)}, u32[]{:S(2)}) %all-to-all-start.3) | async-done | bytes 294944 | tf_op jit(solution)/shard_map/all_to_all | solution.py:341
  154.8 1.0 collective-permute-start.30
  155.8 1.6 collective-permute-start.29
  157.4 2.4 %collective-permute-done.27.s2 = bf16[256,768]{1,0:T(8,128)(2,1)S(1)} collective-permute-done((bf16[256,768]{1,0:T(8,128)(2,1)S(1)}, bf16[256,768]{1,0:T(8,128)(2,1)S(1)}, u32[]{:S(2)}, u32[]{:S(2)}) %collective-permute-start.27) | collective-permute-done | bytes 393248 | tf_op jit(solution)/shard_map/ppermute | solution.py:337
  159.8 8.7 %collective-permute-done.28.s3 = bf16[256,768]{1,0:T(8,128)(2,1)S(1)} collective-permute-done((bf16[256,768]{1,0:T(8,128)(2,1)S(1)}, bf16[256,768]{1,0:T(8,128)(2,1)S(1)}, u32[]{:S(2)}, u32[]{:S(2)}) %collective-permute-start.28) | collective-permute-done | bytes 393248 | tf_op jit(solution)/shard_map/ppermute | solution.py:337
  168.6 2.4 %shard_map.134 = bf16[512,768]{1,0:T(8,128)(2,1)} custom-call(s32[3,12]{1,0:T(4,128)S(1)} %copy-done.23, s32[2]{0:T(128)S(1)} %pad_add_fusion.where.place, bf16[256,768]{1,0:T(8,128)(2,1)S(1)} %get-tuple-element.193.s0, bf16[256,768]{1,0:T(8,128)(2,1)S(1)} %collective-permute-done.26.s1, bf16[256,768]{1,0:T(8,128)(2,1)S(1)} %collective-permute-done.27.s2, ...), custom_call_target="tpu_custom_call" | custom-call | flops 805306368 | bytes 4194304 | tf_op jit(solution)/shard_map/pallas_call | solution.py:77
  171.0 2.5 %shard_map.135 = (f32[192,768]{1,0:T(8,128)}, f32[192,768]{1,0:T(8,128)}, f32[192,768]{1,0:T(8,128)}, f32[192,768]{1,0:T(8,128)}) custom-call(s32[2]{0:T(128)S(1)} %pad_add_fusion.where.place, bf16[16,72,128]{2,1,0:T(8,128)(2,1)S(1)} %all-to-all-done.3.b0, bf16[16,72,128]{2,1,0:T(8,128)(2,1)S(1)} %collective-permute-done.29.b1, ...), custom_call_target="tpu_custom_call" | custom-call | bytes 4194304 | tf_op jit(solution)/shard_map/pallas_call | solution.py:77
  (114 shorter events, 16.0 us)
Async XLA Ops:
  0.7 1.1 copy-start
  3.8 10.1 %copy-start.7 = (bf16[192,768]{1,0:T(8,128)(2,1)S(1)}, bf16[192,768]{1,0:T(8,128)(2,1)}, u32[]{:S(2)}) copy-start(bf16[192,768]{1,0:T(8,128)(2,1)} %w_query.1) | copy-start | bytes 884740
  3.8 10.1 %copy-start.8 = (bf16[192,768]{1,0:T(8,128)(2,1)S(1)}, bf16[192,768]{1,0:T(8,128)(2,1)}, u32[]{:S(2)}) copy-start(bf16[192,768]{1,0:T(8,128)(2,1)} %w_key.1) | copy-start | bytes 884740
  3.8 10.1 %copy-start.9 = (bf16[192,768]{1,0:T(8,128)(2,1)S(1)}, bf16[192,768]{1,0:T(8,128)(2,1)}, u32[]{:S(2)}) copy-start(bf16[192,768]{1,0:T(8,128)(2,1)} %w_value.1) | copy-start | bytes 884740
  3.8 7.8 %collective-permute-start.1 = (bf16[64,768]{1,0:T(8,128)(2,1)S(1)}, bf16[64,768]{1,0:T(8,128)(2,1)S(1)}, u32[]{:S(2)}, u32[]{:S(2)}) collective-permute-start(bf16[64,768]{1,0:T(8,128)(2,1)S(1)} %get-tuple-element.106), channel_id=1, source_target_pairs={{0,2},{1,3},{2,0},{3,1},{4,6},{5,7},{6,4},{7,5},{8,10},{9,11},{10,... | collective-permute-start | bytes 294920 | tf_op jit(solution)/shard_map/ppermute | solution.py:337
  6.0 6.7 %collective-permute-start.2 = (bf16[64,768]{1,0:T(8,128)(2,1)S(1)}, bf16[64,768]{1,0:T(8,128)(2,1)S(1)}, u32[]{:S(2)}, u32[]{:S(2)}) collective-permute-start(bf16[64,768]{1,0:T(8,128)(2,1)S(1)} %get-tuple-element.107), channel_id=1, source_target_pairs={{0,3},{1,2},{2,1},{3,0},{4,7},{5,6},{6,5},{7,4},{8,11},{9,10},{10,... | collective-permute-start | bytes 294920 | tf_op jit(solution)/shard_map/ppermute | solution.py:337
  11.6 2.4 %copy-start.24 = (bf16[512,768]{1,0:T(8,128)(2,1)S(1)}, bf16[512,768]{1,0:T(8,128)(2,1)}, u32[]{:S(2)}) copy-start(bf16[512,768]{1,0:T(8,128)(2,1)} %source.5) | copy-start | bytes 2359300
  12.7 8.9 %collective-permute-start.4 = (bf16[192,768]{1,0:T(8,128)(2,1)S(1)}, bf16[192,768]{1,0:T(8,128)(2,1)S(1)}, u32[]{:S(2)}, u32[]{:S(2)}) collective-permute-start(bf16[192,768]{1,0:T(8,128)(2,1)S(1)} %get-tuple-element.124), channel_id=1, source_target_pairs={{0,2},{1,3},{2,0},{3,1},{4,6},{5,7},{6,4},{7,5},{8,10},{9,11},{10,... | collective-permute-start | bytes 884744 | tf_op jit(solution)/shard_map/ppermute | solution.py:337
  12.7 4.2 %collective-permute-start = (bf16[64,768]{1,0:T(8,128)(2,1)S(1)}, bf16[64,768]{1,0:T(8,128)(2,1)S(1)}, u32[]{:S(2)}, u32[]{:S(2)}) collective-permute-start(bf16[64,768]{1,0:T(8,128)(2,1)S(1)} %get-tuple-element.105), channel_id=1, source_target_pairs={{0,1},{1,0},{2,3},{3,2},{4,5},{5,4},{6,7},{7,6},{8,9},{9,8},{10,11... | collective-permute-start | bytes 294920 | tf_op jit(solution)/shard_map/ppermute | solution.py:337
  16.9 11.1 %copy-start.31 = (bf16[192,768]{1,0:T(8,128)(2,1)S(1)}, bf16[192,768]{1,0:T(8,128)(2,1)}, u32[]{:S(2)}) copy-start(bf16[192,768]{1,0:T(8,128)(2,1)} %copy-done.30) | copy-start | bytes 884740
  16.9 12.7 %copy-start.29 = (bf16[192,768]{1,0:T(8,128)(2,1)S(1)}, bf16[192,768]{1,0:T(8,128)(2,1)}, u32[]{:S(2)}) copy-start(bf16[192,768]{1,0:T(8,128)(2,1)} %copy-done.28) | copy-start | bytes 884740
  21.6 11.2 %copy-start.3 = (bf16[192,768]{1,0:T(8,128)(2,1)}, bf16[192,768]{1,0:T(8,128)(2,1)S(1)}, u32[]{:S(2)}) copy-start(bf16[192,768]{1,0:T(8,128)(2,1)S(1)} %collective-permute-done.4.x2) | copy-start | bytes 884740
  21.6 21.8 %all-to-all-start = ((bf16[8,240,128]{2,1,0:T(8,128)(2,1)}), bf16[8,240,128]{2,1,0:T(8,128)(2,1)S(1)}, u32[]{:S(2)}, u32[]{:S(2)}) async-start(bf16[8,240,128]{2,1,0:T(8,128)(2,1)} %get-tuple-element.135), calls=%async_computation | async-start | bytes 983040 | tf_op jit(solution)/shard_map/all_to_all | solution.py:341
  28.1 4.7 %collective-permute-start.3 = (bf16[192,768]{1,0:T(8,128)(2,1)S(1)}, bf16[192,768]{1,0:T(8,128)(2,1)S(1)}, u32[]{:S(2)}, u32[]{:S(2)}) collective-permute-start(bf16[192,768]{1,0:T(8,128)(2,1)S(1)} %copy-done.31), channel_id=1, source_target_pairs={{0,1},{1,0},{2,3},{3,2},{4,5},{5,4},{6,7},{7,6},{8,9},{9,8},{10,11... | collective-permute-start | bytes 884744 | tf_op jit(solution)/shard_map/ppermute | solution.py:337
  29.7 9.6 %collective-permute-start.5 = (bf16[192,768]{1,0:T(8,128)(2,1)S(1)}, bf16[192,768]{1,0:T(8,128)(2,1)S(1)}, u32[]{:S(2)}, u32[]{:S(2)}) collective-permute-start(bf16[192,768]{1,0:T(8,128)(2,1)S(1)} %copy-done.29), channel_id=1, source_target_pairs={{0,3},{1,2},{2,1},{3,0},{4,7},{5,6},{6,5},{7,4},{8,11},{9,10},{10,... | collective-permute-start | bytes 884744 | tf_op jit(solution)/shard_map/ppermute | solution.py:337
  30.6 15.4 %collective-permute-start.6 = (bf16[256,768]{1,0:T(8,128)(2,1)}, bf16[256,768]{1,0:T(8,128)(2,1)}, u32[]{:S(2)}, u32[]{:S(2)}) collective-permute-start(bf16[256,768]{1,0:T(8,128)(2,1)} %get-tuple-element.130), channel_id=1, source_target_pairs={{0,1},{1,0},{2,3},{3,2},{4,5},{5,4},{6,7},{7,6},{8,9},{9,8},{10,11... | collective-permute-start | bytes 1179656 | tf_op jit(solution)/shard_map/ppermute | solution.py:337
  31.0 15.6 %collective-permute-start.7 = (bf16[256,768]{1,0:T(8,128)(2,1)}, bf16[256,768]{1,0:T(8,128)(2,1)}, u32[]{:S(2)}, u32[]{:S(2)}) collective-permute-start(bf16[256,768]{1,0:T(8,128)(2,1)} %get-tuple-element.131), channel_id=1, source_target_pairs={{0,2},{1,3},{2,0},{3,1},{4,6},{5,7},{6,4},{7,5},{8,10},{9,11},{10,... | collective-permute-start | bytes 1179656 | tf_op jit(solution)/shard_map/ppermute | solution.py:337
  31.6 23.8 %collective-permute-start.8 = (bf16[256,768]{1,0:T(8,128)(2,1)}, bf16[256,768]{1,0:T(8,128)(2,1)}, u32[]{:S(2)}, u32[]{:S(2)}) collective-permute-start(bf16[256,768]{1,0:T(8,128)(2,1)} %get-tuple-element.132), channel_id=1, source_target_pairs={{0,3},{1,2},{2,1},{3,0},{4,7},{5,6},{6,5},{7,4},{8,11},{9,10},{10,... | collective-permute-start | bytes 1179656 | tf_op jit(solution)/shard_map/ppermute | solution.py:337
  39.2 1.0 copy-start.4
  42.1 17.8 %copy-start.23 = (s32[3,12]{1,0:T(4,128)S(1)}, s32[3,12]{1,0:T(4,128)}, u32[]{:S(2)}) copy-start(s32[3,12]{1,0:T(4,128)} %offs.11) | copy-start | bytes 436
  42.1 17.1 %collective-permute-start.9 = (bf16[768,128]{1,0:T(8,128)(2,1)}, bf16[768,128]{1,0:T(8,128)(2,1)S(1)}, u32[]{:S(2)}, u32[]{:S(2)}) collective-permute-start(bf16[768,128]{1,0:T(8,128)(2,1)} %get-tuple-element.134.first_own), channel_id=1, source_target_pairs={{0,4},{4,0},{8,12},{12,8},{16,20},{20,16},{24,28},{28,24},{1,5},{5... | collective-permute-start | bytes 589832 | tf_op jit(solution)/shard_map/ppermute | solution.py:337
  43.4 16.4 %copy-start.33 = (bf16[768,128]{1,0:T(8,128)(2,1)S(1)}, bf16[768,128]{1,0:T(8,128)(2,1)}, u32[]{:S(2)}) copy-start(bf16[768,128]{1,0:T(8,128)(2,1)} %copy-done.32) | copy-start | bytes 589828
  43.5 16.4 %collective-permute-start.12 = (bf16[8,48,128]{2,1,0:T(8,128)(2,1)S(1)}, bf16[8,48,128]{2,1,0:T(8,128)(2,1)S(1)}, u32[]{:S(2)}, u32[]{:S(2)}) collective-permute-start(bf16[8,48,128]{2,1,0:T(8,128)(2,1)S(1)} %slice.4), channel_id=1, source_target_pairs={{0,96},{32,64},{64,32},{96,0},{1,97},{33,65},{65,33},{97,1},{2,98}... | collective-permute-start | bytes 294920 | tf_op jit(solution)/shard_map/ppermute | solution.py:337
  46.0 13.8 %collective-permute-start.11 = (bf16[8,48,128]{2,1,0:T(8,128)(2,1)S(1)}, bf16[8,48,128]{2,1,0:T(8,128)(2,1)S(1)}, u32[]{:S(2)}, u32[]{:S(2)}) collective-permute-start(bf16[8,48,128]{2,1,0:T(8,128)(2,1)S(1)} %slice.4), channel_id=1, source_target_pairs={{0,64},{32,96},{64,0},{96,32},{1,65},{33,97},{65,1},{97,33},{2,66}... | collective-permute-start | bytes 294920 | tf_op jit(solution)/shard_map/ppermute | solution.py:337
  46.7 13.2 %collective-permute-start.10 = (bf16[8,48,128]{2,1,0:T(8,128)(2,1)S(1)}, bf16[8,48,128]{2,1,0:T(8,128)(2,1)S(1)}, u32[]{:S(2)}, u32[]{:S(2)}) collective-permute-start(bf16[8,48,128]{2,1,0:T(8,128)(2,1)S(1)} %slice.4), channel_id=1, source_target_pairs={{0,32},{32,0},{64,96},{96,64},{1,33},{33,1},{65,97},{97,65},{2,34}... | collective-permute-start | bytes 294920 | tf_op jit(solution)/shard_map/ppermute | solution.py:337
  55.3 1.0 copy-start.2
  56.3 1.0 copy-start.5
  59.9 0.9 copy-start.35
  60.8 0.8 copy-start.40
  61.6 13.4 %copy-start.6 = (bf16[192,768]{1,0:T(8,128)(2,1)S(1)}, bf16[192,768]{1,0:T(8,128)(2,1)}, u32[]{:S(2)}) copy-start(bf16[192,768]{1,0:T(8,128)(2,1)} %w_out.3) | copy-start | bytes 884740
  69.5 12.5 %collective-permute-start.16 = (bf16[768,128]{1,0:T(8,128)(2,1)S(1)}, bf16[768,128]{1,0:T(8,128)(2,1)S(1)}, u32[]{:S(2)}, u32[]{:S(2)}) collective-permute-start(bf16[768,128]{1,0:T(8,128)(2,1)S(1)} %get-tuple-element.143), channel_id=1, source_target_pairs={{0,4},{4,0},{8,12},{12,8},{16,20},{20,16},{24,28},{28,24},{1,5},{5... | collective-permute-start | bytes 589832 | tf_op jit(solution)/shard_map/ppermute | solution.py:337
  71.1 8.8 %collective-permute-start.13 = (bf16[8,48,128]{2,1,0:T(8,128)(2,1)S(1)}, bf16[8,48,128]{2,1,0:T(8,128)(2,1)S(1)}, u32[]{:S(2)}, u32[]{:S(2)}) collective-permute-start(bf16[8,48,128]{2,1,0:T(8,128)(2,1)S(1)} %get-tuple-element.140), channel_id=1, source_target_pairs={{0,32},{32,0},{64,96},{96,64},{1,33},{33,1},{65,97},{97,65},{2,34}... | collective-permute-start | bytes 294920 | tf_op jit(solution)/shard_map/ppermute | solution.py:337
  72.3 7.5 %collective-permute-start.14 = (bf16[8,48,128]{2,1,0:T(8,128)(2,1)S(1)}, bf16[8,48,128]{2,1,0:T(8,128)(2,1)S(1)}, u32[]{:S(2)}, u32[]{:S(2)}) collective-permute-start(bf16[8,48,128]{2,1,0:T(8,128)(2,1)S(1)} %get-tuple-element.141), channel_id=1, source_target_pairs={{0,64},{32,96},{64,0},{96,32},{1,65},{33,97},{65,1},{97,33},{2,66}... | collective-permute-start | bytes 294920 | tf_op jit(solution)/shard_map/ppermute | solution.py:337
  74.8 7.2 %collective-permute-start.15 = (bf16[8,48,128]{2,1,0:T(8,128)(2,1)S(1)}, bf16[8,48,128]{2,1,0:T(8,128)(2,1)S(1)}, u32[]{:S(2)}, u32[]{:S(2)}) collective-permute-start(bf16[8,48,128]{2,1,0:T(8,128)(2,1)S(1)} %get-tuple-element.142), channel_id=1, source_target_pairs={{0,96},{32,64},{64,32},{96,0},{1,97},{33,65},{65,33},{97,1},{2,98}... | collective-permute-start | bytes 294920 | tf_op jit(solution)/shard_map/ppermute | solution.py:337
  75.7 0.7 copy-start.41
  76.5 5.5 %copy-start.25 = (bf16[256,768]{1,0:T(8,128)(2,1)}, bf16[256,768]{1,0:T(8,128)(2,1)S(1)}, u32[]{:S(2)}) copy-start(bf16[256,768]{1,0:T(8,128)(2,1)S(1)} %get-tuple-element.174) | copy-start | bytes 1179652
  76.5 6.2 %copy-start.26 = (bf16[256,768]{1,0:T(8,128)(2,1)}, bf16[256,768]{1,0:T(8,128)(2,1)S(1)}, u32[]{:S(2)}) copy-start(bf16[256,768]{1,0:T(8,128)(2,1)S(1)} %get-tuple-element.173) | copy-start | bytes 1179652
  76.5 6.2 %copy-start.27 = (bf16[256,768]{1,0:T(8,128)(2,1)}, bf16[256,768]{1,0:T(8,128)(2,1)S(1)}, u32[]{:S(2)}) copy-start(bf16[256,768]{1,0:T(8,128)(2,1)S(1)} %get-tuple-element.172) | copy-start | bytes 1179652
  79.9 2.8 %copy-start.36 = (bf16[576,128]{1,0:T(8,128)(2,1)}, bf16[576,128]{1,0:T(8,128)(2,1)S(1)}, u32[]{:S(2)}) copy-start(bf16[576,128]{1,0:T(8,128)(2,1)S(1)} %get-tuple-element.159) | copy-start | bytes 442372
  83.5 22.7 %all-to-all-start.1 = ((bf16[8,240,128]{2,1,0:T(8,128)(2,1)}), bf16[8,240,128]{2,1,0:T(8,128)(2,1)S(1)}, u32[]{:S(2)}, u32[]{:S(2)}) async-start(bf16[8,240,128]{2,1,0:T(8,128)(2,1)} %shard_map.128), calls=%async_computation.1 | async-start | bytes 983040 | tf_op jit(solution)/shard_map/all_to_all | solution.py:341
  89.0 20.5 %collective-permute-start.23 = (bf16[256,768]{1,0:T(8,128)(2,1)}, bf16[256,768]{1,0:T(8,128)(2,1)}, u32[]{:S(2)}, u32[]{:S(2)}) collective-permute-start(bf16[256,768]{1,0:T(8,128)(2,1)} %copy-done.27), channel_id=1, source_target_pairs={{0,1},{1,0},{2,3},{3,2},{4,5},{5,4},{6,7},{7,6},{8,9},{9,8},{10,11... | collective-permute-start | bytes 1179656 | tf_op jit(solution)/shard_map/ppermute | solution.py:337
  89.9 5.7 %collective-permute-start.17 = (bf16[576,128]{1,0:T(8,128)(2,1)}, bf16[576,128]{1,0:T(8,128)(2,1)S(1)}, u32[]{:S(2)}, u32[]{:S(2)}) collective-permute-start(bf16[576,128]{1,0:T(8,128)(2,1)} %copy-done.38), channel_id=1, source_target_pairs={{0,32},{32,0},{64,96},{96,64},{1,33},{33,1},{65,97},{97,65},{2,34}... | collective-permute-start | bytes 442376 | tf_op jit(solution)/shard_map/ppermute | solution.py:337
  89.9 24.0 %collective-permute-start.24 = (bf16[256,768]{1,0:T(8,128)(2,1)}, bf16[256,768]{1,0:T(8,128)(2,1)}, u32[]{:S(2)}, u32[]{:S(2)}) collective-permute-start(bf16[256,768]{1,0:T(8,128)(2,1)} %copy-done.26), channel_id=1, source_target_pairs={{0,2},{1,3},{2,0},{3,1},{4,6},{5,7},{6,4},{7,5},{8,10},{9,11},{10,... | collective-permute-start | bytes 1179656 | tf_op jit(solution)/shard_map/ppermute | solution.py:337
  90.9 23.0 %collective-permute-start.25 = (bf16[256,768]{1,0:T(8,128)(2,1)}, bf16[256,768]{1,0:T(8,128)(2,1)}, u32[]{:S(2)}, u32[]{:S(2)}) collective-permute-start(bf16[256,768]{1,0:T(8,128)(2,1)} %copy-done.25), channel_id=1, source_target_pairs={{0,3},{1,2},{2,1},{3,0},{4,7},{5,6},{6,5},{7,4},{8,11},{9,10},{10,... | collective-permute-start | bytes 1179656 | tf_op jit(solution)/shard_map/ppermute | solution.py:337
  91.7 7.7 %collective-permute-start.18 = (bf16[576,128]{1,0:T(8,128)(2,1)}, bf16[576,128]{1,0:T(8,128)(2,1)S(1)}, u32[]{:S(2)}, u32[]{:S(2)}) collective-permute-start(bf16[576,128]{1,0:T(8,128)(2,1)} %copy-done.37), channel_id=1, source_target_pairs={{0,64},{32,96},{64,0},{96,32},{1,65},{33,97},{65,1},{97,33},{2,66}... | collective-permute-start | bytes 442376 | tf_op jit(solution)/shard_map/ppermute | solution.py:337
  96.3 5.4 %collective-permute-start.19 = (bf16[576,128]{1,0:T(8,128)(2,1)}, bf16[576,128]{1,0:T(8,128)(2,1)S(1)}, u32[]{:S(2)}, u32[]{:S(2)}) collective-permute-start(bf16[576,128]{1,0:T(8,128)(2,1)} %copy-done.36), channel_id=1, source_target_pairs={{0,96},{32,64},{64,32},{96,0},{1,97},{33,65},{65,33},{97,1},{2,98}... | collective-permute-start | bytes 442376 | tf_op jit(solution)/shard_map/ppermute | solution.py:337
  106.2 0.9 copy-start.11
  107.2 0.9 copy-start.13
  109.2 10.2 %copy-start.15 = (bf16[576,128]{1,0:T(8,128)(2,1)S(1)}, bf16[576,128]{1,0:T(8,128)(2,1)}, u32[]{:S(2)}) copy-start(bf16[576,128]{1,0:T(8,128)(2,1)} %copy-done.14) | copy-start | bytes 442372
  109.2 10.2 %copy-start.17 = (bf16[576,128]{1,0:T(8,128)(2,1)S(1)}, bf16[576,128]{1,0:T(8,128)(2,1)}, u32[]{:S(2)}) copy-start(bf16[576,128]{1,0:T(8,128)(2,1)} %copy-done.16) | copy-start | bytes 442372
  109.2 10.2 %copy-start.19 = (bf16[576,128]{1,0:T(8,128)(2,1)S(1)}, bf16[576,128]{1,0:T(8,128)(2,1)}, u32[]{:S(2)}) copy-start(bf16[576,128]{1,0:T(8,128)(2,1)} %copy-done.18) | copy-start | bytes 442372
  109.2 10.2 %copy-start.21 = (bf16[576,128]{1,0:T(8,128)(2,1)S(1)}, bf16[576,128]{1,0:T(8,128)(2,1)}, u32[]{:S(2)}) copy-start(bf16[576,128]{1,0:T(8,128)(2,1)} %copy-done.20) | copy-start | bytes 442372
  109.2 5.0 %collective-permute-start.20 = (bf16[576,128]{1,0:T(8,128)(2,1)S(1)}, bf16[576,128]{1,0:T(8,128)(2,1)S(1)}, u32[]{:S(2)}, u32[]{:S(2)}) collective-permute-start(bf16[576,128]{1,0:T(8,128)(2,1)S(1)} %get-tuple-element.168), channel_id=1, source_target_pairs={{0,32},{32,0},{64,96},{96,64},{1,33},{33,1},{65,97},{97,65},{2,34}... | collective-permute-start | bytes 442376 | tf_op jit(solution)/shard_map/ppermute | solution.py:337
  109.3 7.4 %collective-permute-start.21 = (bf16[576,128]{1,0:T(8,128)(2,1)S(1)}, bf16[576,128]{1,0:T(8,128)(2,1)S(1)}, u32[]{:S(2)}, u32[]{:S(2)}) collective-permute-start(bf16[576,128]{1,0:T(8,128)(2,1)S(1)} %get-tuple-element.169), channel_id=1, source_target_pairs={{0,64},{32,96},{64,0},{96,32},{1,65},{33,97},{65,1},{97,33},{2,66}... | collective-permute-start | bytes 442376 | tf_op jit(solution)/shard_map/ppermute | solution.py:337
  109.5 10.0 %collective-permute-start.22 = (bf16[576,128]{1,0:T(8,128)(2,1)S(1)}, bf16[576,128]{1,0:T(8,128)(2,1)S(1)}, u32[]{:S(2)}, u32[]{:S(2)}) collective-permute-start(bf16[576,128]{1,0:T(8,128)(2,1)S(1)} %get-tuple-element.170), channel_id=1, source_target_pairs={{0,96},{32,64},{64,32},{96,0},{1,97},{33,65},{65,33},{97,1},{2,98}... | collective-permute-start | bytes 442376 | tf_op jit(solution)/shard_map/ppermute | solution.py:337
  113.9 14.0 %copy-start.42 = (bf16[256,768]{1,0:T(8,128)(2,1)S(1)}, bf16[256,768]{1,0:T(8,128)(2,1)}, u32[]{:S(2)}) copy-start(bf16[256,768]{1,0:T(8,128)(2,1)} %copy-done.41) | copy-start | bytes 1179652
  120.5 16.9 %all-to-all-start.2 = ((bf16[16,72,128]{2,1,0:T(8,128)(2,1)}), bf16[16,72,128]{2,1,0:T(8,128)(2,1)S(1)}, u32[]{:S(2)}, u32[]{:S(2)}) async-start(bf16[16,72,128]{2,1,0:T(8,128)(2,1)} %shard_map.131), calls=%async_computation.2 | async-start | bytes 589824 | tf_op jit(solution)/shard_map/all_to_all | solution.py:341
  138.1 16.0 %all-to-all-start.3 = ((bf16[16,72,128]{2,1,0:T(8,128)(2,1)}), bf16[16,72,128]{2,1,0:T(8,128)(2,1)S(1)}, u32[]{:S(2)}, u32[]{:S(2)}) async-start(bf16[16,72,128]{2,1,0:T(8,128)(2,1)} %shard_map.132), calls=%async_computation.3 | async-start | bytes 589824 | tf_op jit(solution)/shard_map/all_to_all | solution.py:341
  144.7 11.1 %collective-permute-start.26 = (bf16[256,768]{1,0:T(8,128)(2,1)S(1)}, bf16[256,768]{1,0:T(8,128)(2,1)S(1)}, u32[]{:S(2)}, u32[]{:S(2)}) collective-permute-start(bf16[256,768]{1,0:T(8,128)(2,1)S(1)} %get-tuple-element.194), channel_id=1, source_target_pairs={{0,1},{1,0},{2,3},{3,2},{4,5},{5,4},{6,7},{7,6},{8,9},{9,8},{10,11... | collective-permute-start | bytes 1179656 | tf_op jit(solution)/shard_map/ppermute | solution.py:337
  146.6 13.3 %collective-permute-start.27 = (bf16[256,768]{1,0:T(8,128)(2,1)S(1)}, bf16[256,768]{1,0:T(8,128)(2,1)S(1)}, u32[]{:S(2)}, u32[]{:S(2)}) collective-permute-start(bf16[256,768]{1,0:T(8,128)(2,1)S(1)} %get-tuple-element.195), channel_id=1, source_target_pairs={{0,2},{1,3},{2,0},{3,1},{4,6},{5,7},{6,4},{7,5},{8,10},{9,11},{10,... | collective-permute-start | bytes 1179656 | tf_op jit(solution)/shard_map/ppermute | solution.py:337
  147.0 21.6 %collective-permute-start.28 = (bf16[256,768]{1,0:T(8,128)(2,1)S(1)}, bf16[256,768]{1,0:T(8,128)(2,1)S(1)}, u32[]{:S(2)}, u32[]{:S(2)}) collective-permute-start(bf16[256,768]{1,0:T(8,128)(2,1)S(1)} %get-tuple-element.196), channel_id=1, source_target_pairs={{0,3},{1,2},{2,1},{3,0},{4,7},{5,6},{6,5},{7,4},{8,11},{9,10},{10,... | collective-permute-start | bytes 1179656 | tf_op jit(solution)/shard_map/ppermute | solution.py:337
  154.1 16.9 %collective-permute-start.31 = (bf16[16,72,128]{2,1,0:T(8,128)(2,1)S(1)}, bf16[16,72,128]{2,1,0:T(8,128)(2,1)S(1)}, u32[]{:S(2)}, u32[]{:S(2)}) collective-permute-start(bf16[16,72,128]{2,1,0:T(8,128)(2,1)S(1)} %all-to-all-done.3.b0), channel_id=1, source_target_pairs={{0,96},{32,64},{64,32},{96,0},{1,97},{33,65},{65,33},{97,1},{2,98}... | collective-permute-start | bytes 884744 | tf_op jit(solution)/shard_map/ppermute | solution.py:337
  154.8 16.2 %collective-permute-start.30 = (bf16[16,72,128]{2,1,0:T(8,128)(2,1)S(1)}, bf16[16,72,128]{2,1,0:T(8,128)(2,1)S(1)}, u32[]{:S(2)}, u32[]{:S(2)}) collective-permute-start(bf16[16,72,128]{2,1,0:T(8,128)(2,1)S(1)} %all-to-all-done.3.b0), channel_id=1, source_target_pairs={{0,64},{32,96},{64,0},{96,32},{1,65},{33,97},{65,1},{97,33},{2,66}... | collective-permute-start | bytes 884744 | tf_op jit(solution)/shard_map/ppermute | solution.py:337
  155.8 15.2 %collective-permute-start.29 = (bf16[16,72,128]{2,1,0:T(8,128)(2,1)S(1)}, bf16[16,72,128]{2,1,0:T(8,128)(2,1)S(1)}, u32[]{:S(2)}, u32[]{:S(2)}) collective-permute-start(bf16[16,72,128]{2,1,0:T(8,128)(2,1)S(1)} %all-to-all-done.3.b0), channel_id=1, source_target_pairs={{0,32},{32,0},{64,96},{96,64},{1,33},{33,1},{65,97},{97,65},{2,34}... | collective-permute-start | bytes 884744 | tf_op jit(solution)/shard_map/ppermute | solution.py:337
  (15 other events, 10.2 us)
